TPU v7x, 32 devices: a whole 2x2x4 slice. The times are simulated.
32 devices in a mesh: row: 16 (over z, x, core), col: 2 (over y).
Axes of the slice: x: 2, y: 2, z: 4, core: 2. Of those that a mesh axis runs over, the one named last changes fastest.
Arguments:
- sigma_anc: float32 [48, 48, 128, 128], P('row', 'col'), as said below
- factor: float32 [16, 32, 128, 128], P('row', 'col'), may hold values from -1.25 to 1.25
- diag_inv: float32 [32, 128, 128], P('col'), as said below
- struct: int32 [32, 16], P('col'), may hold values from 0 to 47, all different within a row
Outputs:
- z_off: float32 [32, 48, 128, 128], P('col', 'row')
- z_diag: float32 [32, 128, 128], P(('col', 'row'))
Inputs may be any that keep to these rules, and one draw needn't show every extreme that they name: Each row of struct names 16 different ancestor blocks, and every ancestor block is named by some row. sigma_anc is symmetric: block [b, a] is the transpose of block [a, b]. Each diag_inv[k] is lower triangular with a positive diagonal.
All inputs are finite; a program needn't handle non-finite values.
Results may differ from a plain program's by a relative error of at most 0.0003.
Values sent between devices are 32-bit elements; how exact they have to be, the bound alone decides.
No kernel may reach another device: no remote copies, remote signals or barrier semaphores. Data moves between devices by JAX's collectives and lax.ppermute only.
A program may use at most 128 MiB of HBM per device.

v0:
```python
import jax
import jax.numpy as jnp
from jax import lax
from jax.sharding import PartitionSpec as P

highest = lax.Precision.HIGHEST


def select_blocks(sigma_rows, slot_ids):
    return jnp.take(sigma_rows, slot_ids, axis=1)


def body(sigma_anc, factor, diag_inv, struct):
    row_count = sigma_anc.shape[0]
    node_count = diag_inv.shape[0]
    width = diag_inv.shape[1]
    row_index = lax.axis_index("row")
    own_rows = row_index * row_count + jnp.arange(row_count, dtype=jnp.int32)
    sigma_rows = lax.all_gather(sigma_anc, "col", axis=1, tiled=True)
    u_local = jnp.einsum("skij,kjl->skil", factor, diag_inv, precision=highest)
    empty = jnp.zeros((node_count, row_count, width, width), jnp.float32)

    def one_slot(running, element):
        u_slot, id_slot = element
        y_sum, u_rows = running
        picked = select_blocks(sigma_rows, id_slot)
        y_sum = y_sum + jnp.einsum("akij,kjl->kail", picked, u_slot, precision=highest)
        match = (id_slot[:, None] == own_rows[None, :]).astype(jnp.float32)
        u_rows = u_rows + match[:, :, None, None] * u_slot[:, None, :, :]
        return ((y_sum, u_rows), None)

    result, unused_out = lax.scan(
        one_slot,
        (empty, empty),
        (lax.all_gather(u_local, "row", axis=0, tiled=True), jnp.transpose(struct)),
    )
    y_rows, u_rows = result
    member = jnp.any(struct[:, :, None] == own_rows[None, None, :], axis=1)
    z_off = jnp.where(member[:, :, None, None], -y_rows, 0.0)
    partial_sum = jnp.einsum("kaij,kail->kjl", u_rows, y_rows, precision=highest)
    share_count = node_count // lax.axis_size("row")
    start_node = row_index * share_count
    inverse_share = lax.dynamic_slice_in_dim(diag_inv, start_node, share_count, 0)
    inverse_part = jnp.einsum("kij,kil->kjl", inverse_share, inverse_share, precision=highest)
    summed = lax.psum(partial_sum, "row")
    mine = lax.dynamic_slice_in_dim(summed, start_node, share_count, 0)
    return (z_off, inverse_part + mine)


def solution(mesh):
    in_specs = (
        P("row", "col", None, None),
        P("row", "col", None, None),
        P("col", None, None),
        P("col", None),
    )
    out_specs = (P("col", "row", None, None), P(("col", "row"), None, None))
    return jax.shard_map(body, mesh=mesh, in_specs=in_specs, out_specs=out_specs, check_vma=False)
```

profile of v0, /device:TPU:0, one launch (start us, length us, event | category | flops | bytes accessed | tf_op | source)
XLA Modules:
  0.0 654.7 jit_solution(2303652439403514152)
XLA Ops:
  8.7 1.8 convolution_bitcast_fusion.1
  10.6 1.4 copy.17
  12.1 117.0 %all-gather.3.cloned.1.call-done = f32[3,48,128,128]{3,2,1,0:T(8,128)} async-done(((f32[3,24,128,128]{3,2,1,0:T(8,128)}), f32[3,48,128,128]{3,2,1,0:T(8,128)}) %all-gather.3.cloned.1.call-update) | async-done | bytes 9437200 | tf_op jit(solution)/shard_map/all_gather | solution.py:19
  129.1 129.1 %all-gather.5.cloned.1.call-done = f32[16,16,128,128]{3,2,1,0:T(8,128)} async-done(((f32[1,16,128,128]{3,2,1,0:T(8,128)}), f32[16,16,128,128]{3,2,1,0:T(8,128)}) %all-gather.5.cloned.1.call-update) | async-done | bytes 16777232 | tf_op jit(solution)/shard_map/all_gather | solution.py:35
  258.2 287.6 %while.13 = (s32[]{:T(128)}, f32[16,3,128,128]{3,2,1,0:T(8,128)}, f32[16,3,128,128]{3,2,1,0:T(8,128)}, s32[16,16]{1,0:T(8,128)S(1)}, f32[3,48,128,128]{3,2,1,0:T...) while((s32[]{:T(128)}, f32[16,3,128,128]{3,2,1,0:T(8,128)}, ...), condition=%wide.region_2.3_spmd.clone, body=%wide.region_1.2_spmd.clone.sunk | while | flops 1212679424 | bytes 26220016 | solution.py:32
  258.2 6.1 gather_fusion
  264.3 6.2 select_add_fusion.4
  270.6 1.3 dynamic-slice_bitcast_fusion.2
  271.9 2.1 select_add_fusion.5
  273.9 6.1 gather_fusion
  280.0 6.7 %select_add_fusion.4 = f32[16,3,128,128]{3,2,1,0:T(8,128)} fusion(f32[16,3,128,128]{3,2,1,0:T(8,128)} %get-tuple-element.149, f32[16,3,128,128]{3,2,1,0:T(8,128)} %gather_fusion, pred[16]{0:T(512)(128)(4,1)S(1)} %get-tuple-element.137, pred[]{:T(512)S(6)} %compare.3, f32[16,16,128,128]{3,2,1,0:T(8,128)} %get-tuple-element.162, s32[]{:T(128)} %get-tuple-element.148), kind=kOutput, calls=%fused_computation.5.clone.1 | convolution fusion | flops 1210318848 | bytes 10486289 | tf_op jit(solution)/shard_map/while/body/eval_jaxpr/akij,kjl->kail/dot_general | solution.py:27
  286.8 1.3 dynamic-slice_bitcast_fusion.2
  288.1 4.0 select_add_fusion.5
  292.1 6.1 gather_fusion
  298.1 6.7 %select_add_fusion.4 = f32[16,3,128,128]{3,2,1,0:T(8,128)} fusion(f32[16,3,128,128]{3,2,1,0:T(8,128)} %get-tuple-element.149, f32[16,3,128,128]{3,2,1,0:T(8,128)} %gather_fusion, pred[16]{0:T(512)(128)(4,1)S(1)} %get-tuple-element.137, pred[]{:T(512)S(6)} %compare.3, f32[16,16,128,128]{3,2,1,0:T(8,128)} %get-tuple-element.162, s32[]{:T(128)} %get-tuple-element.148), kind=kOutput, calls=%fused_computation.5.clone.1 | convolution fusion | flops 1210318848 | bytes 10486289 | tf_op jit(solution)/shard_map/while/body/eval_jaxpr/akij,kjl->kail/dot_general | solution.py:27
  304.9 1.3 dynamic-slice_bitcast_fusion.2
  306.2 4.0 select_add_fusion.5
  310.2 6.1 gather_fusion
  316.3 6.7 %select_add_fusion.4 = f32[16,3,128,128]{3,2,1,0:T(8,128)} fusion(f32[16,3,128,128]{3,2,1,0:T(8,128)} %get-tuple-element.149, f32[16,3,128,128]{3,2,1,0:T(8,128)} %gather_fusion, pred[16]{0:T(512)(128)(4,1)S(1)} %get-tuple-element.137, pred[]{:T(512)S(6)} %compare.3, f32[16,16,128,128]{3,2,1,0:T(8,128)} %get-tuple-element.162, s32[]{:T(128)} %get-tuple-element.148), kind=kOutput, calls=%fused_computation.5.clone.1 | convolution fusion | flops 1210318848 | bytes 10486289 | tf_op jit(solution)/shard_map/while/body/eval_jaxpr/akij,kjl->kail/dot_general | solution.py:27
  323.0 1.3 dynamic-slice_bitcast_fusion.2
  324.3 4.0 select_add_fusion.5
  328.3 6.1 gather_fusion
  334.4 6.7 %select_add_fusion.4 = f32[16,3,128,128]{3,2,1,0:T(8,128)} fusion(f32[16,3,128,128]{3,2,1,0:T(8,128)} %get-tuple-element.149, f32[16,3,128,128]{3,2,1,0:T(8,128)} %gather_fusion, pred[16]{0:T(512)(128)(4,1)S(1)} %get-tuple-element.137, pred[]{:T(512)S(6)} %compare.3, f32[16,16,128,128]{3,2,1,0:T(8,128)} %get-tuple-element.162, s32[]{:T(128)} %get-tuple-element.148), kind=kOutput, calls=%fused_computation.5.clone.1 | convolution fusion | flops 1210318848 | bytes 10486289 | tf_op jit(solution)/shard_map/while/body/eval_jaxpr/akij,kjl->kail/dot_general | solution.py:27
  341.2 1.3 dynamic-slice_bitcast_fusion.2
  342.5 4.0 select_add_fusion.5
  346.4 6.1 gather_fusion
  352.5 6.7 %select_add_fusion.4 = f32[16,3,128,128]{3,2,1,0:T(8,128)} fusion(f32[16,3,128,128]{3,2,1,0:T(8,128)} %get-tuple-element.149, f32[16,3,128,128]{3,2,1,0:T(8,128)} %gather_fusion, pred[16]{0:T(512)(128)(4,1)S(1)} %get-tuple-element.137, pred[]{:T(512)S(6)} %compare.3, f32[16,16,128,128]{3,2,1,0:T(8,128)} %get-tuple-element.162, s32[]{:T(128)} %get-tuple-element.148), kind=kOutput, calls=%fused_computation.5.clone.1 | convolution fusion | flops 1210318848 | bytes 10486289 | tf_op jit(solution)/shard_map/while/body/eval_jaxpr/akij,kjl->kail/dot_general | solution.py:27
  360.6 4.0 select_add_fusion.5
  364.6 6.1 gather_fusion
  370.6 6.7 %select_add_fusion.4 = f32[16,3,128,128]{3,2,1,0:T(8,128)} fusion(f32[16,3,128,128]{3,2,1,0:T(8,128)} %get-tuple-element.149, f32[16,3,128,128]{3,2,1,0:T(8,128)} %gather_fusion, pred[16]{0:T(512)(128)(4,1)S(1)} %get-tuple-element.137, pred[]{:T(512)S(6)} %compare.3, f32[16,16,128,128]{3,2,1,0:T(8,128)} %get-tuple-element.162, s32[]{:T(128)} %get-tuple-element.148), kind=kOutput, calls=%fused_computation.5.clone.1 | convolution fusion | flops 1210318848 | bytes 10486289 | tf_op jit(solution)/shard_map/while/body/eval_jaxpr/akij,kjl->kail/dot_general | solution.py:27
  378.7 4.0 select_add_fusion.5
  382.7 6.1 gather_fusion
  388.8 6.7 %select_add_fusion.4 = f32[16,3,128,128]{3,2,1,0:T(8,128)} fusion(f32[16,3,128,128]{3,2,1,0:T(8,128)} %get-tuple-element.149, f32[16,3,128,128]{3,2,1,0:T(8,128)} %gather_fusion, pred[16]{0:T(512)(128)(4,1)S(1)} %get-tuple-element.137, pred[]{:T(512)S(6)} %compare.3, f32[16,16,128,128]{3,2,1,0:T(8,128)} %get-tuple-element.162, s32[]{:T(128)} %get-tuple-element.148), kind=kOutput, calls=%fused_computation.5.clone.1 | convolution fusion | flops 1210318848 | bytes 10486289 | tf_op jit(solution)/shard_map/while/body/eval_jaxpr/akij,kjl->kail/dot_general | solution.py:27
  396.8 4.0 select_add_fusion.5
  400.8 6.1 gather_fusion
  406.9 6.7 %select_add_fusion.4 = f32[16,3,128,128]{3,2,1,0:T(8,128)} fusion(f32[16,3,128,128]{3,2,1,0:T(8,128)} %get-tuple-element.149, f32[16,3,128,128]{3,2,1,0:T(8,128)} %gather_fusion, pred[16]{0:T(512)(128)(4,1)S(1)} %get-tuple-element.137, pred[]{:T(512)S(6)} %compare.3, f32[16,16,128,128]{3,2,1,0:T(8,128)} %get-tuple-element.162, s32[]{:T(128)} %get-tuple-element.148), kind=kOutput, calls=%fused_computation.5.clone.1 | convolution fusion | flops 1210318848 | bytes 10486289 | tf_op jit(solution)/shard_map/while/body/eval_jaxpr/akij,kjl->kail/dot_general | solution.py:27
  414.9 4.0 select_add_fusion.5
  418.9 6.1 gather_fusion
  425.0 6.7 %select_add_fusion.4 = f32[16,3,128,128]{3,2,1,0:T(8,128)} fusion(f32[16,3,128,128]{3,2,1,0:T(8,128)} %get-tuple-element.149, f32[16,3,128,128]{3,2,1,0:T(8,128)} %gather_fusion, pred[16]{0:T(512)(128)(4,1)S(1)} %get-tuple-element.137, pred[]{:T(512)S(6)} %compare.3, f32[16,16,128,128]{3,2,1,0:T(8,128)} %get-tuple-element.162, s32[]{:T(128)} %get-tuple-element.148), kind=kOutput, calls=%fused_computation.5.clone.1 | convolution fusion | flops 1210318848 | bytes 10486289 | tf_op jit(solution)/shard_map/while/body/eval_jaxpr/akij,kjl->kail/dot_general | solution.py:27
  433.1 4.0 select_add_fusion.5
  437.0 6.1 gather_fusion
  443.1 6.7 %select_add_fusion.4 = f32[16,3,128,128]{3,2,1,0:T(8,128)} fusion(f32[16,3,128,128]{3,2,1,0:T(8,128)} %get-tuple-element.149, f32[16,3,128,128]{3,2,1,0:T(8,128)} %gather_fusion, pred[16]{0:T(512)(128)(4,1)S(1)} %get-tuple-element.137, pred[]{:T(512)S(6)} %compare.3, f32[16,16,128,128]{3,2,1,0:T(8,128)} %get-tuple-element.162, s32[]{:T(128)} %get-tuple-element.148), kind=kOutput, calls=%fused_computation.5.clone.1 | convolution fusion | flops 1210318848 | bytes 10486289 | tf_op jit(solution)/shard_map/while/body/eval_jaxpr/akij,kjl->kail/dot_general | solution.py:27
  451.2 4.0 select_add_fusion.5
  455.2 6.1 gather_fusion
  461.2 6.7 %select_add_fusion.4 = f32[16,3,128,128]{3,2,1,0:T(8,128)} fusion(f32[16,3,128,128]{3,2,1,0:T(8,128)} %get-tuple-element.149, f32[16,3,128,128]{3,2,1,0:T(8,128)} %gather_fusion, pred[16]{0:T(512)(128)(4,1)S(1)} %get-tuple-element.137, pred[]{:T(512)S(6)} %compare.3, f32[16,16,128,128]{3,2,1,0:T(8,128)} %get-tuple-element.162, s32[]{:T(128)} %get-tuple-element.148), kind=kOutput, calls=%fused_computation.5.clone.1 | convolution fusion | flops 1210318848 | bytes 10486289 | tf_op jit(solution)/shard_map/while/body/eval_jaxpr/akij,kjl->kail/dot_general | solution.py:27
  468.0 1.3 dynamic-slice_bitcast_fusion.2
  469.3 4.0 select_add_fusion.5
  473.3 6.1 gather_fusion
  479.4 6.7 %select_add_fusion.4 = f32[16,3,128,128]{3,2,1,0:T(8,128)} fusion(f32[16,3,128,128]{3,2,1,0:T(8,128)} %get-tuple-element.149, f32[16,3,128,128]{3,2,1,0:T(8,128)} %gather_fusion, pred[16]{0:T(512)(128)(4,1)S(1)} %get-tuple-element.137, pred[]{:T(512)S(6)} %compare.3, f32[16,16,128,128]{3,2,1,0:T(8,128)} %get-tuple-element.162, s32[]{:T(128)} %get-tuple-element.148), kind=kOutput, calls=%fused_computation.5.clone.1 | convolution fusion | flops 1210318848 | bytes 10486289 | tf_op jit(solution)/shard_map/while/body/eval_jaxpr/akij,kjl->kail/dot_general | solution.py:27
  487.4 4.0 select_add_fusion.5
  491.4 6.1 gather_fusion
  497.5 6.7 %select_add_fusion.4 = f32[16,3,128,128]{3,2,1,0:T(8,128)} fusion(f32[16,3,128,128]{3,2,1,0:T(8,128)} %get-tuple-element.149, f32[16,3,128,128]{3,2,1,0:T(8,128)} %gather_fusion, pred[16]{0:T(512)(128)(4,1)S(1)} %get-tuple-element.137, pred[]{:T(512)S(6)} %compare.3, f32[16,16,128,128]{3,2,1,0:T(8,128)} %get-tuple-element.162, s32[]{:T(128)} %get-tuple-element.148), kind=kOutput, calls=%fused_computation.5.clone.1 | convolution fusion | flops 1210318848 | bytes 10486289 | tf_op jit(solution)/shard_map/while/body/eval_jaxpr/akij,kjl->kail/dot_general | solution.py:27
  505.6 4.0 select_add_fusion.5
  509.5 6.1 gather_fusion
  515.6 6.7 %select_add_fusion.4 = f32[16,3,128,128]{3,2,1,0:T(8,128)} fusion(f32[16,3,128,128]{3,2,1,0:T(8,128)} %get-tuple-element.149, f32[16,3,128,128]{3,2,1,0:T(8,128)} %gather_fusion, pred[16]{0:T(512)(128)(4,1)S(1)} %get-tuple-element.137, pred[]{:T(512)S(6)} %compare.3, f32[16,16,128,128]{3,2,1,0:T(8,128)} %get-tuple-element.162, s32[]{:T(128)} %get-tuple-element.148), kind=kOutput, calls=%fused_computation.5.clone.1 | convolution fusion | flops 1210318848 | bytes 10486289 | tf_op jit(solution)/shard_map/while/body/eval_jaxpr/akij,kjl->kail/dot_general | solution.py:27
  523.7 4.0 select_add_fusion.5
  527.7 6.1 gather_fusion
  533.7 6.7 %select_add_fusion.4 = f32[16,3,128,128]{3,2,1,0:T(8,128)} fusion(f32[16,3,128,128]{3,2,1,0:T(8,128)} %get-tuple-element.149, f32[16,3,128,128]{3,2,1,0:T(8,128)} %gather_fusion, pred[16]{0:T(512)(128)(4,1)S(1)} %get-tuple-element.137, pred[]{:T(512)S(6)} %compare.3, f32[16,16,128,128]{3,2,1,0:T(8,128)} %get-tuple-element.162, s32[]{:T(128)} %get-tuple-element.148), kind=kOutput, calls=%fused_computation.5.clone.1 | convolution fusion | flops 1210318848 | bytes 10486289 | tf_op jit(solution)/shard_map/while/body/eval_jaxpr/akij,kjl->kail/dot_general | solution.py:27
  540.5 1.3 dynamic-slice_bitcast_fusion.2
  541.8 4.0 select_add_fusion.5
  545.8 9.0 %convolution_bitcast_fusion = f32[16,128,128]{2,1,0:T(8,128)} fusion(f32[16,3,128,128]{3,2,1,0:T(8,128)} %get-tuple-element.41, f32[16,3,128,128]{3,2,1,0:T(8,128)} %get-tuple-element.40), kind=kOutput, calls=%fused_computation.24 | convolution fusion | flops 1207959552 | bytes 7340032 | tf_op jit(solution)/shard_map/kaij,kail->kjl/dot_general | solution.py:40
  555.1 3.9 negate_select_fusion
  559.0 87.4 %all-reduce.2.cloned.1.call-done = f32[16,128,128]{2,1,0:T(8,128)} async-done(((f32[16,128,128]{2,1,0:T(8,128)}), f32[16,128,128]{2,1,0:T(8,128)}) %all-reduce.2.cloned.1.call-update) | async-done | bytes 1048592 | tf_op jit(solution)/shard_map/psum | solution.py:45
  646.4 1.8 fusion.15
  (107 shorter events, 15.3 us)
Async XLA Ops:
  7.2 1.2 copy-start
  7.2 1.5 copy-start.1
  7.2 121.9 %all-gather.3.cloned.1.call-start = ((), (), s32[]{:S(2)}) async-start(), calls=%async_computation | async-start | bytes 14155776 | tf_op jit(solution)/shard_map/all_gather | solution.py:19
  7.9 4.1 copy-start.2
  7.9 250.2 %all-gather.5.cloned.1.call-start = ((), (), s32[]{:S(2)}) async-start(), calls=%async_computation.1 | async-start | bytes 17825792 | tf_op jit(solution)/shard_map/all_gather | solution.py:35
  11.9 634.4 %all-reduce.2.cloned.1.call-start = ((), (), s32[]{:S(2)}) async-start(), calls=%async_computation.2 | async-start | bytes 2097152 | tf_op jit(solution)/shard_map/psum | solution.py:45
Sparse Core Ops, SparseCore 0:
  9.6 119.4 all-gather.2
  131.2 126.8 all-gather.4
  554.9 91.4 all-reduce.1
where the time goes:
time: 657 us; the launch traced here: 655 us
  waiting for transfers between devices  334 us (51%)
  local copies, waits for them, and re-layouts  120 us (18%)
  matrix products  119 us (18%)
  other arithmetic  67.2 us (10%)
  between operations  13.8 us (2%)
    all_gather x1, waiting for transfers between devices, body(): lax.all_gather(u_local, 'row', axis=0, tiled=True)  129 us
    all_gather x1, waiting for transfers between devices, body(): sigma_rows = lax.all_gather(sigma_anc, 'col', axis=1, tiled=True)  117 us
    dot_general x16, matrix products, one_slot(): jnp.einsum('akij,kjl->kail', picked, u_slot, precision=highest)  106 us
    gather x16, local copies, waits for them, and re-layouts, select_blocks(): return jnp.take(sigma_rows, slot_ids, axis=1)  97 us
    psum x1, waiting for transfers between devices, body(): summed = lax.psum(partial_sum, 'row')  87.4 us
    add x16, other arithmetic, one_slot(): u_rows = u_rows + match[:, :, None, None] * u_slot[:, None, :, :]  61.4 us
    squeeze x16, local copies, waits for them, and re-layouts, body(): lax.scan(one_slot, (empty, empty), (lax.all_gather(u_local, 'row', axis=0...  20.7 us
  transfers between devices with their start and end apart: 3, of which 3 were waited for; matrix products, arithmetic and copies ran while one was open for 1% of the time, Pallas kernels for 0%

commit v1 on v0

v1 whole, which is shorter than its diff:
```python
import functools

import jax
import jax.numpy as jnp
import numpy as np
from jax import lax
from jax.experimental import pallas as pl
from jax.experimental.pallas import tpu as pltpu
from jax.sharding import PartitionSpec as P

F32 = jnp.float32
BF16 = jnp.bfloat16
I32 = jnp.int32
MIB = 1024 * 1024
VMEM = pltpu.VMEM
SMEM = pltpu.SMEM
VMEM_LIMIT = 62 * MIB


def cost(microseconds):
    return pl.CostEstimate(flops=int(microseconds * 1e9), bytes_accessed=1000, transcendentals=0)


COSTS = dict(plan=1.0, u=1.0, sums=3.0)


def split(x):
    hi = x.astype(BF16)
    return hi, (x - hi.astype(F32)).astype(BF16)


def wide(x):
    hi, lo = split(x)
    return jnp.concatenate([hi, lo], axis=-1)


def tall(x):
    both = wide(x)
    return jnp.concatenate([both, both], axis=-2)


def fold(product):
    half = product.shape[-1] // 2
    return product[..., :half] + product[..., half:]


def dot(left, right):
    return jnp.dot(left, right, preferred_element_type=F32)


def dot_t(left, right):
    stacked = jnp.concatenate(split(left), axis=0)
    return fold(
        lax.dot_general(stacked, tall(right), (((0,), (0,)), ((), ())), preferred_element_type=F32)
    )


class Plan:
    def __init__(self, nodes, pieces, rows):
        self.place = 0
        self.slot = self.place + nodes * pieces
        self.node = self.slot + nodes * rows
        self.spare = self.node + nodes
        self.size = self.spare + 1


def plan_kernel(dims, plan, where, table, chip_of, struct, token, out):
    del token
    nodes, pieces, rows, cols, n_col = dims
    row, col = where[0], where[1]
    core = lax.rem(row, 2)

    def clear(index, carry):
        out[plan.slot + index] = -1
        return carry

    lax.fori_loop(0, nodes * rows, clear, 0)

    def locate(kk, carry):
        side = jnp.where(kk >= nodes // 2, 1 - core, core)
        n = 2 * chip_of[lax.rem(kk, nodes // 2)] + side
        origin = (row - core + side) * pieces
        out[plan.node + kk] = n
        for j in range(pieces):
            block = struct[n, table[origin + j]]
            shift = lax.div(block, cols) - col
            out[plan.place + kk * pieces + j] = block + jnp.where(shift < 0, n_col - col, -col) * cols
            first = block - row * rows
            inside = (first >= 0) & (first < rows)
            out[jnp.where(inside, plan.slot + kk * rows + first, plan.spare)] = j
        return carry

    lax.fori_loop(0, nodes, locate, 0)


def make_plan(plan, dims, where, table, chip_of, struct, token):
    smem = pl.BlockSpec(memory_space=SMEM)
    return pl.pallas_call(
        functools.partial(plan_kernel, dims, plan),
        out_shape=jax.ShapeDtypeStruct((plan.size,), I32),
        in_specs=[smem] * 4 + [pl.BlockSpec(memory_space=pl.ANY)],
        out_specs=smem,
        cost_estimate=cost(COSTS["plan"]),
        name="plan",
    )(where, table, chip_of, struct, token)


def u_kernel(chips, other, where, own, partner, inverse, token, out, square_out, f_buf, d_buf, u_buf, square, sems):
    del token
    core = lax.rem(where[0], 2)
    count = len(chips)
    loads = []
    for index, chip in enumerate(chips):
        n = 2 * chip + (1 - core if other else core)
        loads.append(
            [
                pltpu.make_async_copy(inverse.at[n], d_buf.at[index], sems.at[0, index]),
                pltpu.make_async_copy(own.at[n], f_buf.at[1 if other else 0, index], sems.at[1, index]),
                pltpu.make_async_copy(partner.at[n], f_buf.at[0 if other else 1, index], sems.at[2, index]),
            ]
        )
    last = pltpu.make_async_copy(inverse.at[where[0]], d_buf.at[count], sems.at[0, count])
    for copies in loads:
        for copy in copies:
            copy.start()
    last.start()
    for index in range(count):
        for copy in loads[index]:
            copy.wait()
        right = tall(d_buf[index])
        for side in range(2):
            u_buf[side, index] = fold(dot(wide(f_buf[side, index]), right))
    stores = [pltpu.make_async_copy(u_buf, out, sems.at[1, count])]
    stores[0].start()
    last.wait()
    square[0] = dot_t(d_buf[count], d_buf[count])
    stores.append(pltpu.make_async_copy(square, square_out, sems.at[2, count]))
    stores[1].start()
    for copy in stores:
        copy.wait()


def u_blocks(chips, other, where, own, partner, inverse, token):
    count = len(chips)
    block = inverse.shape[1:]
    any_spec = pl.BlockSpec(memory_space=pl.ANY)
    return pl.pallas_call(
        functools.partial(u_kernel, chips, other),
        out_shape=[jax.ShapeDtypeStruct((2, count) + block, F32), jax.ShapeDtypeStruct((1,) + block, F32)],
        in_specs=[pl.BlockSpec(memory_space=SMEM)] + [any_spec] * 4,
        out_specs=[any_spec] * 2,
        scratch_shapes=[
            pltpu.VMEM((2, count) + block, F32),
            pltpu.VMEM((count + 1,) + block, F32),
            pltpu.VMEM((2, count) + block, F32),
            pltpu.VMEM((1,) + block, F32),
            pltpu.SemaphoreType.DMA((3, count + 1)),
        ],
        compiler_params=pltpu.CompilerParams(vmem_limit_bytes=VMEM_LIMIT),
        cost_estimate=cost(COSTS["u"]),
        name="u_blocks",
    )(where, own, partner, inverse, token)


def sums_kernel(dims, plan, where, tables, near, far, *refs):
    rows, zs, chip_of, sets, hops = dims
    arrays, refs = refs[: sets * hops], refs[sets * hops :]
    z_out, p_outs, (u_buf, buf, z_buf, p_buf, sems) = refs[0], refs[1:4], refs[4:]
    per_set = u_buf.shape[2]
    pieces = u_buf.shape[1]
    width = u_buf.shape[-1]
    cols = near.shape[1]
    my_x = lax.rem(lax.div(where[0], 2), 2)
    my_z = lax.div(where[0], 4)
    sigma_loads = [
        pltpu.make_async_copy(near, buf.at[:, pl.ds(0, cols)], sems.at[0]),
        pltpu.make_async_copy(far, buf.at[:, pl.ds(cols, far.shape[1])], sems.at[1]),
    ]
    u_loads = [
        [
            pltpu.make_async_copy(arrays[a * hops + h].at[s], u_buf.at[a, s * hops + h], sems.at[2 + a])
            for h in range(hops)
            for s in range(2)
        ]
        for a in range(sets)
    ]
    for copies in [u_loads[0], sigma_loads] + u_loads[1:]:
        for copy in copies:
            copy.start()
    p_buf[...] = jnp.zeros_like(p_buf)

    def slot_of(kk, i):
        return tables[plan.slot + kk * rows + i]

    def products(kk, a, t, chosen):
        spots = [p_buf.shape[0] // 2 * (a // 2) + zs, p_buf.shape[0] // 2 * (a // 2)]
        chip = chip_of[0]
        at = (a % 2) * per_set + t
        for index in range(1, len(chip_of)):
            chip = jnp.where(at == index, chip_of[index], chip)
        spot = jnp.where(lax.rem(chip, 2) == my_x, spots[1], spots[0]) + lax.rem(lax.div(chip, 2) - my_z + zs, zs)
        y = jnp.zeros((len(chosen) * width, 2 * width), F32)
        for j in range(pieces):
            place = tables[plan.place + kk * pieces + j]
            left = jnp.concatenate([buf[i, place] for i in chosen], axis=0)
            y = y + dot(wide(left), tall(u_buf[a, j, t]))
        y = fold(y)
        for k, i in enumerate(chosen):
            part = y[k * width : (k + 1) * width]
            z_buf[kk, i] = -part
            p_buf[spot] += dot_t(u_buf[a, slot_of(kk, i), t], part)

    def node(kk, a, t):
        count = jnp.int32(0)
        for i in range(rows):
            count += jnp.where(slot_of(kk, i) >= 0, 1, 0)
        for i in range(rows):

            @pl.when(slot_of(kk, i) < 0)
            def absent():
                z_buf[kk, i] = jnp.zeros((width, width), F32)

        first = jnp.int32(rows - 1)
        last = jnp.int32(0)
        for i in range(rows):
            here = slot_of(kk, i) >= 0
            last = jnp.where(here, i, last)
            first = jnp.where(here, jnp.minimum(first, i), first)

        @pl.when(count == 1)
        def single():
            products(kk, a, t, [first])

        @pl.when(count == 2)
        def double():
            products(kk, a, t, [first, last])

        @pl.when(count >= 3)
        def several():
            products(kk, a, t, list(range(rows)))

    stores = []
    for a in range(sets):
        for copy in u_loads[a] + (sigma_loads if a == 0 else []):
            copy.wait()

        def step(t, carry):
            node(a * per_set + t, a, t)
            return carry

        lax.fori_loop(0, per_set, step, 0)
        for t in range(per_set):
            kk = a * per_set + t
            stores.append(pltpu.make_async_copy(z_buf.at[kk], z_out.at[tables[plan.node + kk]], sems.at[2 + sets]))
            stores[-1].start()
    for k, p_out in enumerate(p_outs):
        size = zs if k < 2 else 2 * zs
        stores.append(pltpu.make_async_copy(p_buf.at[pl.ds(k * zs, size)], p_out, sems.at[3 + sets + k]))
        stores[-1].start()
    for copy in stores:
        copy.wait()


def all_sums(plan, where, tables, near, far, u_sets, chip_of, zs):
    _, per_set, width, _ = u_sets[0][0].shape
    sets, hops = len(u_sets), len(u_sets[0])
    pieces = 2 * hops
    rows, cols = near.shape[:2]
    nodes = sets * per_set
    any_spec = pl.BlockSpec(memory_space=pl.ANY)
    smem = pl.BlockSpec(memory_space=SMEM)
    operands = [near, far] + [u for arrays in u_sets for u in arrays]
    shapes = [(nodes, rows), (zs,), (zs,), (2 * zs,)]
    return pl.pallas_call(
        functools.partial(sums_kernel, (rows, zs, chip_of, sets, hops), plan),
        in_specs=[smem, smem] + [any_spec] * len(operands),
        out_specs=[any_spec] * len(shapes),
        out_shape=[jax.ShapeDtypeStruct(shape + (width, width), F32) for shape in shapes],
        scratch_shapes=[
            pltpu.VMEM((sets, pieces, per_set, width, width), F32),
            pltpu.VMEM((rows, cols + far.shape[1], width, width), F32),
            pltpu.VMEM((nodes, rows, width, width), F32),
            pltpu.VMEM((4 * zs, width, width), F32),
            pltpu.SemaphoreType.DMA((6 + sets,)),
        ],
        compiler_params=pltpu.CompilerParams(vmem_limit_bytes=VMEM_LIMIT),
        cost_estimate=cost(COSTS["sums"]),
        name="all_sums",
    )(where, tables, *operands)


def ring_order(chips):
    return list(range(0, chips, 2)) + list(range(1, chips, 2))[::-1]


def body(n_row, n_col, sigma, factor, diag_inv, struct):
    rows, cols, width, _ = sigma.shape
    nodes = diag_inv.shape[0]
    window = cols * n_col
    chips = n_row // 2
    order = ring_order(chips)
    zs = chips // 2
    row = lax.axis_index("row")
    col = lax.axis_index("col")
    permute = lax.ppermute
    where = jnp.stack([row, col]).astype(I32)

    def pairs(step):
        return [(order[i] * 2 + c, order[(i + step) % chips] * 2 + c) for i in range(chips) for c in range(2)]

    swap_core = [(r, r ^ 1) for r in range(n_row)]
    swap_x = [(r, r ^ 2) for r in range(n_row)]
    full_hops = (chips - 1) // 2

    table = np.zeros((n_row, n_row), np.int32)
    for r in range(n_row):
        p = order.index(r // 2)
        hops = [0] + [-h for h in range(1, full_hops + 1)] + list(range(1, full_hops + 1)) + [chips // 2]
        for w in range(2):
            for j, h in enumerate(hops):
                table[r, w * chips + j] = 2 * order[(p + h) % chips] + ((r % 2) ^ w)
    pieces = n_row

    chunk_z = [[0, zs - 1], list(range(1, zs - 1))]
    chunks = [[2 * z + x for z in zz for x in range(2)] for zz in chunk_z]
    chip_of = sum(chunks, [])

    def swapped(array):
        return permute(array, "row", swap_core)

    def tie(values, *tokens):
        return lax.optimization_barrier((*values, *tokens))[: len(values)]

    def over_col(source):
        got = [permute(source, "col", [((c + d) % n_col, c) for c in range(n_col)]) for d in range(1, n_col)]
        return got[0] if len(got) == 1 else jnp.concatenate(got, axis=1)

    own_factor = factor[0]
    part_factor = swapped(own_factor)
    far = over_col(sigma)
    u_own = []
    for chunk in chunks:
        u, square = u_blocks(chunk, False, where, own_factor, part_factor, diag_inv, struct)
        u_own.append(u)
    moved = [[(u, u)] for u in u_own]
    plan = Plan(nodes, pieces, rows)
    tables = None
    for hop in range(full_hops + 1):
        for k in range(2):
            front = tie(moved[k][hop])
            if hop == 2 and k == 0:
                front = tie(front, tables)
            if hop == full_hops and k == 0:
                front = tie(front, *u_other)
            ways = ((1, -1) if hop < full_hops else (1,) if k == 0 else (-1,))
            moved[k].append(tuple(permute(front[0 if way > 0 else 1], "row", pairs(way)) for way in ways))
        if hop == 1:
            u_other = [
                u_blocks(chunk, True, where, own_factor, part_factor, diag_inv, moved[0][2][0])[0] for chunk in chunks
            ]
        if hop == 0:
            tables = make_plan(
                plan, (nodes, pieces, rows, cols, n_col), where, table.reshape(-1), np.asarray(chip_of, np.int32), struct, moved[0][1][0]
            )
    gathered = [
        [u_own[k]] + [r for r, _ in moved[k][1:-1]] + [l for _, l in moved[k][1:-1]] + list(moved[k][-1])
        for k in range(2)
    ]
    for k in range(2):
        pieces_here = tie(tuple(gathered[k][1:]), *moved[k][-1])
        gathered.append([u_other[k]] + [swapped(u) for u in pieces_here])
    z_off, mine, across, theirs = all_sums(plan, where, tables, sigma, far, gathered, chip_of, zs)

    got = swapped(theirs)
    part_sum = (mine + got[:zs]) + permute(across + got[zs:], "row", swap_x)
    z_diag = square + part_sum[:1]
    for m in range(1, zs):
        links = [(r, (r + 4 * m) % n_row) for r in range(n_row)]
        z_diag = z_diag + permute(part_sum[m : m + 1], "row", links)
    return z_off, z_diag


def solution(mesh):
    in_specs = (
        P("row", "col", None, None),
        P("row", "col", None, None),
        P("col", None, None),
        P("col", None),
    )
    out_specs = (P("col", "row", None, None), P(("col", "row"), None, None))
    run = functools.partial(body, mesh.shape["row"], mesh.shape["col"])
    return jax.shard_map(run, mesh=mesh, in_specs=in_specs, out_specs=out_specs, check_vma=False)
```

time: 657 us -> 149 us (0.23)
  waiting for transfers between devices: 334 us -> 80.5 us
  matrix products: 119 us -> 0 us
  local copies, waits for them, and re-layouts: 120 us -> 2.07 us
  other arithmetic: 67.2 us -> 3.23 us
  Pallas kernels: 0 us -> 34.1 us
  starting transfers between devices: 0.12 us -> 27 us
  between operations: 13.8 us -> 0.81 us
    all_gather x2 -> x0, waiting for transfers between devices: 246 us -> none  [the longest x1 129 us: body(): lax.all_gather(u_local, 'row', axis=0, tiled=True)]
    dot_general x19 -> x0, matrix products: 119 us -> none  [the longest x16 106 us: one_slot(): jnp.einsum('akij,kjl->kail', picked, u_slot, precision=highest)]
    gather x16 -> x0, local copies, waits for them, and re-layouts: 97 us -> none  [select_blocks(): return jnp.take(sigma_rows, slot_ids, axis=1)]
    psum x1 -> x0, waiting for transfers between devices: 87.4 us -> none  [body(): summed = lax.psum(partial_sum, 'row')]
    ppermute x0 -> x35, waiting for transfers between devices: none -> 80.5 us  [the longest x14 56.8 us: body(): permute(front[0 if way > 0 else 1], 'row', pairs(way))]
    add x33 -> x3, other arithmetic: 61.5 us -> 2.64 us  [the longest x2 1.99 us: body(): part_sum = mine + got[:zs] + permute(across + got[zs:], 'row', swap_x)]
    pallas_call x0 -> x6, Pallas kernels: none -> 34.1 us  [the longest x1 16.8 us: all_sums(): pl.pallas_call(functools.partial(sums_kernel, (rows, zs, chip_of, sets, h...]
    ppermute x0 -> x35, starting transfers between devices: none -> 27 us  [the longest x14 14.1 us: body(): permute(front[0 if way > 0 else 1], 'row', pairs(way))]
  transfers between devices with their start and end apart: 3 -> 35, of which waited for: 3 -> 32; matrix products, arithmetic and copies ran while one was open for 1% -> 0% of each run, Pallas kernels for 0% -> 12%
where the time goes in v1:
time: 149 us; the launch traced here: 148 us
  waiting for transfers between devices  80.5 us (54%)
  Pallas kernels  34.1 us (23%)
  starting transfers between devices  27 us (18%)
  other arithmetic  3.23 us (2%)
  local copies, waits for them, and re-layouts  2.07 us (1%)
    ppermute x14, waiting for transfers between devices, body(): permute(front[0 if way > 0 else 1], 'row', pairs(way))  56.8 us
    pallas_call x1, Pallas kernels, all_sums(): pl.pallas_call(functools.partial(sums_kernel, (rows, zs, chip_of, sets, h...  16.8 us
    ppermute x14, starting transfers between devices, body(): permute(front[0 if way > 0 else 1], 'row', pairs(way))  14.1 us
    pallas_call x4, Pallas kernels, u_blocks(): pl.pallas_call(functools.partial(u_kernel, chips, other), out_shape=[jax....  13.3 us
    ppermute x16, waiting for transfers between devices, swapped(): return permute(array, 'row', swap_core)  10.4 us
    ppermute x1, waiting for transfers between devices, body(): part_sum = mine + got[:zs] + permute(across + got[zs:], 'row', swap_x)  6.61 us
    ppermute x3, waiting for transfers between devices, body(): z_diag = z_diag + permute(part_sum[m:m + 1], 'row', links)  5.31 us
    ppermute x3, starting transfers between devices, body(): z_diag = z_diag + permute(part_sum[m:m + 1], 'row', links)  4.61 us
  transfers between devices with their start and end apart: 35, of which 32 were waited for; matrix products, arithmetic and copies ran while one was open for 0% of the time, Pallas kernels for 12%

profile of v1, /device:TPU:0, one launch (start us, length us, event | category | flops | bytes accessed | tf_op | source)
XLA Modules:
  0.0 147.7 jit_solution(2662489007197344550)
XLA Ops:
  0.6 0.5 collective-permute-start
  1.1 2.6 %collective-permute-start.2 = (f32[3,24,128,128]{3,2,1,0:T(8,128)}, f32[3,24,128,128]{3,2,1,0:T(8,128)}, u32[]{:S(2)}, u32[]{:S(2)}) collective-permute-start(f32[3,24,128,128]{3,2,1,0:T(8,128)} %near.1), channel_id=1, source_target_pairs={{1,0},{0,1},{3,2},{2,3},{5,4},{4,5},{7,6},{6,7},{9,8},{8,9},{11,10... | collective-permute-start | bytes 14155784 | tf_op jit(solution)/shard_map/ppermute | solution.py:335
  3.7 0.6 pad_add_fusion.where
  4.3 1.0 copy-done.21
  5.3 3.3 %u_blocks.7 = (f32[2,4,128,128]{3,2,1,0:T(8,128)}, f32[1,128,128]{2,1,0:T(8,128)}) custom-call(s32[2]{0:T(128)} %pad_add_fusion.where, f32[16,128,128]{2,1,0:T(8,128)} %bitcast.4, f32[16,128,128]{2,1,0:T(8,128)} %copy-done.21, f32[16,128,128]{2,1,0:T(8,128)} %inverse.7, s32[16,16]{1,0:T(8,128)} %token_.3), custom_call_target="tpu_custom_call" | custom-call | flops 1000000000 | bytes 1000 | tf_op jit(solution)/shard_map/u_blocks/pallas_call | solution.py:147
  8.6 2.3 %collective-permute-start.9 = (f32[2,4,128,128]{3,2,1,0:T(8,128)}, f32[2,4,128,128]{3,2,1,0:T(8,128)S(1)}, u32[]{:S(2)}, u32[]{:S(2)}) collective-permute-start(f32[2,4,128,128]{3,2,1,0:T(8,128)} %get-tuple-element.57.refs_8_), channel_id=1, source_target_pairs={{0,8},{2,10},{8,16},{10,18},{16,24},{18,26},{24,28},{26,30},{28,20... | collective-permute-start | bytes 1572872 | tf_op jit(solution)/shard_map/ppermute | solution.py:356
  10.9 3.3 %u_blocks.4 = (f32[2,4,128,128]{3,2,1,0:T(8,128)}, f32[1,128,128]{2,1,0:T(8,128)}) custom-call(s32[2]{0:T(128)} %pad_add_fusion.where, f32[16,128,128]{2,1,0:T(8,128)} %bitcast.5, f32[16,128,128]{2,1,0:T(8,128)} %copy-done.21, f32[16,128,128]{2,1,0:T(8,128)} %inverse.7, s32[16,16]{1,0:T(8,128)} %token_.3), custom_call_target="tpu_custom_call" | custom-call | flops 1000000000 | bytes 1000 | tf_op jit(solution)/shard_map/u_blocks/pallas_call | solution.py:147
  14.3 2.1 %collective-permute-start.1 = (f32[2,4,128,128]{3,2,1,0:T(8,128)}, f32[2,4,128,128]{3,2,1,0:T(8,128)}, u32[]{:S(2)}, u32[]{:S(2)}) collective-permute-start(f32[2,4,128,128]{3,2,1,0:T(8,128)} %get-tuple-element.44.refs_0_), channel_id=1, source_target_pairs={{0,8},{2,10},{8,16},{10,18},{16,24},{18,26},{24,28},{26,30},{28,20... | collective-permute-start | bytes 1572872 | tf_op jit(solution)/shard_map/ppermute | solution.py:356
  16.4 7.4 %collective-permute-done.9.refs_9_ = f32[2,4,128,128]{3,2,1,0:T(8,128)S(1)} collective-permute-done((f32[2,4,128,128]{3,2,1,0:T(8,128)}, f32[2,4,128,128]{3,2,1,0:T(8,128)S(1)}, u32[]{:S(2)}, u32[]{:S(2)}) %collective-permute-start.9) | collective-permute-done | bytes 524320 | tf_op jit(solution)/shard_map/ppermute | solution.py:356
  23.8 2.2 %collective-permute-done.10.refs_12_ = f32[2,4,128,128]{3,2,1,0:T(8,128)S(1)} collective-permute-done((f32[2,4,128,128]{3,2,1,0:T(8,128)}, f32[2,4,128,128]{3,2,1,0:T(8,128)S(1)}, u32[]{:S(2)}, u32[]{:S(2)}) %collective-permute-start.10) | collective-permute-done | bytes 524320 | tf_op jit(solution)/shard_map/ppermute | solution.py:356
  26.0 1.6 %collective-permute-start.11 = (f32[2,4,128,128]{3,2,1,0:T(8,128)S(1)}, f32[2,4,128,128]{3,2,1,0:T(8,128)S(1)}, u32[]{:S(2)}, u32[]{:S(2)}) collective-permute-start(f32[2,4,128,128]{3,2,1,0:T(8,128)S(1)} %collective-permute-done.9.refs_9_), channel_id=1, source_target_pairs={{0,8},{2,10},{8,16},{10,18},{16,24},{18,26},{24,28},{26,30},{28,20... | collective-permute-start | bytes 1572872 | tf_op jit(solution)/shard_map/ppermute | solution.py:356
  27.5 0.4 collective-permute-start.12
  28.0 7.1 %collective-permute-done.1.token.refs_1_ = f32[2,4,128,128]{3,2,1,0:T(8,128)} collective-permute-done((f32[2,4,128,128]{3,2,1,0:T(8,128)}, f32[2,4,128,128]{3,2,1,0:T(8,128)}, u32[]{:S(2)}, u32[]{:S(2)}) %collective-permute-start.1) | collective-permute-done | bytes 524320 | tf_op jit(solution)/shard_map/ppermute | solution.py:356
  35.1 2.1 %collective-permute-done.3.refs_4_ = f32[2,4,128,128]{3,2,1,0:T(8,128)S(1)} collective-permute-done((f32[2,4,128,128]{3,2,1,0:T(8,128)}, f32[2,4,128,128]{3,2,1,0:T(8,128)S(1)}, u32[]{:S(2)}, u32[]{:S(2)}) %collective-permute-start.3) | collective-permute-done | bytes 524320 | tf_op jit(solution)/shard_map/ppermute | solution.py:356
  37.2 1.6 %collective-permute-start.4 = (f32[2,4,128,128]{3,2,1,0:T(8,128)}, f32[2,4,128,128]{3,2,1,0:T(8,128)}, u32[]{:S(2)}, u32[]{:S(2)}) collective-permute-start(f32[2,4,128,128]{3,2,1,0:T(8,128)} %collective-permute-done.1.token.refs_1_), channel_id=1, source_target_pairs={{0,8},{2,10},{8,16},{10,18},{16,24},{18,26},{24,28},{26,30},{28,20... | collective-permute-start | bytes 1572872 | tf_op jit(solution)/shard_map/ppermute | solution.py:356
  38.8 0.4 collective-permute-start.5
  39.2 7.0 %collective-permute-done.11.refs_10_ = f32[2,4,128,128]{3,2,1,0:T(8,128)S(1)} collective-permute-done((f32[2,4,128,128]{3,2,1,0:T(8,128)S(1)}, f32[2,4,128,128]{3,2,1,0:T(8,128)S(1)}, u32[]{:S(2)}, u32[]{:S(2)}) %collective-permute-start.11) | collective-permute-done | bytes 524320 | tf_op jit(solution)/shard_map/ppermute | solution.py:356
  46.2 2.2 %collective-permute-done.12.refs_13_ = f32[2,4,128,128]{3,2,1,0:T(8,128)S(1)} collective-permute-done((f32[2,4,128,128]{3,2,1,0:T(8,128)S(1)}, f32[2,4,128,128]{3,2,1,0:T(8,128)S(1)}, u32[]{:S(2)}, u32[]{:S(2)}) %collective-permute-start.12) | collective-permute-done | bytes 524320 | tf_op jit(solution)/shard_map/ppermute | solution.py:356
  48.4 1.6 %collective-permute-start.13 = (f32[2,4,128,128]{3,2,1,0:T(8,128)S(1)}, f32[2,4,128,128]{3,2,1,0:T(8,128)}, u32[]{:S(2)}, u32[]{:S(2)}) collective-permute-start(f32[2,4,128,128]{3,2,1,0:T(8,128)S(1)} %collective-permute-done.11.refs_10_), channel_id=1, source_target_pairs={{0,8},{2,10},{8,16},{10,18},{16,24},{18,26},{24,28},{26,30},{28,20... | collective-permute-start | bytes 1572872 | tf_op jit(solution)/shard_map/ppermute | solution.py:356
  50.0 0.4 collective-permute-start.14
  50.5 4.1 %plan.1.tables = s32[321]{0:T(512)} custom-call(s32[2]{0:T(128)} %pad_add_fusion.where, s32[256]{0:T(256)} %constant.12.clone.table, s32[8]{0:T(128)} %constant.13.clone.chip_of, s32[16,16]{1,0:T(8,128)} %token_.3, f32[2,4,128,128]{3,2,1,0:T(8,128)} %collective-permute-done.1.token.refs_1_), custom_call_target="tpu_custom_call" | custom-call | flops 1000000000 | bytes 1000 | tf_op jit(solution)/shard_map/plan/pallas_call | solution.py:98
  54.5 3.0 %collective-permute-done.4.token.refs_2_ = f32[2,4,128,128]{3,2,1,0:T(8,128)} collective-permute-done((f32[2,4,128,128]{3,2,1,0:T(8,128)}, f32[2,4,128,128]{3,2,1,0:T(8,128)}, u32[]{:S(2)}, u32[]{:S(2)}) %collective-permute-start.4) | collective-permute-done | bytes 524320 | tf_op jit(solution)/shard_map/ppermute | solution.py:356
  57.6 2.2 %collective-permute-done.5.refs_5_ = f32[2,4,128,128]{3,2,1,0:T(8,128)} collective-permute-done((f32[2,4,128,128]{3,2,1,0:T(8,128)S(1)}, f32[2,4,128,128]{3,2,1,0:T(8,128)}, u32[]{:S(2)}, u32[]{:S(2)}) %collective-permute-start.5) | collective-permute-done | bytes 524320 | tf_op jit(solution)/shard_map/ppermute | solution.py:356
  59.8 1.6 %collective-permute-start.6 = (f32[2,4,128,128]{3,2,1,0:T(8,128)}, f32[2,4,128,128]{3,2,1,0:T(8,128)}, u32[]{:S(2)}, u32[]{:S(2)}) collective-permute-start(f32[2,4,128,128]{3,2,1,0:T(8,128)} %collective-permute-done.4.token.refs_2_), channel_id=1, source_target_pairs={{0,8},{2,10},{8,16},{10,18},{16,24},{18,26},{24,28},{26,30},{28,20... | collective-permute-start | bytes 1572872 | tf_op jit(solution)/shard_map/ppermute | solution.py:356
  61.4 0.4 collective-permute-start.7
  61.8 7.0 %collective-permute-done.13.refs_11_ = f32[2,4,128,128]{3,2,1,0:T(8,128)} collective-permute-done((f32[2,4,128,128]{3,2,1,0:T(8,128)S(1)}, f32[2,4,128,128]{3,2,1,0:T(8,128)}, u32[]{:S(2)}, u32[]{:S(2)}) %collective-permute-start.13) | collective-permute-done | bytes 524320 | tf_op jit(solution)/shard_map/ppermute | solution.py:356
  68.8 2.2 %collective-permute-done.14.refs_14_ = f32[2,4,128,128]{3,2,1,0:T(8,128)} collective-permute-done((f32[2,4,128,128]{3,2,1,0:T(8,128)S(1)}, f32[2,4,128,128]{3,2,1,0:T(8,128)}, u32[]{:S(2)}, u32[]{:S(2)}) %collective-permute-start.14) | collective-permute-done | bytes 524320 | tf_op jit(solution)/shard_map/ppermute | solution.py:356
  71.0 3.3 %u_blocks.6 = (f32[2,4,128,128]{3,2,1,0:T(8,128)}, f32[1,128,128]{2,1,0:T(8,128)}) custom-call(s32[2]{0:T(128)} %pad_add_fusion.where, f32[16,128,128]{2,1,0:T(8,128)} %bitcast.6, f32[16,128,128]{2,1,0:T(8,128)} %copy-done.21, f32[16,128,128]{2,1,0:T(8,128)} %inverse.7, f32[2,4,128,128]{3,2,1,0:T(8,128)} %collective-permute-done.4.token.refs_2_), custom_call_target="tpu_custom_call" | custom-call | flops 1000000000 | bytes 1000 | tf_op jit(solution)/shard_map/u_blocks/pallas_call | solution.py:147
  74.3 3.3 %u_blocks.5 = (f32[2,4,128,128]{3,2,1,0:T(8,128)}, f32[1,128,128]{2,1,0:T(8,128)}) custom-call(s32[2]{0:T(128)} %pad_add_fusion.where, f32[16,128,128]{2,1,0:T(8,128)} %bitcast.7, f32[16,128,128]{2,1,0:T(8,128)} %copy-done.21, f32[16,128,128]{2,1,0:T(8,128)} %inverse.7, f32[2,4,128,128]{3,2,1,0:T(8,128)} %collective-permute-done.4.token.refs_2_), custom_call_target="tpu_custom_call" | custom-call | flops 1000000000 | bytes 1000 | tf_op jit(solution)/shard_map/u_blocks/pallas_call | solution.py:147
  77.7 1.9 %collective-permute-done.6.refs_3_ = f32[2,4,128,128]{3,2,1,0:T(8,128)} collective-permute-done((f32[2,4,128,128]{3,2,1,0:T(8,128)}, f32[2,4,128,128]{3,2,1,0:T(8,128)}, u32[]{:S(2)}, u32[]{:S(2)}) %collective-permute-start.6) | collective-permute-done | bytes 524320 | tf_op jit(solution)/shard_map/ppermute | solution.py:356
  79.6 2.7 %collective-permute-done.7.refs_6_ = f32[2,4,128,128]{3,2,1,0:T(8,128)} collective-permute-done((f32[2,4,128,128]{3,2,1,0:T(8,128)}, f32[2,4,128,128]{3,2,1,0:T(8,128)}, u32[]{:S(2)}, u32[]{:S(2)}) %collective-permute-start.7) | collective-permute-done | bytes 524320 | tf_op jit(solution)/shard_map/ppermute | solution.py:356
  82.2 1.6 %collective-permute-start.8 = (f32[2,4,128,128]{3,2,1,0:T(8,128)}, f32[2,4,128,128]{3,2,1,0:T(8,128)S(1)}, u32[]{:S(2)}, u32[]{:S(2)}) collective-permute-start(f32[2,4,128,128]{3,2,1,0:T(8,128)} %collective-permute-done.6.refs_3_), channel_id=1, source_target_pairs={{0,8},{2,10},{8,16},{10,18},{16,24},{18,26},{24,28},{26,30},{28,20... | collective-permute-start | bytes 1572872 | tf_op jit(solution)/shard_map/ppermute | solution.py:356
  83.8 8.5 %collective-permute-done.15.refs_15_ = f32[2,4,128,128]{3,2,1,0:T(8,128)} collective-permute-done((f32[2,4,128,128]{3,2,1,0:T(8,128)}, f32[2,4,128,128]{3,2,1,0:T(8,128)}, u32[]{:S(2)}, u32[]{:S(2)}) %collective-permute-start.15) | collective-permute-done | bytes 524320 | tf_op jit(solution)/shard_map/ppermute | solution.py:356
  92.4 0.5 collective-permute-start.24
  92.9 1.3 collective-permute-done.8.refs_7_
  94.2 0.8 collective-permute-done.23.refs_25_
  95.0 0.1 collective-permute-start.27
  95.2 0.3 collective-permute-start.28
  95.5 0.5 collective-permute-done.25.refs_27_
  96.1 0.4 collective-permute-done.26.refs_28_
  96.7 0.8 collective-permute-done.27.refs_29_
  97.6 0.6 collective-permute-done.28.refs_30_
  98.4 0.6 collective-permute-done.29.refs_31_
  99.1 0.6 collective-permute-done.16.refs_17_
  99.9 0.6 collective-permute-done.17.refs_18_
  100.6 1.4 collective-permute-done.18.refs_19_
  102.1 0.6 collective-permute-done.20.refs_21_
  102.7 0.7 collective-permute-done.21.refs_22_
  103.5 0.5 collective-permute-done.22.refs_23_
  104.1 0.2 copy-done.18
  104.3 0.8 copy-done.19
  105.1 1.3 collective-permute-done.2.far
  106.5 16.8 %all_sums.1 = (f32[16,3,128,128]{3,2,1,0:T(8,128)}, f32[4,128,128]{2,1,0:T(8,128)}, f32[4,128,128]{2,1,0:T(8,128)}, f32[8,128,128]{2,1,0:T(8,128)}) custom-call(s32[2]{0:T(128)} %pad_add_fusion.where, s32[321]{0:T(512)} %plan.1.tables, f32[3,24,128,128]{3,2,1,0:T(8,128)} %near.1, f32[3,24,128,128]{3,2,1,0:T(8,128)} %collective-permute-done.2.far, ...), custom_call_target="tpu_custom_call" | custom-call | flops 3000000000 | bytes 1000 | tf_op jit(solution)/shard_map/all_sums/pallas_call | solution.py:274
  123.3 2.1 %collective-permute-done.30 = f32[8,128,128]{2,1,0:T(8,128)S(1)} collective-permute-done((f32[8,128,128]{2,1,0:T(8,128)}, f32[8,128,128]{2,1,0:T(8,128)S(1)}, u32[]{:S(2)}, u32[]{:S(2)}) %collective-permute-start.30) | collective-permute-done | bytes 524320 | tf_op jit(solution)/shard_map/ppermute | solution.py:329
  125.4 1.0 slice_add_fusion
  126.4 3.1 %collective-permute-start.31 = (f32[4,128,128]{2,1,0:T(8,128)S(1)}, f32[4,128,128]{2,1,0:T(8,128)S(1)}, u32[]{:S(2)}, u32[]{:S(2)}) collective-permute-start(f32[4,128,128]{2,1,0:T(8,128)S(1)} %slice_add_fusion), channel_id=1, source_target_pairs={{0,4},{2,6},{4,0},{6,2},{8,12},{10,14},{12,8},{14,10},{16,20},{18,... | collective-permute-start | bytes 786440 | tf_op jit(solution)/shard_map/ppermute | solution.py:375
  129.5 6.6 %collective-permute-done.31 = f32[4,128,128]{2,1,0:T(8,128)S(1)} collective-permute-done((f32[4,128,128]{2,1,0:T(8,128)S(1)}, f32[4,128,128]{2,1,0:T(8,128)S(1)}, u32[]{:S(2)}, u32[]{:S(2)}) %collective-permute-start.31) | collective-permute-done | bytes 262176 | tf_op jit(solution)/shard_map/ppermute | solution.py:375
  136.1 1.0 fusion
  137.1 1.4 collective-permute-start.32
  138.5 2.5 %collective-permute-start.34 = (f32[1,128,128]{2,1,0:T(8,128)S(1)}, f32[1,128,128]{2,1,0:T(8,128)S(1)}, u32[]{:S(2)}, u32[]{:S(2)}) collective-permute-start(f32[1,128,128]{2,1,0:T(8,128)S(1)} %get-tuple-element.83), channel_id=1, source_target_pairs={{0,24},{2,26},{4,28},{6,30},{8,0},{10,2},{12,4},{14,6},{16,8},{18,... | collective-permute-start | bytes 196616 | tf_op jit(solution)/shard_map/ppermute | solution.py:379
  141.0 0.7 collective-permute-start.33
  141.8 1.9 %collective-permute-done.32 = f32[1,128,128]{2,1,0:T(8,128)S(1)} collective-permute-done((f32[1,128,128]{2,1,0:T(8,128)S(1)}, f32[1,128,128]{2,1,0:T(8,128)S(1)}, u32[]{:S(2)}, u32[]{:S(2)}) %collective-permute-start.32) | collective-permute-done | bytes 65568 | tf_op jit(solution)/shard_map/ppermute | solution.py:379
  143.7 3.4 %collective-permute-done.33 = f32[1,128,128]{2,1,0:T(8,128)S(1)} collective-permute-done((f32[1,128,128]{2,1,0:T(8,128)S(1)}, f32[1,128,128]{2,1,0:T(8,128)S(1)}, u32[]{:S(2)}, u32[]{:S(2)}) %collective-permute-start.33) | collective-permute-done | bytes 65568 | tf_op jit(solution)/shard_map/ppermute | solution.py:379
  147.1 0.7 fusion.3
  (61 shorter events, 1.4 us)
Async XLA Ops:
  0.6 3.7 %collective-permute-start = (f32[16,128,128]{2,1,0:T(8,128)}, f32[16,128,128]{2,1,0:T(8,128)S(1)}, u32[]{:S(2)}, u32[]{:S(2)}) collective-permute-start(f32[16,128,128]{2,1,0:T(8,128)} %bitcast.3), channel_id=1, source_target_pairs={{0,2},{2,0},{4,6},{6,4},{8,10},{10,8},{12,14},{14,12},{16,18},{18,... | collective-permute-start | bytes 3145736 | tf_op jit(solution)/shard_map/ppermute | solution.py:329
  1.1 105.3 %collective-permute-start.2 = (f32[3,24,128,128]{3,2,1,0:T(8,128)}, f32[3,24,128,128]{3,2,1,0:T(8,128)}, u32[]{:S(2)}, u32[]{:S(2)}) collective-permute-start(f32[3,24,128,128]{3,2,1,0:T(8,128)} %near.1), channel_id=1, source_target_pairs={{1,0},{0,1},{3,2},{2,3},{5,4},{4,5},{7,6},{6,7},{9,8},{8,9},{11,10... | collective-permute-start | bytes 14155784 | tf_op jit(solution)/shard_map/ppermute | solution.py:335
  4.3 1.0 copy-start.21
  8.6 15.1 %collective-permute-start.9 = (f32[2,4,128,128]{3,2,1,0:T(8,128)}, f32[2,4,128,128]{3,2,1,0:T(8,128)S(1)}, u32[]{:S(2)}, u32[]{:S(2)}) collective-permute-start(f32[2,4,128,128]{3,2,1,0:T(8,128)} %get-tuple-element.57.refs_8_), channel_id=1, source_target_pairs={{0,8},{2,10},{8,16},{10,18},{16,24},{18,26},{24,28},{26,30},{28,20... | collective-permute-start | bytes 1572872 | tf_op jit(solution)/shard_map/ppermute | solution.py:356
  10.9 15.0 %collective-permute-start.10 = (f32[2,4,128,128]{3,2,1,0:T(8,128)}, f32[2,4,128,128]{3,2,1,0:T(8,128)S(1)}, u32[]{:S(2)}, u32[]{:S(2)}) collective-permute-start(f32[2,4,128,128]{3,2,1,0:T(8,128)} %get-tuple-element.57.refs_8_), channel_id=1, source_target_pairs={{0,4},{2,6},{8,0},{10,2},{16,8},{18,10},{24,16},{26,18},{28,24},{3... | collective-permute-start | bytes 1572872 | tf_op jit(solution)/shard_map/ppermute | solution.py:356
  14.3 20.8 %collective-permute-start.1 = (f32[2,4,128,128]{3,2,1,0:T(8,128)}, f32[2,4,128,128]{3,2,1,0:T(8,128)}, u32[]{:S(2)}, u32[]{:S(2)}) collective-permute-start(f32[2,4,128,128]{3,2,1,0:T(8,128)} %get-tuple-element.44.refs_0_), channel_id=1, source_target_pairs={{0,8},{2,10},{8,16},{10,18},{16,24},{18,26},{24,28},{26,30},{28,20... | collective-permute-start | bytes 1572872 | tf_op jit(solution)/shard_map/ppermute | solution.py:356
  16.4 20.8 %collective-permute-start.3 = (f32[2,4,128,128]{3,2,1,0:T(8,128)}, f32[2,4,128,128]{3,2,1,0:T(8,128)S(1)}, u32[]{:S(2)}, u32[]{:S(2)}) collective-permute-start(f32[2,4,128,128]{3,2,1,0:T(8,128)} %get-tuple-element.44.refs_0_), channel_id=1, source_target_pairs={{0,4},{2,6},{8,0},{10,2},{16,8},{18,10},{24,16},{26,18},{28,24},{3... | collective-permute-start | bytes 1572872 | tf_op jit(solution)/shard_map/ppermute | solution.py:356
  23.8 68.6 %copy-start = (f32[2,4,128,128]{3,2,1,0:T(8,128)}, f32[2,4,128,128]{3,2,1,0:T(8,128)S(1)}, u32[]{:S(2)}) copy-start(f32[2,4,128,128]{3,2,1,0:T(8,128)S(1)} %collective-permute-done.9.refs_9_) | copy-start | bytes 1572868
  26.0 68.2 %copy-start.1 = (f32[2,4,128,128]{3,2,1,0:T(8,128)}, f32[2,4,128,128]{3,2,1,0:T(8,128)S(1)}, u32[]{:S(2)}) copy-start(f32[2,4,128,128]{3,2,1,0:T(8,128)S(1)} %collective-permute-done.10.refs_12_) | copy-start | bytes 1572868
  26.0 20.3 %collective-permute-start.11 = (f32[2,4,128,128]{3,2,1,0:T(8,128)S(1)}, f32[2,4,128,128]{3,2,1,0:T(8,128)S(1)}, u32[]{:S(2)}, u32[]{:S(2)}) collective-permute-start(f32[2,4,128,128]{3,2,1,0:T(8,128)S(1)} %collective-permute-done.9.refs_9_), channel_id=1, source_target_pairs={{0,8},{2,10},{8,16},{10,18},{16,24},{18,26},{24,28},{26,30},{28,20... | collective-permute-start | bytes 1572872 | tf_op jit(solution)/shard_map/ppermute | solution.py:356
  27.5 20.9 %collective-permute-start.12 = (f32[2,4,128,128]{3,2,1,0:T(8,128)S(1)}, f32[2,4,128,128]{3,2,1,0:T(8,128)S(1)}, u32[]{:S(2)}, u32[]{:S(2)}) collective-permute-start(f32[2,4,128,128]{3,2,1,0:T(8,128)S(1)} %collective-permute-done.10.refs_12_), channel_id=1, source_target_pairs={{0,4},{2,6},{8,0},{10,2},{16,8},{18,10},{24,16},{26,18},{28,24},{3... | collective-permute-start | bytes 1572872 | tf_op jit(solution)/shard_map/ppermute | solution.py:356
  37.2 61.8 %copy-start.2 = (f32[2,4,128,128]{3,2,1,0:T(8,128)}, f32[2,4,128,128]{3,2,1,0:T(8,128)S(1)}, u32[]{:S(2)}) copy-start(f32[2,4,128,128]{3,2,1,0:T(8,128)S(1)} %collective-permute-done.3.refs_4_) | copy-start | bytes 1572868
  37.2 20.4 %collective-permute-start.4 = (f32[2,4,128,128]{3,2,1,0:T(8,128)}, f32[2,4,128,128]{3,2,1,0:T(8,128)}, u32[]{:S(2)}, u32[]{:S(2)}) collective-permute-start(f32[2,4,128,128]{3,2,1,0:T(8,128)} %collective-permute-done.1.token.refs_1_), channel_id=1, source_target_pairs={{0,8},{2,10},{8,16},{10,18},{16,24},{18,26},{24,28},{26,30},{28,20... | collective-permute-start | bytes 1572872 | tf_op jit(solution)/shard_map/ppermute | solution.py:356
  38.8 21.0 %collective-permute-start.5 = (f32[2,4,128,128]{3,2,1,0:T(8,128)S(1)}, f32[2,4,128,128]{3,2,1,0:T(8,128)}, u32[]{:S(2)}, u32[]{:S(2)}) collective-permute-start(f32[2,4,128,128]{3,2,1,0:T(8,128)S(1)} %collective-permute-done.3.refs_4_), channel_id=1, source_target_pairs={{0,4},{2,6},{8,0},{10,2},{16,8},{18,10},{24,16},{26,18},{28,24},{3... | collective-permute-start | bytes 1572872 | tf_op jit(solution)/shard_map/ppermute | solution.py:356
  46.2 13.5 %copy-start.3 = (f32[2,4,128,128]{3,2,1,0:T(8,128)}, f32[2,4,128,128]{3,2,1,0:T(8,128)S(1)}, u32[]{:S(2)}) copy-start(f32[2,4,128,128]{3,2,1,0:T(8,128)S(1)} %collective-permute-done.11.refs_10_) | copy-start | bytes 1572868
  48.4 20.4 %copy-start.4 = (f32[2,4,128,128]{3,2,1,0:T(8,128)}, f32[2,4,128,128]{3,2,1,0:T(8,128)S(1)}, u32[]{:S(2)}) copy-start(f32[2,4,128,128]{3,2,1,0:T(8,128)S(1)} %collective-permute-done.12.refs_13_) | copy-start | bytes 1572868
  48.4 20.4 %collective-permute-start.13 = (f32[2,4,128,128]{3,2,1,0:T(8,128)S(1)}, f32[2,4,128,128]{3,2,1,0:T(8,128)}, u32[]{:S(2)}, u32[]{:S(2)}) collective-permute-start(f32[2,4,128,128]{3,2,1,0:T(8,128)S(1)} %collective-permute-done.11.refs_10_), channel_id=1, source_target_pairs={{0,8},{2,10},{8,16},{10,18},{16,24},{18,26},{24,28},{26,30},{28,20... | collective-permute-start | bytes 1572872 | tf_op jit(solution)/shard_map/ppermute | solution.py:356
  50.0 21.0 %collective-permute-start.14 = (f32[2,4,128,128]{3,2,1,0:T(8,128)S(1)}, f32[2,4,128,128]{3,2,1,0:T(8,128)}, u32[]{:S(2)}, u32[]{:S(2)}) collective-permute-start(f32[2,4,128,128]{3,2,1,0:T(8,128)S(1)} %collective-permute-done.12.refs_13_), channel_id=1, source_target_pairs={{0,4},{2,6},{8,0},{10,2},{16,8},{18,10},{24,16},{26,18},{28,24},{3... | collective-permute-start | bytes 1572872 | tf_op jit(solution)/shard_map/ppermute | solution.py:356
  59.8 19.8 %collective-permute-start.6 = (f32[2,4,128,128]{3,2,1,0:T(8,128)}, f32[2,4,128,128]{3,2,1,0:T(8,128)}, u32[]{:S(2)}, u32[]{:S(2)}) collective-permute-start(f32[2,4,128,128]{3,2,1,0:T(8,128)} %collective-permute-done.4.token.refs_2_), channel_id=1, source_target_pairs={{0,8},{2,10},{8,16},{10,18},{16,24},{18,26},{24,28},{26,30},{28,20... | collective-permute-start | bytes 1572872 | tf_op jit(solution)/shard_map/ppermute | solution.py:356
  61.4 20.9 %collective-permute-start.7 = (f32[2,4,128,128]{3,2,1,0:T(8,128)}, f32[2,4,128,128]{3,2,1,0:T(8,128)}, u32[]{:S(2)}, u32[]{:S(2)}) collective-permute-start(f32[2,4,128,128]{3,2,1,0:T(8,128)} %collective-permute-done.5.refs_5_), channel_id=1, source_target_pairs={{0,4},{2,6},{8,0},{10,2},{16,8},{18,10},{24,16},{26,18},{28,24},{3... | collective-permute-start | bytes 1572872 | tf_op jit(solution)/shard_map/ppermute | solution.py:356
  71.0 21.4 %collective-permute-start.15 = (f32[2,4,128,128]{3,2,1,0:T(8,128)}, f32[2,4,128,128]{3,2,1,0:T(8,128)}, u32[]{:S(2)}, u32[]{:S(2)}) collective-permute-start(f32[2,4,128,128]{3,2,1,0:T(8,128)} %collective-permute-done.14.refs_14_), channel_id=1, source_target_pairs={{0,4},{2,6},{8,0},{10,2},{16,8},{18,10},{24,16},{26,18},{28,24},{3... | collective-permute-start | bytes 1572872 | tf_op jit(solution)/shard_map/ppermute | solution.py:356
  82.2 64.8 %copy-start.20 = (f32[1,128,128]{2,1,0:T(8,128)S(1)}, f32[1,128,128]{2,1,0:T(8,128)}, u32[]{:S(2)}) copy-start(f32[1,128,128]{2,1,0:T(8,128)} %get-tuple-element.78) | copy-start | bytes 196612
  82.2 11.9 %collective-permute-start.8 = (f32[2,4,128,128]{3,2,1,0:T(8,128)}, f32[2,4,128,128]{3,2,1,0:T(8,128)S(1)}, u32[]{:S(2)}, u32[]{:S(2)}) collective-permute-start(f32[2,4,128,128]{3,2,1,0:T(8,128)} %collective-permute-done.6.refs_3_), channel_id=1, source_target_pairs={{0,8},{2,10},{8,16},{10,18},{16,24},{18,26},{24,28},{26,30},{28,20... | collective-permute-start | bytes 1572872 | tf_op jit(solution)/shard_map/ppermute | solution.py:356
  92.4 2.6 %collective-permute-start.23 = (f32[2,4,128,128]{3,2,1,0:T(8,128)S(1)}, f32[2,4,128,128]{3,2,1,0:T(8,128)S(1)}, u32[]{:S(2)}, u32[]{:S(2)}) collective-permute-start(f32[2,4,128,128]{3,2,1,0:T(8,128)S(1)} %collective-permute-done.9.refs_9_), channel_id=1, source_target_pairs={{0,2},{2,0},{4,6},{6,4},{8,10},{10,8},{12,14},{14,12},{16,18},{18,... | collective-permute-start | bytes 1572872 | tf_op jit(solution)/shard_map/ppermute | solution.py:329
  92.4 2.9 %collective-permute-start.24 = (f32[2,4,128,128]{3,2,1,0:T(8,128)}, f32[2,4,128,128]{3,2,1,0:T(8,128)S(1)}, u32[]{:S(2)}, u32[]{:S(2)}) collective-permute-start(f32[2,4,128,128]{3,2,1,0:T(8,128)} %copy-done.3), channel_id=1, source_target_pairs={{0,2},{2,0},{4,6},{6,4},{8,10},{10,8},{12,14},{14,12},{16,18},{18,... | collective-permute-start | bytes 1572872 | tf_op jit(solution)/shard_map/ppermute | solution.py:329
  92.9 3.1 %collective-permute-start.25 = (f32[2,4,128,128]{3,2,1,0:T(8,128)}, f32[2,4,128,128]{3,2,1,0:T(8,128)S(1)}, u32[]{:S(2)}, u32[]{:S(2)}) collective-permute-start(f32[2,4,128,128]{3,2,1,0:T(8,128)} %collective-permute-done.13.refs_11_), channel_id=1, source_target_pairs={{0,2},{2,0},{4,6},{6,4},{8,10},{10,8},{12,14},{14,12},{16,18},{18,... | collective-permute-start | bytes 1572872 | tf_op jit(solution)/shard_map/ppermute | solution.py:329
  94.2 8.0 %copy-start.5 = (f32[2,4,128,128]{3,2,1,0:T(8,128)}, f32[2,4,128,128]{3,2,1,0:T(8,128)S(1)}, u32[]{:S(2)}) copy-start(f32[2,4,128,128]{3,2,1,0:T(8,128)S(1)} %collective-permute-done.8.refs_7_) | copy-start | bytes 1572868
  94.2 2.4 %collective-permute-start.26 = (f32[2,4,128,128]{3,2,1,0:T(8,128)S(1)}, f32[2,4,128,128]{3,2,1,0:T(8,128)S(1)}, u32[]{:S(2)}, u32[]{:S(2)}) collective-permute-start(f32[2,4,128,128]{3,2,1,0:T(8,128)S(1)} %collective-permute-done.10.refs_12_), channel_id=1, source_target_pairs={{0,2},{2,0},{4,6},{6,4},{8,10},{10,8},{12,14},{14,12},{16,18},{18,... | collective-permute-start | bytes 1572872 | tf_op jit(solution)/shard_map/ppermute | solution.py:329
  95.0 9.0 %copy-start.6 = (f32[2,4,128,128]{3,2,1,0:T(8,128)}, f32[2,4,128,128]{3,2,1,0:T(8,128)S(1)}, u32[]{:S(2)}) copy-start(f32[2,4,128,128]{3,2,1,0:T(8,128)S(1)} %collective-permute-done.23.refs_25_) | copy-start | bytes 1572868
  95.0 2.5 %collective-permute-start.27 = (f32[2,4,128,128]{3,2,1,0:T(8,128)}, f32[2,4,128,128]{3,2,1,0:T(8,128)S(1)}, u32[]{:S(2)}, u32[]{:S(2)}) collective-permute-start(f32[2,4,128,128]{3,2,1,0:T(8,128)} %copy-done.4), channel_id=1, source_target_pairs={{0,2},{2,0},{4,6},{6,4},{8,10},{10,8},{12,14},{14,12},{16,18},{18,... | collective-permute-start | bytes 1572872 | tf_op jit(solution)/shard_map/ppermute | solution.py:329
  95.2 8.8 %copy-start.7 = (f32[2,4,128,128]{3,2,1,0:T(8,128)}, f32[2,4,128,128]{3,2,1,0:T(8,128)S(1)}, u32[]{:S(2)}) copy-start(f32[2,4,128,128]{3,2,1,0:T(8,128)S(1)} %collective-permute-done.24.refs_26_) | copy-start | bytes 1572868
  95.2 3.0 %collective-permute-start.28 = (f32[2,4,128,128]{3,2,1,0:T(8,128)}, f32[2,4,128,128]{3,2,1,0:T(8,128)S(1)}, u32[]{:S(2)}, u32[]{:S(2)}) collective-permute-start(f32[2,4,128,128]{3,2,1,0:T(8,128)} %collective-permute-done.14.refs_14_), channel_id=1, source_target_pairs={{0,2},{2,0},{4,6},{6,4},{8,10},{10,8},{12,14},{14,12},{16,18},{18,... | collective-permute-start | bytes 1572872 | tf_op jit(solution)/shard_map/ppermute | solution.py:329
  96.0 8.0 %copy-start.8 = (f32[2,4,128,128]{3,2,1,0:T(8,128)}, f32[2,4,128,128]{3,2,1,0:T(8,128)S(1)}, u32[]{:S(2)}) copy-start(f32[2,4,128,128]{3,2,1,0:T(8,128)S(1)} %collective-permute-done.25.refs_27_) | copy-start | bytes 1572868
  96.0 3.0 %collective-permute-start.29 = (f32[2,4,128,128]{3,2,1,0:T(8,128)}, f32[2,4,128,128]{3,2,1,0:T(8,128)S(1)}, u32[]{:S(2)}, u32[]{:S(2)}) collective-permute-start(f32[2,4,128,128]{3,2,1,0:T(8,128)} %collective-permute-done.15.refs_15_), channel_id=1, source_target_pairs={{0,2},{2,0},{4,6},{6,4},{8,10},{10,8},{12,14},{14,12},{16,18},{18,... | collective-permute-start | bytes 1572872 | tf_op jit(solution)/shard_map/ppermute | solution.py:329
  96.5 7.5 %copy-start.9 = (f32[2,4,128,128]{3,2,1,0:T(8,128)}, f32[2,4,128,128]{3,2,1,0:T(8,128)S(1)}, u32[]{:S(2)}) copy-start(f32[2,4,128,128]{3,2,1,0:T(8,128)S(1)} %collective-permute-done.26.refs_28_) | copy-start | bytes 1572868
  96.5 3.2 %collective-permute-start.16 = (f32[2,4,128,128]{3,2,1,0:T(8,128)}, f32[2,4,128,128]{3,2,1,0:T(8,128)S(1)}, u32[]{:S(2)}, u32[]{:S(2)}) collective-permute-start(f32[2,4,128,128]{3,2,1,0:T(8,128)} %collective-permute-done.1.token.refs_1_), channel_id=1, source_target_pairs={{0,2},{2,0},{4,6},{6,4},{8,10},{10,8},{12,14},{14,12},{16,18},{18,... | collective-permute-start | bytes 1572872 | tf_op jit(solution)/shard_map/ppermute | solution.py:329
  97.5 9.0 %copy-start.10 = (f32[2,4,128,128]{3,2,1,0:T(8,128)}, f32[2,4,128,128]{3,2,1,0:T(8,128)S(1)}, u32[]{:S(2)}) copy-start(f32[2,4,128,128]{3,2,1,0:T(8,128)S(1)} %collective-permute-done.27.refs_29_) | copy-start | bytes 1572868
  97.5 3.0 %collective-permute-start.17 = (f32[2,4,128,128]{3,2,1,0:T(8,128)}, f32[2,4,128,128]{3,2,1,0:T(8,128)S(1)}, u32[]{:S(2)}, u32[]{:S(2)}) collective-permute-start(f32[2,4,128,128]{3,2,1,0:T(8,128)} %collective-permute-done.4.token.refs_2_), channel_id=1, source_target_pairs={{0,2},{2,0},{4,6},{6,4},{8,10},{10,8},{12,14},{14,12},{16,18},{18,... | collective-permute-start | bytes 1572872 | tf_op jit(solution)/shard_map/ppermute | solution.py:329
  98.2 5.8 %copy-start.11 = (f32[2,4,128,128]{3,2,1,0:T(8,128)}, f32[2,4,128,128]{3,2,1,0:T(8,128)S(1)}, u32[]{:S(2)}) copy-start(f32[2,4,128,128]{3,2,1,0:T(8,128)S(1)} %collective-permute-done.28.refs_30_) | copy-start | bytes 1572868
  98.2 3.7 %collective-permute-start.18 = (f32[2,4,128,128]{3,2,1,0:T(8,128)}, f32[2,4,128,128]{3,2,1,0:T(8,128)S(1)}, u32[]{:S(2)}, u32[]{:S(2)}) collective-permute-start(f32[2,4,128,128]{3,2,1,0:T(8,128)} %collective-permute-done.6.refs_3_), channel_id=1, source_target_pairs={{0,2},{2,0},{4,6},{6,4},{8,10},{10,8},{12,14},{14,12},{16,18},{18,... | collective-permute-start | bytes 1572872 | tf_op jit(solution)/shard_map/ppermute | solution.py:329
  99.0 5.1 %copy-start.12 = (f32[2,4,128,128]{3,2,1,0:T(8,128)}, f32[2,4,128,128]{3,2,1,0:T(8,128)S(1)}, u32[]{:S(2)}) copy-start(f32[2,4,128,128]{3,2,1,0:T(8,128)S(1)} %collective-permute-done.29.refs_31_) | copy-start | bytes 1572868
  99.0 3.1 %collective-permute-start.19 = (f32[2,4,128,128]{3,2,1,0:T(8,128)S(1)}, f32[2,4,128,128]{3,2,1,0:T(8,128)S(1)}, u32[]{:S(2)}, u32[]{:S(2)}) collective-permute-start(f32[2,4,128,128]{3,2,1,0:T(8,128)S(1)} %collective-permute-done.3.refs_4_), channel_id=1, source_target_pairs={{0,2},{2,0},{4,6},{6,4},{8,10},{10,8},{12,14},{14,12},{16,18},{18,... | collective-permute-start | bytes 1572872 | tf_op jit(solution)/shard_map/ppermute | solution.py:329
  99.7 6.7 %copy-start.13 = (f32[2,4,128,128]{3,2,1,0:T(8,128)}, f32[2,4,128,128]{3,2,1,0:T(8,128)S(1)}, u32[]{:S(2)}) copy-start(f32[2,4,128,128]{3,2,1,0:T(8,128)S(1)} %collective-permute-done.16.refs_17_) | copy-start | bytes 1572868
  99.7 3.0 %collective-permute-start.20 = (f32[2,4,128,128]{3,2,1,0:T(8,128)}, f32[2,4,128,128]{3,2,1,0:T(8,128)S(1)}, u32[]{:S(2)}, u32[]{:S(2)}) collective-permute-start(f32[2,4,128,128]{3,2,1,0:T(8,128)} %collective-permute-done.5.refs_5_), channel_id=1, source_target_pairs={{0,2},{2,0},{4,6},{6,4},{8,10},{10,8},{12,14},{14,12},{16,18},{18,... | collective-permute-start | bytes 1572872 | tf_op jit(solution)/shard_map/ppermute | solution.py:329
  100.5 3.6 %copy-start.14 = (f32[2,4,128,128]{3,2,1,0:T(8,128)}, f32[2,4,128,128]{3,2,1,0:T(8,128)S(1)}, u32[]{:S(2)}) copy-start(f32[2,4,128,128]{3,2,1,0:T(8,128)S(1)} %collective-permute-done.17.refs_18_) | copy-start | bytes 1572868
  100.5 3.0 %collective-permute-start.21 = (f32[2,4,128,128]{3,2,1,0:T(8,128)}, f32[2,4,128,128]{3,2,1,0:T(8,128)S(1)}, u32[]{:S(2)}, u32[]{:S(2)}) collective-permute-start(f32[2,4,128,128]{3,2,1,0:T(8,128)} %collective-permute-done.7.refs_6_), channel_id=1, source_target_pairs={{0,2},{2,0},{4,6},{6,4},{8,10},{10,8},{12,14},{14,12},{16,18},{18,... | collective-permute-start | bytes 1572872 | tf_op jit(solution)/shard_map/ppermute | solution.py:329
  102.0 2.1 %copy-start.15 = (f32[2,4,128,128]{3,2,1,0:T(8,128)}, f32[2,4,128,128]{3,2,1,0:T(8,128)S(1)}, u32[]{:S(2)}) copy-start(f32[2,4,128,128]{3,2,1,0:T(8,128)S(1)} %collective-permute-done.18.refs_19_) | copy-start | bytes 1572868
  102.0 2.0 %collective-permute-start.22 = (f32[2,4,128,128]{3,2,1,0:T(8,128)S(1)}, f32[2,4,128,128]{3,2,1,0:T(8,128)S(1)}, u32[]{:S(2)}, u32[]{:S(2)}) collective-permute-start(f32[2,4,128,128]{3,2,1,0:T(8,128)S(1)} %collective-permute-done.8.refs_7_), channel_id=1, source_target_pairs={{0,2},{2,0},{4,6},{6,4},{8,10},{10,8},{12,14},{14,12},{16,18},{18,... | collective-permute-start | bytes 1572872 | tf_op jit(solution)/shard_map/ppermute | solution.py:329
  102.1 2.0 %copy-start.16 = (f32[2,4,128,128]{3,2,1,0:T(8,128)}, f32[2,4,128,128]{3,2,1,0:T(8,128)S(1)}, u32[]{:S(2)}) copy-start(f32[2,4,128,128]{3,2,1,0:T(8,128)S(1)} %collective-permute-done.19.refs_20_) | copy-start | bytes 1572868
  102.7 1.4 copy-start.17
  103.5 0.8 copy-start.18
  104.3 0.8 copy-start.19
  123.2 2.2 %collective-permute-start.30 = (f32[8,128,128]{2,1,0:T(8,128)}, f32[8,128,128]{2,1,0:T(8,128)S(1)}, u32[]{:S(2)}, u32[]{:S(2)}) collective-permute-start(f32[8,128,128]{2,1,0:T(8,128)} %get-tuple-element.80), channel_id=1, source_target_pairs={{0,2},{2,0},{4,6},{6,4},{8,10},{10,8},{12,14},{14,12},{16,18},{18,... | collective-permute-start | bytes 1572872 | tf_op jit(solution)/shard_map/ppermute | solution.py:329
  126.4 9.7 %collective-permute-start.31 = (f32[4,128,128]{2,1,0:T(8,128)S(1)}, f32[4,128,128]{2,1,0:T(8,128)S(1)}, u32[]{:S(2)}, u32[]{:S(2)}) collective-permute-start(f32[4,128,128]{2,1,0:T(8,128)S(1)} %slice_add_fusion), channel_id=1, source_target_pairs={{0,4},{2,6},{4,0},{6,2},{8,12},{10,14},{12,8},{14,10},{16,20},{18,... | collective-permute-start | bytes 786440 | tf_op jit(solution)/shard_map/ppermute | solution.py:375
  137.1 6.6 %collective-permute-start.32 = (f32[1,128,128]{2,1,0:T(8,128)S(1)}, f32[1,128,128]{2,1,0:T(8,128)S(1)}, u32[]{:S(2)}, u32[]{:S(2)}) collective-permute-start(f32[1,128,128]{2,1,0:T(8,128)S(1)} %get-tuple-element.82), channel_id=1, source_target_pairs={{0,8},{2,10},{4,12},{6,14},{8,16},{10,18},{12,20},{14,22},{16,24},... | collective-permute-start | bytes 196616 | tf_op jit(solution)/shard_map/ppermute | solution.py:379
  138.5 5.2 %collective-permute-start.34 = (f32[1,128,128]{2,1,0:T(8,128)S(1)}, f32[1,128,128]{2,1,0:T(8,128)S(1)}, u32[]{:S(2)}, u32[]{:S(2)}) collective-permute-start(f32[1,128,128]{2,1,0:T(8,128)S(1)} %get-tuple-element.83), channel_id=1, source_target_pairs={{0,24},{2,26},{4,28},{6,30},{8,0},{10,2},{12,4},{14,6},{16,8},{18,... | collective-permute-start | bytes 196616 | tf_op jit(solution)/shard_map/ppermute | solution.py:379
  141.0 6.0 %collective-permute-start.33 = (f32[1,128,128]{2,1,0:T(8,128)S(1)}, f32[1,128,128]{2,1,0:T(8,128)S(1)}, u32[]{:S(2)}, u32[]{:S(2)}) collective-permute-start(f32[1,128,128]{2,1,0:T(8,128)S(1)} %get-tuple-element.84), channel_id=1, source_target_pairs={{0,16},{2,18},{4,20},{6,22},{8,24},{10,26},{12,28},{14,30},{16,0},... | collective-permute-start | bytes 196616 | tf_op jit(solution)/shard_map/ppermute | solution.py:379

commit v2 on v1

--- a/solution.py
+++ b/solution.py
@@ -184,31 +184,58 @@
         ]
         for a in range(sets)
     ]
-    for copies in [u_loads[0], sigma_loads] + u_loads[1:]:
+    first_loads = [
+        [
+            pltpu.make_async_copy(arrays[h].at[s, t], u_buf.at[0, s * hops + h, t], sems.at[6 + sets + t])
+            for h in range(hops)
+            for s in range(2)
+        ]
+        for t in range(per_set)
+    ]
+    for copies in [sigma_loads] + first_loads + u_loads[1:]:
         for copy in copies:
             copy.start()
-    p_buf[...] = jnp.zeros_like(p_buf)
 
     def slot_of(kk, i):
         return tables[plan.slot + kk * rows + i]
 
     def products(kk, a, t, chosen):
-        spots = [p_buf.shape[0] // 2 * (a // 2) + zs, p_buf.shape[0] // 2 * (a // 2)]
-        chip = chip_of[0]
-        at = (a % 2) * per_set + t
-        for index in range(1, len(chip_of)):
-            chip = jnp.where(at == index, chip_of[index], chip)
-        spot = jnp.where(lax.rem(chip, 2) == my_x, spots[1], spots[0]) + lax.rem(lax.div(chip, 2) - my_z + zs, zs)
-        y = jnp.zeros((len(chosen) * width, 2 * width), F32)
-        for j in range(pieces):
-            place = tables[plan.place + kk * pieces + j]
-            left = jnp.concatenate([buf[i, place] for i in chosen], axis=0)
-            y = y + dot(wide(left), tall(u_buf[a, j, t]))
-        y = fold(y)
+        size = len(chosen) * width
+        y = jnp.zeros((2 * size, 2 * width), F32)
+        for j in range(0, pieces, 2):
+            lefts, rights = [], []
+            for slot in (j, j + 1):
+                place = tables[plan.place + kk * pieces + slot]
+                left = jnp.concatenate([buf[i, place] for i in chosen], axis=0)
+                lefts.append(jnp.concatenate(split(left), axis=0))
+                rights.append(wide(u_buf[a, slot, t]))
+            y = y + dot(jnp.concatenate(lefts, axis=1), jnp.concatenate(rights, axis=0))
+        y = fold(y[:size] + y[size:])
         for k, i in enumerate(chosen):
-            part = y[k * width : (k + 1) * width]
-            z_buf[kk, i] = -part
-            p_buf[spot] += dot_t(u_buf[a, slot_of(kk, i), t], part)
+            z_buf[kk, i] = -y[k * width : (k + 1) * width]
+
+    def diagonals(a):
+        for t in range(per_set):
+            kk = a * per_set + t
+            own = len(chip_of)
+            chip = jnp.int32(chip_of[0])
+            for index in range(1, own):
+                chip = jnp.where(lax.rem(kk, own) == index, chip_of[index], chip)
+            spot = jnp.where(kk >= own, 2 * zs, 0) + jnp.where(lax.rem(chip, 2) == my_x, 0, zs)
+            spot = spot + lax.rem(lax.div(chip, 2) - my_z + zs, zs)
+            ups, downs = [], []
+            for i in range(rows):
+                slot = jnp.maximum(slot_of(kk, i), 0)
+                ups.append(jnp.concatenate(split(u_buf[a, slot, t]), axis=0))
+                downs.append(tall(z_buf[kk, i]))
+            p_buf[spot] = -fold(
+                lax.dot_general(
+                    jnp.concatenate(ups, axis=0),
+                    jnp.concatenate(downs, axis=0),
+                    (((0,), (0,)), ((), ())),
+                    preferred_element_type=F32,
+                )
+            )
 
     def node(kk, a, t):
         count = jnp.int32(0)
@@ -239,26 +266,50 @@
         def several():
             products(kk, a, t, list(range(rows)))
 
+    for copy in sigma_loads:
+        copy.wait()
+
+    def step(kk, carry):
+        a, t = lax.div(kk, per_set), lax.rem(kk, per_set)
+
+        @pl.when(a == 0)
+        def arrive():
+            def one(s, carry):
+                pltpu.make_async_copy(arrays[0].at[0, 0], u_buf.at[0, s, t], sems.at[6 + sets + t]).wait()
+                return carry
+
+            lax.fori_loop(0, pieces, one, 0)
+
+        for index in range(1, sets):
+
+            @pl.when(kk == index * per_set)
+            def arrive_set():
+                for copy in u_loads[index]:
+                    copy.wait()
+
+        node(kk, a, t)
+
+        @pl.when(t == per_set - 1)
+        def close_set():
+            diagonals(a)
+
+        pltpu.make_async_copy(z_buf.at[kk], z_out.at[tables[plan.node + kk]], sems.at[2 + sets]).start()
+        return carry
+
+    lax.fori_loop(0, sets * per_set, step, 0)
     stores = []
-    for a in range(sets):
-        for copy in u_loads[a] + (sigma_loads if a == 0 else []):
-            copy.wait()
-
-        def step(t, carry):
-            node(a * per_set + t, a, t)
-            return carry
-
-        lax.fori_loop(0, per_set, step, 0)
-        for t in range(per_set):
-            kk = a * per_set + t
-            stores.append(pltpu.make_async_copy(z_buf.at[kk], z_out.at[tables[plan.node + kk]], sems.at[2 + sets]))
-            stores[-1].start()
     for k, p_out in enumerate(p_outs):
         size = zs if k < 2 else 2 * zs
         stores.append(pltpu.make_async_copy(p_buf.at[pl.ds(k * zs, size)], p_out, sems.at[3 + sets + k]))
         stores[-1].start()
     for copy in stores:
         copy.wait()
+
+    def leave(kk, carry):
+        pltpu.make_async_copy(z_buf.at[0], z_out.at[0], sems.at[2 + sets]).wait()
+        return carry
+
+    lax.fori_loop(0, sets * per_set, leave, 0)
 
 
 def all_sums(plan, where, tables, near, far, u_sets, chip_of, zs):
@@ -281,7 +332,7 @@
             pltpu.VMEM((rows, cols + far.shape[1], width, width), F32),
             pltpu.VMEM((nodes, rows, width, width), F32),
             pltpu.VMEM((4 * zs, width, width), F32),
-            pltpu.SemaphoreType.DMA((6 + sets,)),
+            pltpu.SemaphoreType.DMA((6 + sets + per_set,)),
         ],
         compiler_params=pltpu.CompilerParams(vmem_limit_bytes=VMEM_LIMIT),
         cost_estimate=cost(COSTS["sums"]),
@@ -372,11 +423,13 @@
     z_off, mine, across, theirs = all_sums(plan, where, tables, sigma, far, gathered, chip_of, zs)
 
     got = swapped(theirs)
-    part_sum = (mine + got[:zs]) + permute(across + got[zs:], "row", swap_x)
-    z_diag = square + part_sum[:1]
-    for m in range(1, zs):
-        links = [(r, (r + 4 * m) % n_row) for r in range(n_row)]
-        z_diag = z_diag + permute(part_sum[m : m + 1], "row", links)
+    here, there = mine + got[:zs], across + got[zs:]
+    z_diag = square + here[:1]
+    routes = [(m, flip) for flip in (1, 0) for m in range(zs) if m + flip > 0]
+    for m, flip in routes:
+        links = [(r, ((r + 4 * m) % n_row) ^ (2 * flip)) for r in range(n_row)]
+        source = there if flip else here
+        z_diag = z_diag + permute(source[m : m + 1], "row", links)
     return z_off, z_diag
 
 

time: 149 us -> 145 us (0.973)
  waiting for transfers between devices: 80.5 us -> 74 us
  starting transfers between devices: 27 us -> 31.1 us
    ppermute x4 -> x7, waiting for transfers between devices: 11.9 us -> 5.43 us  [body(): z_diag = z_diag + permute(source[m:m + 1], 'row', links)]
    ppermute x4 -> x7, starting transfers between devices: 7.71 us -> 11.8 us  [body(): z_diag = z_diag + permute(source[m:m + 1], 'row', links)]
  transfers between devices with their start and end apart: 35 -> 38, of which waited for: 32 -> 33; matrix products, arithmetic and copies ran while one was open for 0% -> 0% of each run, Pallas kernels for 12% -> 12%
where the time goes in v2:
time: 145 us; the launch traced here: 144 us
  waiting for transfers between devices  74 us (51%)
  Pallas kernels  34 us (23%)
  starting transfers between devices  31.1 us (21%)
  other arithmetic  2.38 us (2%)
  local copies, waits for them, and re-layouts  2.04 us (1%)
    ppermute x14, waiting for transfers between devices, body(): permute(front[0 if way > 0 else 1], 'row', pairs(way))  56.8 us
    pallas_call x1, Pallas kernels, all_sums(): pl.pallas_call(functools.partial(sums_kernel, (rows, zs, chip_of, sets, h...  16.6 us
    ppermute x14, starting transfers between devices, body(): permute(front[0 if way > 0 else 1], 'row', pairs(way))  14 us
    pallas_call x4, Pallas kernels, u_blocks(): pl.pallas_call(functools.partial(u_kernel, chips, other), out_shape=[jax....  13.3 us
    ppermute x7, starting transfers between devices, body(): z_diag = z_diag + permute(source[m:m + 1], 'row', links)  11.8 us
    ppermute x16, waiting for transfers between devices, swapped(): return permute(array, 'row', swap_core)  10.4 us
    ppermute x7, waiting for transfers between devices, body(): z_diag = z_diag + permute(source[m:m + 1], 'row', links)  5.43 us
    pallas_call x1, Pallas kernels, make_plan(): pl.pallas_call(functools.partial(plan_kernel, dims, plan), out_shape=jax....  4.07 us
  transfers between devices with their start and end apart: 38, of which 33 were waited for; matrix products, arithmetic and copies ran while one was open for 0% of the time, Pallas kernels for 12%

profile of v2, /device:TPU:0, one launch (start us, length us, event | category | flops | bytes accessed | tf_op | source)
XLA Modules:
  0.0 144.4 jit_solution(5480023456326608017)
XLA Ops:
  0.6 0.5 collective-permute-start
  1.1 2.6 %collective-permute-start.2 = (f32[3,24,128,128]{3,2,1,0:T(8,128)}, f32[3,24,128,128]{3,2,1,0:T(8,128)}, u32[]{:S(2)}, u32[]{:S(2)}) collective-permute-start(f32[3,24,128,128]{3,2,1,0:T(8,128)} %near.1), channel_id=1, source_target_pairs={{1,0},{0,1},{3,2},{2,3},{5,4},{4,5},{7,6},{6,7},{9,8},{8,9},{11,10... | collective-permute-start | bytes 14155784 | tf_op jit(solution)/shard_map/ppermute | solution.py:386
  3.7 0.6 pad_add_fusion.where
  4.4 1.0 copy-done.21
  5.3 3.3 %u_blocks.7 = (f32[2,4,128,128]{3,2,1,0:T(8,128)}, f32[1,128,128]{2,1,0:T(8,128)}) custom-call(s32[2]{0:T(128)} %pad_add_fusion.where, f32[16,128,128]{2,1,0:T(8,128)} %bitcast.4, f32[16,128,128]{2,1,0:T(8,128)} %copy-done.21, f32[16,128,128]{2,1,0:T(8,128)} %inverse.7, s32[16,16]{1,0:T(8,128)} %token_.3), custom_call_target="tpu_custom_call" | custom-call | flops 1000000000 | bytes 1000 | tf_op jit(solution)/shard_map/u_blocks/pallas_call | solution.py:147
  8.7 2.3 %collective-permute-start.9 = (f32[2,4,128,128]{3,2,1,0:T(8,128)}, f32[2,4,128,128]{3,2,1,0:T(8,128)S(1)}, u32[]{:S(2)}, u32[]{:S(2)}) collective-permute-start(f32[2,4,128,128]{3,2,1,0:T(8,128)} %get-tuple-element.57.refs_8_), channel_id=1, source_target_pairs={{0,8},{2,10},{8,16},{10,18},{16,24},{18,26},{24,28},{26,30},{28,20... | collective-permute-start | bytes 1572872 | tf_op jit(solution)/shard_map/ppermute | solution.py:407
  10.9 3.3 %u_blocks.4 = (f32[2,4,128,128]{3,2,1,0:T(8,128)}, f32[1,128,128]{2,1,0:T(8,128)}) custom-call(s32[2]{0:T(128)} %pad_add_fusion.where, f32[16,128,128]{2,1,0:T(8,128)} %bitcast.5, f32[16,128,128]{2,1,0:T(8,128)} %copy-done.21, f32[16,128,128]{2,1,0:T(8,128)} %inverse.7, s32[16,16]{1,0:T(8,128)} %token_.3), custom_call_target="tpu_custom_call" | custom-call | flops 1000000000 | bytes 1000 | tf_op jit(solution)/shard_map/u_blocks/pallas_call | solution.py:147
  14.3 2.1 %collective-permute-start.1 = (f32[2,4,128,128]{3,2,1,0:T(8,128)}, f32[2,4,128,128]{3,2,1,0:T(8,128)}, u32[]{:S(2)}, u32[]{:S(2)}) collective-permute-start(f32[2,4,128,128]{3,2,1,0:T(8,128)} %get-tuple-element.44.refs_0_), channel_id=1, source_target_pairs={{0,8},{2,10},{8,16},{10,18},{16,24},{18,26},{24,28},{26,30},{28,20... | collective-permute-start | bytes 1572872 | tf_op jit(solution)/shard_map/ppermute | solution.py:407
  16.4 7.4 %collective-permute-done.9.refs_9_ = f32[2,4,128,128]{3,2,1,0:T(8,128)S(1)} collective-permute-done((f32[2,4,128,128]{3,2,1,0:T(8,128)}, f32[2,4,128,128]{3,2,1,0:T(8,128)S(1)}, u32[]{:S(2)}, u32[]{:S(2)}) %collective-permute-start.9) | collective-permute-done | bytes 524320 | tf_op jit(solution)/shard_map/ppermute | solution.py:407
  23.8 2.2 %collective-permute-done.10.refs_12_ = f32[2,4,128,128]{3,2,1,0:T(8,128)S(1)} collective-permute-done((f32[2,4,128,128]{3,2,1,0:T(8,128)}, f32[2,4,128,128]{3,2,1,0:T(8,128)S(1)}, u32[]{:S(2)}, u32[]{:S(2)}) %collective-permute-start.10) | collective-permute-done | bytes 524320 | tf_op jit(solution)/shard_map/ppermute | solution.py:407
  26.0 1.6 %collective-permute-start.11 = (f32[2,4,128,128]{3,2,1,0:T(8,128)S(1)}, f32[2,4,128,128]{3,2,1,0:T(8,128)S(1)}, u32[]{:S(2)}, u32[]{:S(2)}) collective-permute-start(f32[2,4,128,128]{3,2,1,0:T(8,128)S(1)} %collective-permute-done.9.refs_9_), channel_id=1, source_target_pairs={{0,8},{2,10},{8,16},{10,18},{16,24},{18,26},{24,28},{26,30},{28,20... | collective-permute-start | bytes 1572872 | tf_op jit(solution)/shard_map/ppermute | solution.py:407
  27.5 0.5 collective-permute-start.12
  28.0 7.1 %collective-permute-done.1.token.refs_1_ = f32[2,4,128,128]{3,2,1,0:T(8,128)} collective-permute-done((f32[2,4,128,128]{3,2,1,0:T(8,128)}, f32[2,4,128,128]{3,2,1,0:T(8,128)}, u32[]{:S(2)}, u32[]{:S(2)}) %collective-permute-start.1) | collective-permute-done | bytes 524320 | tf_op jit(solution)/shard_map/ppermute | solution.py:407
  35.1 2.1 %collective-permute-done.3.refs_4_ = f32[2,4,128,128]{3,2,1,0:T(8,128)S(1)} collective-permute-done((f32[2,4,128,128]{3,2,1,0:T(8,128)}, f32[2,4,128,128]{3,2,1,0:T(8,128)S(1)}, u32[]{:S(2)}, u32[]{:S(2)}) %collective-permute-start.3) | collective-permute-done | bytes 524320 | tf_op jit(solution)/shard_map/ppermute | solution.py:407
  37.2 1.6 %collective-permute-start.4 = (f32[2,4,128,128]{3,2,1,0:T(8,128)}, f32[2,4,128,128]{3,2,1,0:T(8,128)}, u32[]{:S(2)}, u32[]{:S(2)}) collective-permute-start(f32[2,4,128,128]{3,2,1,0:T(8,128)} %collective-permute-done.1.token.refs_1_), channel_id=1, source_target_pairs={{0,8},{2,10},{8,16},{10,18},{16,24},{18,26},{24,28},{26,30},{28,20... | collective-permute-start | bytes 1572872 | tf_op jit(solution)/shard_map/ppermute | solution.py:407
  38.8 0.5 collective-permute-start.5
  39.2 7.0 %collective-permute-done.11.refs_10_ = f32[2,4,128,128]{3,2,1,0:T(8,128)S(1)} collective-permute-done((f32[2,4,128,128]{3,2,1,0:T(8,128)S(1)}, f32[2,4,128,128]{3,2,1,0:T(8,128)S(1)}, u32[]{:S(2)}, u32[]{:S(2)}) %collective-permute-start.11) | collective-permute-done | bytes 524320 | tf_op jit(solution)/shard_map/ppermute | solution.py:407
  46.2 2.2 %collective-permute-done.12.refs_13_ = f32[2,4,128,128]{3,2,1,0:T(8,128)S(1)} collective-permute-done((f32[2,4,128,128]{3,2,1,0:T(8,128)S(1)}, f32[2,4,128,128]{3,2,1,0:T(8,128)S(1)}, u32[]{:S(2)}, u32[]{:S(2)}) %collective-permute-start.12) | collective-permute-done | bytes 524320 | tf_op jit(solution)/shard_map/ppermute | solution.py:407
  48.4 1.6 %collective-permute-start.13 = (f32[2,4,128,128]{3,2,1,0:T(8,128)S(1)}, f32[2,4,128,128]{3,2,1,0:T(8,128)}, u32[]{:S(2)}, u32[]{:S(2)}) collective-permute-start(f32[2,4,128,128]{3,2,1,0:T(8,128)S(1)} %collective-permute-done.11.refs_10_), channel_id=1, source_target_pairs={{0,8},{2,10},{8,16},{10,18},{16,24},{18,26},{24,28},{26,30},{28,20... | collective-permute-start | bytes 1572872 | tf_op jit(solution)/shard_map/ppermute | solution.py:407
  50.0 0.5 collective-permute-start.14
  50.5 4.1 %plan.1.tables = s32[321]{0:T(512)} custom-call(s32[2]{0:T(128)} %pad_add_fusion.where, s32[256]{0:T(256)} %constant.12.clone.table, s32[8]{0:T(128)} %constant.13.clone.chip_of, s32[16,16]{1,0:T(8,128)} %token_.3, f32[2,4,128,128]{3,2,1,0:T(8,128)} %collective-permute-done.1.token.refs_1_), custom_call_target="tpu_custom_call" | custom-call | flops 1000000000 | bytes 1000 | tf_op jit(solution)/shard_map/plan/pallas_call | solution.py:98
  54.5 3.0 %collective-permute-done.4.token.refs_2_ = f32[2,4,128,128]{3,2,1,0:T(8,128)} collective-permute-done((f32[2,4,128,128]{3,2,1,0:T(8,128)}, f32[2,4,128,128]{3,2,1,0:T(8,128)}, u32[]{:S(2)}, u32[]{:S(2)}) %collective-permute-start.4) | collective-permute-done | bytes 524320 | tf_op jit(solution)/shard_map/ppermute | solution.py:407
  57.6 2.2 %collective-permute-done.5.refs_5_ = f32[2,4,128,128]{3,2,1,0:T(8,128)} collective-permute-done((f32[2,4,128,128]{3,2,1,0:T(8,128)S(1)}, f32[2,4,128,128]{3,2,1,0:T(8,128)}, u32[]{:S(2)}, u32[]{:S(2)}) %collective-permute-start.5) | collective-permute-done | bytes 524320 | tf_op jit(solution)/shard_map/ppermute | solution.py:407
  59.8 1.6 %collective-permute-start.6 = (f32[2,4,128,128]{3,2,1,0:T(8,128)}, f32[2,4,128,128]{3,2,1,0:T(8,128)}, u32[]{:S(2)}, u32[]{:S(2)}) collective-permute-start(f32[2,4,128,128]{3,2,1,0:T(8,128)} %collective-permute-done.4.token.refs_2_), channel_id=1, source_target_pairs={{0,8},{2,10},{8,16},{10,18},{16,24},{18,26},{24,28},{26,30},{28,20... | collective-permute-start | bytes 1572872 | tf_op jit(solution)/shard_map/ppermute | solution.py:407
  61.4 0.5 collective-permute-start.7
  61.8 7.0 %collective-permute-done.13.refs_11_ = f32[2,4,128,128]{3,2,1,0:T(8,128)} collective-permute-done((f32[2,4,128,128]{3,2,1,0:T(8,128)S(1)}, f32[2,4,128,128]{3,2,1,0:T(8,128)}, u32[]{:S(2)}, u32[]{:S(2)}) %collective-permute-start.13) | collective-permute-done | bytes 524320 | tf_op jit(solution)/shard_map/ppermute | solution.py:407
  68.8 2.2 %collective-permute-done.14.refs_14_ = f32[2,4,128,128]{3,2,1,0:T(8,128)} collective-permute-done((f32[2,4,128,128]{3,2,1,0:T(8,128)S(1)}, f32[2,4,128,128]{3,2,1,0:T(8,128)}, u32[]{:S(2)}, u32[]{:S(2)}) %collective-permute-start.14) | collective-permute-done | bytes 524320 | tf_op jit(solution)/shard_map/ppermute | solution.py:407
  71.0 3.3 %u_blocks.6 = (f32[2,4,128,128]{3,2,1,0:T(8,128)}, f32[1,128,128]{2,1,0:T(8,128)}) custom-call(s32[2]{0:T(128)} %pad_add_fusion.where, f32[16,128,128]{2,1,0:T(8,128)} %bitcast.6, f32[16,128,128]{2,1,0:T(8,128)} %copy-done.21, f32[16,128,128]{2,1,0:T(8,128)} %inverse.7, f32[2,4,128,128]{3,2,1,0:T(8,128)} %collective-permute-done.4.token.refs_2_), custom_call_target="tpu_custom_call" | custom-call | flops 1000000000 | bytes 1000 | tf_op jit(solution)/shard_map/u_blocks/pallas_call | solution.py:147
  74.4 3.3 %u_blocks.5 = (f32[2,4,128,128]{3,2,1,0:T(8,128)}, f32[1,128,128]{2,1,0:T(8,128)}) custom-call(s32[2]{0:T(128)} %pad_add_fusion.where, f32[16,128,128]{2,1,0:T(8,128)} %bitcast.7, f32[16,128,128]{2,1,0:T(8,128)} %copy-done.21, f32[16,128,128]{2,1,0:T(8,128)} %inverse.7, f32[2,4,128,128]{3,2,1,0:T(8,128)} %collective-permute-done.4.token.refs_2_), custom_call_target="tpu_custom_call" | custom-call | flops 1000000000 | bytes 1000 | tf_op jit(solution)/shard_map/u_blocks/pallas_call | solution.py:147
  77.7 1.9 %collective-permute-done.6.refs_3_ = f32[2,4,128,128]{3,2,1,0:T(8,128)} collective-permute-done((f32[2,4,128,128]{3,2,1,0:T(8,128)}, f32[2,4,128,128]{3,2,1,0:T(8,128)}, u32[]{:S(2)}, u32[]{:S(2)}) %collective-permute-start.6) | collective-permute-done | bytes 524320 | tf_op jit(solution)/shard_map/ppermute | solution.py:407
  79.6 2.7 %collective-permute-done.7.refs_6_ = f32[2,4,128,128]{3,2,1,0:T(8,128)} collective-permute-done((f32[2,4,128,128]{3,2,1,0:T(8,128)}, f32[2,4,128,128]{3,2,1,0:T(8,128)}, u32[]{:S(2)}, u32[]{:S(2)}) %collective-permute-start.7) | collective-permute-done | bytes 524320 | tf_op jit(solution)/shard_map/ppermute | solution.py:407
  82.3 1.6 %collective-permute-start.8 = (f32[2,4,128,128]{3,2,1,0:T(8,128)}, f32[2,4,128,128]{3,2,1,0:T(8,128)S(1)}, u32[]{:S(2)}, u32[]{:S(2)}) collective-permute-start(f32[2,4,128,128]{3,2,1,0:T(8,128)} %collective-permute-done.6.refs_3_), channel_id=1, source_target_pairs={{0,8},{2,10},{8,16},{10,18},{16,24},{18,26},{24,28},{26,30},{28,20... | collective-permute-start | bytes 1572872 | tf_op jit(solution)/shard_map/ppermute | solution.py:407
  83.8 8.5 %collective-permute-done.15.refs_15_ = f32[2,4,128,128]{3,2,1,0:T(8,128)} collective-permute-done((f32[2,4,128,128]{3,2,1,0:T(8,128)}, f32[2,4,128,128]{3,2,1,0:T(8,128)}, u32[]{:S(2)}, u32[]{:S(2)}) %collective-permute-start.15) | collective-permute-done | bytes 524320 | tf_op jit(solution)/shard_map/ppermute | solution.py:407
  92.4 0.5 collective-permute-start.24
  92.9 1.3 collective-permute-done.8.refs_7_
  94.2 0.8 collective-permute-done.23.refs_25_
  95.0 0.1 collective-permute-start.27
  95.2 0.3 collective-permute-start.28
  95.5 0.5 collective-permute-done.25.refs_27_
  96.1 0.4 collective-permute-done.26.refs_28_
  96.7 0.8 collective-permute-done.27.refs_29_
  97.6 0.6 collective-permute-done.28.refs_30_
  98.4 0.6 collective-permute-done.29.refs_31_
  99.1 0.6 collective-permute-done.16.refs_17_
  99.9 0.6 collective-permute-done.17.refs_18_
  100.6 1.4 collective-permute-done.18.refs_19_
  102.1 0.6 collective-permute-done.20.refs_21_
  102.7 0.7 collective-permute-done.21.refs_22_
  103.5 0.5 collective-permute-done.22.refs_23_
  104.1 0.2 copy-done.18
  104.3 0.8 copy-done.19
  105.1 1.4 collective-permute-done.2.far
  106.5 16.6 %all_sums.1 = (f32[16,3,128,128]{3,2,1,0:T(8,128)}, f32[4,128,128]{2,1,0:T(8,128)}, f32[4,128,128]{2,1,0:T(8,128)}, f32[8,128,128]{2,1,0:T(8,128)}) custom-call(s32[2]{0:T(128)} %pad_add_fusion.where, s32[321]{0:T(512)} %plan.1.tables, f32[3,24,128,128]{3,2,1,0:T(8,128)} %near.1, f32[3,24,128,128]{3,2,1,0:T(8,128)} %collective-permute-done.2.far, ...), custom_call_target="tpu_custom_call" | custom-call | flops 3000000000 | bytes 1000 | tf_op jit(solution)/shard_map/all_sums/pallas_call | solution.py:325
  123.2 2.1 %collective-permute-done.30 = f32[8,128,128]{2,1,0:T(8,128)S(1)} collective-permute-done((f32[8,128,128]{2,1,0:T(8,128)}, f32[8,128,128]{2,1,0:T(8,128)S(1)}, u32[]{:S(2)}, u32[]{:S(2)}) %collective-permute-start.30) | collective-permute-done | bytes 524320 | tf_op jit(solution)/shard_map/ppermute | solution.py:380
  125.3 1.1 slice_add_fusion
  126.5 3.3 %collective-permute-start.34 = (f32[1,128,128]{2,1,0:T(8,128)S(1)}, f32[1,128,128]{2,1,0:T(8,128)S(1)}, u32[]{:S(2)}, u32[]{:S(2)}) collective-permute-start(f32[1,128,128]{2,1,0:T(8,128)S(1)} %get-tuple-element.85), channel_id=1, source_target_pairs={{0,28},{2,30},{4,24},{6,26},{8,4},{10,6},{12,0},{14,2},{16,12},{18... | collective-permute-start | bytes 196616 | tf_op jit(solution)/shard_map/ppermute | solution.py:432
  129.8 1.9 %collective-permute-start.33 = (f32[1,128,128]{2,1,0:T(8,128)S(1)}, f32[1,128,128]{2,1,0:T(8,128)S(1)}, u32[]{:S(2)}, u32[]{:S(2)}) collective-permute-start(f32[1,128,128]{2,1,0:T(8,128)S(1)} %get-tuple-element.86), channel_id=1, source_target_pairs={{0,20},{2,22},{4,16},{6,18},{8,28},{10,30},{12,24},{14,26},{16,4},... | collective-permute-start | bytes 196616 | tf_op jit(solution)/shard_map/ppermute | solution.py:432
  131.7 2.7 %collective-permute-start.32 = (f32[1,128,128]{2,1,0:T(8,128)S(1)}, f32[1,128,128]{2,1,0:T(8,128)S(1)}, u32[]{:S(2)}, u32[]{:S(2)}) collective-permute-start(f32[1,128,128]{2,1,0:T(8,128)S(1)} %get-tuple-element.87), channel_id=1, source_target_pairs={{0,12},{2,14},{4,8},{6,10},{8,20},{10,22},{12,16},{14,18},{16,28},... | collective-permute-start | bytes 196616 | tf_op jit(solution)/shard_map/ppermute | solution.py:432
  134.5 3.8 %collective-permute-start.37 = (f32[1,128,128]{2,1,0:T(8,128)S(1)}, f32[1,128,128]{2,1,0:T(8,128)S(1)}, u32[]{:S(2)}, u32[]{:S(2)}) collective-permute-start(f32[1,128,128]{2,1,0:T(8,128)S(1)} %get-tuple-element.89), channel_id=1, source_target_pairs={{0,24},{2,26},{4,28},{6,30},{8,0},{10,2},{12,4},{14,6},{16,8},{18,... | collective-permute-start | bytes 196616 | tf_op jit(solution)/shard_map/ppermute | solution.py:432
  138.3 0.9 collective-permute-done.33
  139.1 0.3 collective-permute-done.32
  139.4 2.0 %collective-permute-done.35 = f32[1,128,128]{2,1,0:T(8,128)S(1)} collective-permute-done((f32[1,128,128]{2,1,0:T(8,128)S(1)}, f32[1,128,128]{2,1,0:T(8,128)S(1)}, u32[]{:S(2)}, u32[]{:S(2)}) %collective-permute-start.35) | collective-permute-done | bytes 65568 | tf_op jit(solution)/shard_map/ppermute | solution.py:432
  141.4 2.3 %collective-permute-done.36 = f32[1,128,128]{2,1,0:T(8,128)S(1)} collective-permute-done((f32[1,128,128]{2,1,0:T(8,128)S(1)}, f32[1,128,128]{2,1,0:T(8,128)S(1)}, u32[]{:S(2)}, u32[]{:S(2)}) %collective-permute-start.36) | collective-permute-done | bytes 65568 | tf_op jit(solution)/shard_map/ppermute | solution.py:432
  143.7 0.7 fusion.6
  (67 shorter events, 1.6 us)
Async XLA Ops:
  0.6 3.7 %collective-permute-start = (f32[16,128,128]{2,1,0:T(8,128)}, f32[16,128,128]{2,1,0:T(8,128)S(1)}, u32[]{:S(2)}, u32[]{:S(2)}) collective-permute-start(f32[16,128,128]{2,1,0:T(8,128)} %bitcast.3), channel_id=1, source_target_pairs={{0,2},{2,0},{4,6},{6,4},{8,10},{10,8},{12,14},{14,12},{16,18},{18,... | collective-permute-start | bytes 3145736 | tf_op jit(solution)/shard_map/ppermute | solution.py:380
  1.1 105.3 %collective-permute-start.2 = (f32[3,24,128,128]{3,2,1,0:T(8,128)}, f32[3,24,128,128]{3,2,1,0:T(8,128)}, u32[]{:S(2)}, u32[]{:S(2)}) collective-permute-start(f32[3,24,128,128]{3,2,1,0:T(8,128)} %near.1), channel_id=1, source_target_pairs={{1,0},{0,1},{3,2},{2,3},{5,4},{4,5},{7,6},{6,7},{9,8},{8,9},{11,10... | collective-permute-start | bytes 14155784 | tf_op jit(solution)/shard_map/ppermute | solution.py:386
  4.4 1.0 copy-start.21
  8.7 15.1 %collective-permute-start.9 = (f32[2,4,128,128]{3,2,1,0:T(8,128)}, f32[2,4,128,128]{3,2,1,0:T(8,128)S(1)}, u32[]{:S(2)}, u32[]{:S(2)}) collective-permute-start(f32[2,4,128,128]{3,2,1,0:T(8,128)} %get-tuple-element.57.refs_8_), channel_id=1, source_target_pairs={{0,8},{2,10},{8,16},{10,18},{16,24},{18,26},{24,28},{26,30},{28,20... | collective-permute-start | bytes 1572872 | tf_op jit(solution)/shard_map/ppermute | solution.py:407
  10.9 15.0 %collective-permute-start.10 = (f32[2,4,128,128]{3,2,1,0:T(8,128)}, f32[2,4,128,128]{3,2,1,0:T(8,128)S(1)}, u32[]{:S(2)}, u32[]{:S(2)}) collective-permute-start(f32[2,4,128,128]{3,2,1,0:T(8,128)} %get-tuple-element.57.refs_8_), channel_id=1, source_target_pairs={{0,4},{2,6},{8,0},{10,2},{16,8},{18,10},{24,16},{26,18},{28,24},{3... | collective-permute-start | bytes 1572872 | tf_op jit(solution)/shard_map/ppermute | solution.py:407
  14.3 20.8 %collective-permute-start.1 = (f32[2,4,128,128]{3,2,1,0:T(8,128)}, f32[2,4,128,128]{3,2,1,0:T(8,128)}, u32[]{:S(2)}, u32[]{:S(2)}) collective-permute-start(f32[2,4,128,128]{3,2,1,0:T(8,128)} %get-tuple-element.44.refs_0_), channel_id=1, source_target_pairs={{0,8},{2,10},{8,16},{10,18},{16,24},{18,26},{24,28},{26,30},{28,20... | collective-permute-start | bytes 1572872 | tf_op jit(solution)/shard_map/ppermute | solution.py:407
  16.4 20.8 %collective-permute-start.3 = (f32[2,4,128,128]{3,2,1,0:T(8,128)}, f32[2,4,128,128]{3,2,1,0:T(8,128)S(1)}, u32[]{:S(2)}, u32[]{:S(2)}) collective-permute-start(f32[2,4,128,128]{3,2,1,0:T(8,128)} %get-tuple-element.44.refs_0_), channel_id=1, source_target_pairs={{0,4},{2,6},{8,0},{10,2},{16,8},{18,10},{24,16},{26,18},{28,24},{3... | collective-permute-start | bytes 1572872 | tf_op jit(solution)/shard_map/ppermute | solution.py:407
  23.8 68.6 %copy-start = (f32[2,4,128,128]{3,2,1,0:T(8,128)}, f32[2,4,128,128]{3,2,1,0:T(8,128)S(1)}, u32[]{:S(2)}) copy-start(f32[2,4,128,128]{3,2,1,0:T(8,128)S(1)} %collective-permute-done.9.refs_9_) | copy-start | bytes 1572868
  26.0 68.2 %copy-start.1 = (f32[2,4,128,128]{3,2,1,0:T(8,128)}, f32[2,4,128,128]{3,2,1,0:T(8,128)S(1)}, u32[]{:S(2)}) copy-start(f32[2,4,128,128]{3,2,1,0:T(8,128)S(1)} %collective-permute-done.10.refs_12_) | copy-start | bytes 1572868
  26.0 20.3 %collective-permute-start.11 = (f32[2,4,128,128]{3,2,1,0:T(8,128)S(1)}, f32[2,4,128,128]{3,2,1,0:T(8,128)S(1)}, u32[]{:S(2)}, u32[]{:S(2)}) collective-permute-start(f32[2,4,128,128]{3,2,1,0:T(8,128)S(1)} %collective-permute-done.9.refs_9_), channel_id=1, source_target_pairs={{0,8},{2,10},{8,16},{10,18},{16,24},{18,26},{24,28},{26,30},{28,20... | collective-permute-start | bytes 1572872 | tf_op jit(solution)/shard_map/ppermute | solution.py:407
  27.5 20.9 %collective-permute-start.12 = (f32[2,4,128,128]{3,2,1,0:T(8,128)S(1)}, f32[2,4,128,128]{3,2,1,0:T(8,128)S(1)}, u32[]{:S(2)}, u32[]{:S(2)}) collective-permute-start(f32[2,4,128,128]{3,2,1,0:T(8,128)S(1)} %collective-permute-done.10.refs_12_), channel_id=1, source_target_pairs={{0,4},{2,6},{8,0},{10,2},{16,8},{18,10},{24,16},{26,18},{28,24},{3... | collective-permute-start | bytes 1572872 | tf_op jit(solution)/shard_map/ppermute | solution.py:407
  37.2 61.8 %copy-start.2 = (f32[2,4,128,128]{3,2,1,0:T(8,128)}, f32[2,4,128,128]{3,2,1,0:T(8,128)S(1)}, u32[]{:S(2)}) copy-start(f32[2,4,128,128]{3,2,1,0:T(8,128)S(1)} %collective-permute-done.3.refs_4_) | copy-start | bytes 1572868
  37.2 20.4 %collective-permute-start.4 = (f32[2,4,128,128]{3,2,1,0:T(8,128)}, f32[2,4,128,128]{3,2,1,0:T(8,128)}, u32[]{:S(2)}, u32[]{:S(2)}) collective-permute-start(f32[2,4,128,128]{3,2,1,0:T(8,128)} %collective-permute-done.1.token.refs_1_), channel_id=1, source_target_pairs={{0,8},{2,10},{8,16},{10,18},{16,24},{18,26},{24,28},{26,30},{28,20... | collective-permute-start | bytes 1572872 | tf_op jit(solution)/shard_map/ppermute | solution.py:407
  38.8 21.0 %collective-permute-start.5 = (f32[2,4,128,128]{3,2,1,0:T(8,128)S(1)}, f32[2,4,128,128]{3,2,1,0:T(8,128)}, u32[]{:S(2)}, u32[]{:S(2)}) collective-permute-start(f32[2,4,128,128]{3,2,1,0:T(8,128)S(1)} %collective-permute-done.3.refs_4_), channel_id=1, source_target_pairs={{0,4},{2,6},{8,0},{10,2},{16,8},{18,10},{24,16},{26,18},{28,24},{3... | collective-permute-start | bytes 1572872 | tf_op jit(solution)/shard_map/ppermute | solution.py:407
  46.2 13.5 %copy-start.3 = (f32[2,4,128,128]{3,2,1,0:T(8,128)}, f32[2,4,128,128]{3,2,1,0:T(8,128)S(1)}, u32[]{:S(2)}) copy-start(f32[2,4,128,128]{3,2,1,0:T(8,128)S(1)} %collective-permute-done.11.refs_10_) | copy-start | bytes 1572868
  48.4 20.4 %copy-start.4 = (f32[2,4,128,128]{3,2,1,0:T(8,128)}, f32[2,4,128,128]{3,2,1,0:T(8,128)S(1)}, u32[]{:S(2)}) copy-start(f32[2,4,128,128]{3,2,1,0:T(8,128)S(1)} %collective-permute-done.12.refs_13_) | copy-start | bytes 1572868
  48.4 20.4 %collective-permute-start.13 = (f32[2,4,128,128]{3,2,1,0:T(8,128)S(1)}, f32[2,4,128,128]{3,2,1,0:T(8,128)}, u32[]{:S(2)}, u32[]{:S(2)}) collective-permute-start(f32[2,4,128,128]{3,2,1,0:T(8,128)S(1)} %collective-permute-done.11.refs_10_), channel_id=1, source_target_pairs={{0,8},{2,10},{8,16},{10,18},{16,24},{18,26},{24,28},{26,30},{28,20... | collective-permute-start | bytes 1572872 | tf_op jit(solution)/shard_map/ppermute | solution.py:407
  50.0 21.0 %collective-permute-start.14 = (f32[2,4,128,128]{3,2,1,0:T(8,128)S(1)}, f32[2,4,128,128]{3,2,1,0:T(8,128)}, u32[]{:S(2)}, u32[]{:S(2)}) collective-permute-start(f32[2,4,128,128]{3,2,1,0:T(8,128)S(1)} %collective-permute-done.12.refs_13_), channel_id=1, source_target_pairs={{0,4},{2,6},{8,0},{10,2},{16,8},{18,10},{24,16},{26,18},{28,24},{3... | collective-permute-start | bytes 1572872 | tf_op jit(solution)/shard_map/ppermute | solution.py:407
  59.8 19.8 %collective-permute-start.6 = (f32[2,4,128,128]{3,2,1,0:T(8,128)}, f32[2,4,128,128]{3,2,1,0:T(8,128)}, u32[]{:S(2)}, u32[]{:S(2)}) collective-permute-start(f32[2,4,128,128]{3,2,1,0:T(8,128)} %collective-permute-done.4.token.refs_2_), channel_id=1, source_target_pairs={{0,8},{2,10},{8,16},{10,18},{16,24},{18,26},{24,28},{26,30},{28,20... | collective-permute-start | bytes 1572872 | tf_op jit(solution)/shard_map/ppermute | solution.py:407
  61.4 20.9 %collective-permute-start.7 = (f32[2,4,128,128]{3,2,1,0:T(8,128)}, f32[2,4,128,128]{3,2,1,0:T(8,128)}, u32[]{:S(2)}, u32[]{:S(2)}) collective-permute-start(f32[2,4,128,128]{3,2,1,0:T(8,128)} %collective-permute-done.5.refs_5_), channel_id=1, source_target_pairs={{0,4},{2,6},{8,0},{10,2},{16,8},{18,10},{24,16},{26,18},{28,24},{3... | collective-permute-start | bytes 1572872 | tf_op jit(solution)/shard_map/ppermute | solution.py:407
  71.0 21.3 %collective-permute-start.15 = (f32[2,4,128,128]{3,2,1,0:T(8,128)}, f32[2,4,128,128]{3,2,1,0:T(8,128)}, u32[]{:S(2)}, u32[]{:S(2)}) collective-permute-start(f32[2,4,128,128]{3,2,1,0:T(8,128)} %collective-permute-done.14.refs_14_), channel_id=1, source_target_pairs={{0,4},{2,6},{8,0},{10,2},{16,8},{18,10},{24,16},{26,18},{28,24},{3... | collective-permute-start | bytes 1572872 | tf_op jit(solution)/shard_map/ppermute | solution.py:407
  82.2 61.4 %copy-start.20 = (f32[1,128,128]{2,1,0:T(8,128)S(1)}, f32[1,128,128]{2,1,0:T(8,128)}, u32[]{:S(2)}) copy-start(f32[1,128,128]{2,1,0:T(8,128)} %get-tuple-element.78) | copy-start | bytes 196612
  82.3 11.9 %collective-permute-start.8 = (f32[2,4,128,128]{3,2,1,0:T(8,128)}, f32[2,4,128,128]{3,2,1,0:T(8,128)S(1)}, u32[]{:S(2)}, u32[]{:S(2)}) collective-permute-start(f32[2,4,128,128]{3,2,1,0:T(8,128)} %collective-permute-done.6.refs_3_), channel_id=1, source_target_pairs={{0,8},{2,10},{8,16},{10,18},{16,24},{18,26},{24,28},{26,30},{28,20... | collective-permute-start | bytes 1572872 | tf_op jit(solution)/shard_map/ppermute | solution.py:407
  92.4 2.6 %collective-permute-start.23 = (f32[2,4,128,128]{3,2,1,0:T(8,128)S(1)}, f32[2,4,128,128]{3,2,1,0:T(8,128)S(1)}, u32[]{:S(2)}, u32[]{:S(2)}) collective-permute-start(f32[2,4,128,128]{3,2,1,0:T(8,128)S(1)} %collective-permute-done.9.refs_9_), channel_id=1, source_target_pairs={{0,2},{2,0},{4,6},{6,4},{8,10},{10,8},{12,14},{14,12},{16,18},{18,... | collective-permute-start | bytes 1572872 | tf_op jit(solution)/shard_map/ppermute | solution.py:380
  92.4 2.9 %collective-permute-start.24 = (f32[2,4,128,128]{3,2,1,0:T(8,128)}, f32[2,4,128,128]{3,2,1,0:T(8,128)S(1)}, u32[]{:S(2)}, u32[]{:S(2)}) collective-permute-start(f32[2,4,128,128]{3,2,1,0:T(8,128)} %copy-done.3), channel_id=1, source_target_pairs={{0,2},{2,0},{4,6},{6,4},{8,10},{10,8},{12,14},{14,12},{16,18},{18,... | collective-permute-start | bytes 1572872 | tf_op jit(solution)/shard_map/ppermute | solution.py:380
  92.9 3.1 %collective-permute-start.25 = (f32[2,4,128,128]{3,2,1,0:T(8,128)}, f32[2,4,128,128]{3,2,1,0:T(8,128)S(1)}, u32[]{:S(2)}, u32[]{:S(2)}) collective-permute-start(f32[2,4,128,128]{3,2,1,0:T(8,128)} %collective-permute-done.13.refs_11_), channel_id=1, source_target_pairs={{0,2},{2,0},{4,6},{6,4},{8,10},{10,8},{12,14},{14,12},{16,18},{18,... | collective-permute-start | bytes 1572872 | tf_op jit(solution)/shard_map/ppermute | solution.py:380
  94.1 8.0 %copy-start.5 = (f32[2,4,128,128]{3,2,1,0:T(8,128)}, f32[2,4,128,128]{3,2,1,0:T(8,128)S(1)}, u32[]{:S(2)}) copy-start(f32[2,4,128,128]{3,2,1,0:T(8,128)S(1)} %collective-permute-done.8.refs_7_) | copy-start | bytes 1572868
  94.1 2.4 %collective-permute-start.26 = (f32[2,4,128,128]{3,2,1,0:T(8,128)S(1)}, f32[2,4,128,128]{3,2,1,0:T(8,128)S(1)}, u32[]{:S(2)}, u32[]{:S(2)}) collective-permute-start(f32[2,4,128,128]{3,2,1,0:T(8,128)S(1)} %collective-permute-done.10.refs_12_), channel_id=1, source_target_pairs={{0,2},{2,0},{4,6},{6,4},{8,10},{10,8},{12,14},{14,12},{16,18},{18,... | collective-permute-start | bytes 1572872 | tf_op jit(solution)/shard_map/ppermute | solution.py:380
  95.0 9.0 %copy-start.6 = (f32[2,4,128,128]{3,2,1,0:T(8,128)}, f32[2,4,128,128]{3,2,1,0:T(8,128)S(1)}, u32[]{:S(2)}) copy-start(f32[2,4,128,128]{3,2,1,0:T(8,128)S(1)} %collective-permute-done.23.refs_25_) | copy-start | bytes 1572868
  95.0 2.5 %collective-permute-start.27 = (f32[2,4,128,128]{3,2,1,0:T(8,128)}, f32[2,4,128,128]{3,2,1,0:T(8,128)S(1)}, u32[]{:S(2)}, u32[]{:S(2)}) collective-permute-start(f32[2,4,128,128]{3,2,1,0:T(8,128)} %copy-done.4), channel_id=1, source_target_pairs={{0,2},{2,0},{4,6},{6,4},{8,10},{10,8},{12,14},{14,12},{16,18},{18,... | collective-permute-start | bytes 1572872 | tf_op jit(solution)/shard_map/ppermute | solution.py:380
  95.2 8.8 %copy-start.7 = (f32[2,4,128,128]{3,2,1,0:T(8,128)}, f32[2,4,128,128]{3,2,1,0:T(8,128)S(1)}, u32[]{:S(2)}) copy-start(f32[2,4,128,128]{3,2,1,0:T(8,128)S(1)} %collective-permute-done.24.refs_26_) | copy-start | bytes 1572868
  95.2 3.0 %collective-permute-start.28 = (f32[2,4,128,128]{3,2,1,0:T(8,128)}, f32[2,4,128,128]{3,2,1,0:T(8,128)S(1)}, u32[]{:S(2)}, u32[]{:S(2)}) collective-permute-start(f32[2,4,128,128]{3,2,1,0:T(8,128)} %collective-permute-done.14.refs_14_), channel_id=1, source_target_pairs={{0,2},{2,0},{4,6},{6,4},{8,10},{10,8},{12,14},{14,12},{16,18},{18,... | collective-permute-start | bytes 1572872 | tf_op jit(solution)/shard_map/ppermute | solution.py:380
  96.0 8.0 %copy-start.8 = (f32[2,4,128,128]{3,2,1,0:T(8,128)}, f32[2,4,128,128]{3,2,1,0:T(8,128)S(1)}, u32[]{:S(2)}) copy-start(f32[2,4,128,128]{3,2,1,0:T(8,128)S(1)} %collective-permute-done.25.refs_27_) | copy-start | bytes 1572868
  96.0 3.0 %collective-permute-start.29 = (f32[2,4,128,128]{3,2,1,0:T(8,128)}, f32[2,4,128,128]{3,2,1,0:T(8,128)S(1)}, u32[]{:S(2)}, u32[]{:S(2)}) collective-permute-start(f32[2,4,128,128]{3,2,1,0:T(8,128)} %collective-permute-done.15.refs_15_), channel_id=1, source_target_pairs={{0,2},{2,0},{4,6},{6,4},{8,10},{10,8},{12,14},{14,12},{16,18},{18,... | collective-permute-start | bytes 1572872 | tf_op jit(solution)/shard_map/ppermute | solution.py:380
  96.5 7.5 %copy-start.9 = (f32[2,4,128,128]{3,2,1,0:T(8,128)}, f32[2,4,128,128]{3,2,1,0:T(8,128)S(1)}, u32[]{:S(2)}) copy-start(f32[2,4,128,128]{3,2,1,0:T(8,128)S(1)} %collective-permute-done.26.refs_28_) | copy-start | bytes 1572868
  96.5 3.2 %collective-permute-start.16 = (f32[2,4,128,128]{3,2,1,0:T(8,128)}, f32[2,4,128,128]{3,2,1,0:T(8,128)S(1)}, u32[]{:S(2)}, u32[]{:S(2)}) collective-permute-start(f32[2,4,128,128]{3,2,1,0:T(8,128)} %collective-permute-done.1.token.refs_1_), channel_id=1, source_target_pairs={{0,2},{2,0},{4,6},{6,4},{8,10},{10,8},{12,14},{14,12},{16,18},{18,... | collective-permute-start | bytes 1572872 | tf_op jit(solution)/shard_map/ppermute | solution.py:380
  97.5 9.0 %copy-start.10 = (f32[2,4,128,128]{3,2,1,0:T(8,128)}, f32[2,4,128,128]{3,2,1,0:T(8,128)S(1)}, u32[]{:S(2)}) copy-start(f32[2,4,128,128]{3,2,1,0:T(8,128)S(1)} %collective-permute-done.27.refs_29_) | copy-start | bytes 1572868
  97.5 3.0 %collective-permute-start.17 = (f32[2,4,128,128]{3,2,1,0:T(8,128)}, f32[2,4,128,128]{3,2,1,0:T(8,128)S(1)}, u32[]{:S(2)}, u32[]{:S(2)}) collective-permute-start(f32[2,4,128,128]{3,2,1,0:T(8,128)} %collective-permute-done.4.token.refs_2_), channel_id=1, source_target_pairs={{0,2},{2,0},{4,6},{6,4},{8,10},{10,8},{12,14},{14,12},{16,18},{18,... | collective-permute-start | bytes 1572872 | tf_op jit(solution)/shard_map/ppermute | solution.py:380
  98.2 5.8 %copy-start.11 = (f32[2,4,128,128]{3,2,1,0:T(8,128)}, f32[2,4,128,128]{3,2,1,0:T(8,128)S(1)}, u32[]{:S(2)}) copy-start(f32[2,4,128,128]{3,2,1,0:T(8,128)S(1)} %collective-permute-done.28.refs_30_) | copy-start | bytes 1572868
  98.2 3.7 %collective-permute-start.18 = (f32[2,4,128,128]{3,2,1,0:T(8,128)}, f32[2,4,128,128]{3,2,1,0:T(8,128)S(1)}, u32[]{:S(2)}, u32[]{:S(2)}) collective-permute-start(f32[2,4,128,128]{3,2,1,0:T(8,128)} %collective-permute-done.6.refs_3_), channel_id=1, source_target_pairs={{0,2},{2,0},{4,6},{6,4},{8,10},{10,8},{12,14},{14,12},{16,18},{18,... | collective-permute-start | bytes 1572872 | tf_op jit(solution)/shard_map/ppermute | solution.py:380
  99.0 5.1 %copy-start.12 = (f32[2,4,128,128]{3,2,1,0:T(8,128)}, f32[2,4,128,128]{3,2,1,0:T(8,128)S(1)}, u32[]{:S(2)}) copy-start(f32[2,4,128,128]{3,2,1,0:T(8,128)S(1)} %collective-permute-done.29.refs_31_) | copy-start | bytes 1572868
  99.0 3.1 %collective-permute-start.19 = (f32[2,4,128,128]{3,2,1,0:T(8,128)S(1)}, f32[2,4,128,128]{3,2,1,0:T(8,128)S(1)}, u32[]{:S(2)}, u32[]{:S(2)}) collective-permute-start(f32[2,4,128,128]{3,2,1,0:T(8,128)S(1)} %collective-permute-done.3.refs_4_), channel_id=1, source_target_pairs={{0,2},{2,0},{4,6},{6,4},{8,10},{10,8},{12,14},{14,12},{16,18},{18,... | collective-permute-start | bytes 1572872 | tf_op jit(solution)/shard_map/ppermute | solution.py:380
  99.7 6.7 %copy-start.13 = (f32[2,4,128,128]{3,2,1,0:T(8,128)}, f32[2,4,128,128]{3,2,1,0:T(8,128)S(1)}, u32[]{:S(2)}) copy-start(f32[2,4,128,128]{3,2,1,0:T(8,128)S(1)} %collective-permute-done.16.refs_17_) | copy-start | bytes 1572868
  99.7 3.0 %collective-permute-start.20 = (f32[2,4,128,128]{3,2,1,0:T(8,128)}, f32[2,4,128,128]{3,2,1,0:T(8,128)S(1)}, u32[]{:S(2)}, u32[]{:S(2)}) collective-permute-start(f32[2,4,128,128]{3,2,1,0:T(8,128)} %collective-permute-done.5.refs_5_), channel_id=1, source_target_pairs={{0,2},{2,0},{4,6},{6,4},{8,10},{10,8},{12,14},{14,12},{16,18},{18,... | collective-permute-start | bytes 1572872 | tf_op jit(solution)/shard_map/ppermute | solution.py:380
  100.5 3.6 %copy-start.14 = (f32[2,4,128,128]{3,2,1,0:T(8,128)}, f32[2,4,128,128]{3,2,1,0:T(8,128)S(1)}, u32[]{:S(2)}) copy-start(f32[2,4,128,128]{3,2,1,0:T(8,128)S(1)} %collective-permute-done.17.refs_18_) | copy-start | bytes 1572868
  100.5 3.0 %collective-permute-start.21 = (f32[2,4,128,128]{3,2,1,0:T(8,128)}, f32[2,4,128,128]{3,2,1,0:T(8,128)S(1)}, u32[]{:S(2)}, u32[]{:S(2)}) collective-permute-start(f32[2,4,128,128]{3,2,1,0:T(8,128)} %collective-permute-done.7.refs_6_), channel_id=1, source_target_pairs={{0,2},{2,0},{4,6},{6,4},{8,10},{10,8},{12,14},{14,12},{16,18},{18,... | collective-permute-start | bytes 1572872 | tf_op jit(solution)/shard_map/ppermute | solution.py:380
  102.0 2.1 %copy-start.15 = (f32[2,4,128,128]{3,2,1,0:T(8,128)}, f32[2,4,128,128]{3,2,1,0:T(8,128)S(1)}, u32[]{:S(2)}) copy-start(f32[2,4,128,128]{3,2,1,0:T(8,128)S(1)} %collective-permute-done.18.refs_19_) | copy-start | bytes 1572868
  102.0 2.0 %collective-permute-start.22 = (f32[2,4,128,128]{3,2,1,0:T(8,128)S(1)}, f32[2,4,128,128]{3,2,1,0:T(8,128)S(1)}, u32[]{:S(2)}, u32[]{:S(2)}) collective-permute-start(f32[2,4,128,128]{3,2,1,0:T(8,128)S(1)} %collective-permute-done.8.refs_7_), channel_id=1, source_target_pairs={{0,2},{2,0},{4,6},{6,4},{8,10},{10,8},{12,14},{14,12},{16,18},{18,... | collective-permute-start | bytes 1572872 | tf_op jit(solution)/shard_map/ppermute | solution.py:380
  102.1 2.0 %copy-start.16 = (f32[2,4,128,128]{3,2,1,0:T(8,128)}, f32[2,4,128,128]{3,2,1,0:T(8,128)S(1)}, u32[]{:S(2)}) copy-start(f32[2,4,128,128]{3,2,1,0:T(8,128)S(1)} %collective-permute-done.19.refs_20_) | copy-start | bytes 1572868
  102.7 1.4 copy-start.17
  103.5 0.8 copy-start.18
  104.3 0.8 copy-start.19
  123.1 2.2 %collective-permute-start.30 = (f32[8,128,128]{2,1,0:T(8,128)}, f32[8,128,128]{2,1,0:T(8,128)S(1)}, u32[]{:S(2)}, u32[]{:S(2)}) collective-permute-start(f32[8,128,128]{2,1,0:T(8,128)} %get-tuple-element.80), channel_id=1, source_target_pairs={{0,2},{2,0},{4,6},{6,4},{8,10},{10,8},{12,14},{14,12},{16,18},{18,... | collective-permute-start | bytes 1572872 | tf_op jit(solution)/shard_map/ppermute | solution.py:380
  126.4 8.1 %collective-permute-start.31 = (f32[1,128,128]{2,1,0:T(8,128)S(1)}, f32[1,128,128]{2,1,0:T(8,128)S(1)}, u32[]{:S(2)}, u32[]{:S(2)}) collective-permute-start(f32[1,128,128]{2,1,0:T(8,128)S(1)} %get-tuple-element.84), channel_id=1, source_target_pairs={{0,4},{2,6},{4,0},{6,2},{8,12},{10,14},{12,8},{14,10},{16,20},{18,... | collective-permute-start | bytes 196616 | tf_op jit(solution)/shard_map/ppermute | solution.py:432
  126.5 11.8 %collective-permute-start.34 = (f32[1,128,128]{2,1,0:T(8,128)S(1)}, f32[1,128,128]{2,1,0:T(8,128)S(1)}, u32[]{:S(2)}, u32[]{:S(2)}) collective-permute-start(f32[1,128,128]{2,1,0:T(8,128)S(1)} %get-tuple-element.85), channel_id=1, source_target_pairs={{0,28},{2,30},{4,24},{6,26},{8,4},{10,6},{12,0},{14,2},{16,12},{18... | collective-permute-start | bytes 196616 | tf_op jit(solution)/shard_map/ppermute | solution.py:432
  129.8 9.3 %collective-permute-start.33 = (f32[1,128,128]{2,1,0:T(8,128)S(1)}, f32[1,128,128]{2,1,0:T(8,128)S(1)}, u32[]{:S(2)}, u32[]{:S(2)}) collective-permute-start(f32[1,128,128]{2,1,0:T(8,128)S(1)} %get-tuple-element.86), channel_id=1, source_target_pairs={{0,20},{2,22},{4,16},{6,18},{8,28},{10,30},{12,24},{14,26},{16,4},... | collective-permute-start | bytes 196616 | tf_op jit(solution)/shard_map/ppermute | solution.py:432
  131.7 7.7 %collective-permute-start.32 = (f32[1,128,128]{2,1,0:T(8,128)S(1)}, f32[1,128,128]{2,1,0:T(8,128)S(1)}, u32[]{:S(2)}, u32[]{:S(2)}) collective-permute-start(f32[1,128,128]{2,1,0:T(8,128)S(1)} %get-tuple-element.87), channel_id=1, source_target_pairs={{0,12},{2,14},{4,8},{6,10},{8,20},{10,22},{12,16},{14,18},{16,28},... | collective-permute-start | bytes 196616 | tf_op jit(solution)/shard_map/ppermute | solution.py:432
  134.4 7.0 %collective-permute-start.35 = (f32[1,128,128]{2,1,0:T(8,128)S(1)}, f32[1,128,128]{2,1,0:T(8,128)S(1)}, u32[]{:S(2)}, u32[]{:S(2)}) collective-permute-start(f32[1,128,128]{2,1,0:T(8,128)S(1)} %get-tuple-element.88), channel_id=1, source_target_pairs={{0,8},{2,10},{4,12},{6,14},{8,16},{10,18},{12,20},{14,22},{16,24},... | collective-permute-start | bytes 196616 | tf_op jit(solution)/shard_map/ppermute | solution.py:432
  134.5 6.9 %collective-permute-start.37 = (f32[1,128,128]{2,1,0:T(8,128)S(1)}, f32[1,128,128]{2,1,0:T(8,128)S(1)}, u32[]{:S(2)}, u32[]{:S(2)}) collective-permute-start(f32[1,128,128]{2,1,0:T(8,128)S(1)} %get-tuple-element.89), channel_id=1, source_target_pairs={{0,24},{2,26},{4,28},{6,30},{8,0},{10,2},{12,4},{14,6},{16,8},{18,... | collective-permute-start | bytes 196616 | tf_op jit(solution)/shard_map/ppermute | solution.py:432
  138.3 5.4 %collective-permute-start.36 = (f32[1,128,128]{2,1,0:T(8,128)S(1)}, f32[1,128,128]{2,1,0:T(8,128)S(1)}, u32[]{:S(2)}, u32[]{:S(2)}) collective-permute-start(f32[1,128,128]{2,1,0:T(8,128)S(1)} %get-tuple-element.90), channel_id=1, source_target_pairs={{0,16},{2,18},{4,20},{6,22},{8,24},{10,26},{12,28},{14,30},{16,0},... | collective-permute-start | bytes 196616 | tf_op jit(solution)/shard_map/ppermute | solution.py:432

commit v3 on v2

--- a/solution.py
+++ b/solution.py
@@ -21,6 +21,7 @@
     return pl.CostEstimate(flops=int(microseconds * 1e9), bytes_accessed=1000, transcendentals=0)
 
 
+GROUP = 6
 COSTS = dict(plan=1.0, u=1.0, sums=3.0)
 
 
@@ -61,7 +62,9 @@
         self.slot = self.place + nodes * pieces
         self.node = self.slot + nodes * rows
         self.spare = self.node + nodes
-        self.size = self.spare + 1
+        self.total = self.spare + 1
+        self.items = self.total + 1
+        self.size = self.items + nodes * rows + 1
 
 
 def plan_kernel(dims, plan, where, table, chip_of, struct, token, out):
@@ -91,6 +94,14 @@
         return carry
 
     lax.fori_loop(0, nodes, locate, 0)
+
+    def collect(kk, count):
+        for i in range(rows):
+            out[plan.items + count] = kk * rows + i
+            count = count + jnp.where(out[plan.slot + kk * rows + i] >= 0, 1, 0)
+        return count
+
+    out[plan.total] = lax.fori_loop(0, nodes, collect, jnp.int32(0))
 
 
 def make_plan(plan, dims, where, table, chip_of, struct, token):
@@ -184,35 +195,36 @@
         ]
         for a in range(sets)
     ]
-    first_loads = [
-        [
-            pltpu.make_async_copy(arrays[h].at[s, t], u_buf.at[0, s * hops + h, t], sems.at[6 + sets + t])
-            for h in range(hops)
-            for s in range(2)
-        ]
-        for t in range(per_set)
-    ]
-    for copies in [sigma_loads] + first_loads + u_loads[1:]:
+    for copies in [sigma_loads] + u_loads:
         for copy in copies:
             copy.start()
 
+    def clear(kk, carry):
+        z_buf[kk] = jnp.zeros(z_buf.shape[1:], F32)
+        return carry
+
+    lax.fori_loop(0, z_buf.shape[0], clear, 0)
+
     def slot_of(kk, i):
         return tables[plan.slot + kk * rows + i]
 
-    def products(kk, a, t, chosen):
-        size = len(chosen) * width
-        y = jnp.zeros((2 * size, 2 * width), F32)
+    total = tables[plan.total]
+
+    def item_of(index):
+        item = tables[plan.items + jnp.minimum(index, total - 1)]
+        return lax.div(item, rows), lax.rem(item, rows)
+
+    def product(kk, i):
+        a, t = lax.div(kk, per_set), lax.rem(kk, per_set)
+        y = jnp.zeros((2 * width, 2 * width), F32)
         for j in range(0, pieces, 2):
             lefts, rights = [], []
             for slot in (j, j + 1):
-                place = tables[plan.place + kk * pieces + slot]
-                left = jnp.concatenate([buf[i, place] for i in chosen], axis=0)
+                left = buf[i, tables[plan.place + kk * pieces + slot]]
                 lefts.append(jnp.concatenate(split(left), axis=0))
                 rights.append(wide(u_buf[a, slot, t]))
             y = y + dot(jnp.concatenate(lefts, axis=1), jnp.concatenate(rights, axis=0))
-        y = fold(y[:size] + y[size:])
-        for k, i in enumerate(chosen):
-            z_buf[kk, i] = -y[k * width : (k + 1) * width]
+        return fold(y[:width] + y[width:])
 
     def diagonals(a):
         for t in range(per_set):
@@ -237,66 +249,40 @@
                 )
             )
 
-    def node(kk, a, t):
-        count = jnp.int32(0)
-        for i in range(rows):
-            count += jnp.where(slot_of(kk, i) >= 0, 1, 0)
-        for i in range(rows):
-
-            @pl.when(slot_of(kk, i) < 0)
-            def absent():
-                z_buf[kk, i] = jnp.zeros((width, width), F32)
-
-        first = jnp.int32(rows - 1)
-        last = jnp.int32(0)
-        for i in range(rows):
-            here = slot_of(kk, i) >= 0
-            last = jnp.where(here, i, last)
-            first = jnp.where(here, jnp.minimum(first, i), first)
-
-        @pl.when(count == 1)
-        def single():
-            products(kk, a, t, [first])
-
-        @pl.when(count == 2)
-        def double():
-            products(kk, a, t, [first, last])
-
-        @pl.when(count >= 3)
-        def several():
-            products(kk, a, t, list(range(rows)))
-
-    for copy in sigma_loads:
+    for copy in sigma_loads + u_loads[0]:
         copy.wait()
 
-    def step(kk, carry):
-        a, t = lax.div(kk, per_set), lax.rem(kk, per_set)
-
-        @pl.when(a == 0)
-        def arrive():
-            def one(s, carry):
-                pltpu.make_async_copy(arrays[0].at[0, 0], u_buf.at[0, s, t], sems.at[6 + sets + t]).wait()
-                return carry
-
-            lax.fori_loop(0, pieces, one, 0)
-
-        for index in range(1, sets):
-
-            @pl.when(kk == index * per_set)
+    def arrive(before, now):
+        for a in range(1, sets):
+
+            @pl.when((before < a) & (now >= a))
             def arrive_set():
-                for copy in u_loads[index]:
+                for copy in u_loads[a]:
                     copy.wait()
 
-        node(kk, a, t)
-
-        @pl.when(t == per_set - 1)
-        def close_set():
-            diagonals(a)
-
-        pltpu.make_async_copy(z_buf.at[kk], z_out.at[tables[plan.node + kk]], sems.at[2 + sets]).start()
+    def close(a, carry):
+        diagonals(a)
+        for t in range(per_set):
+            kk = a * per_set + t
+            pltpu.make_async_copy(z_buf.at[kk], z_out.at[tables[plan.node + kk]], sems.at[2 + sets]).start()
         return carry
 
-    lax.fori_loop(0, sets * per_set, step, 0)
+    def step(group, carry):
+        here, closed = carry
+        found = [item_of(group * GROUP + k) for k in range(GROUP)]
+        now = lax.div(found[-1][0], per_set)
+        behind = lax.div(found[0][0], per_set)
+        lax.fori_loop(closed, behind, close, 0)
+        arrive(here, now)
+        results = [product(kk, i) for kk, i in found]
+        for (kk, i), y in zip(found, results):
+            z_buf[kk, i] = -y
+        return now, behind
+
+    groups = lax.div(total + GROUP - 1, GROUP)
+    here, closed = lax.fori_loop(0, groups, step, (jnp.int32(0), jnp.int32(0)))
+    arrive(here, sets - 1)
+    lax.fori_loop(closed, sets, close, 0)
     stores = []
     for k, p_out in enumerate(p_outs):
         size = zs if k < 2 else 2 * zs

time: 145 us -> 145 us (level)
    ppermute x7, starting transfers between devices: 11.8 us -> 10 us  [body(): z_diag = z_diag + permute(source[m:m + 1], 'row', links)]
  transfers between devices with their start and end apart: 38 -> 38, of which waited for: 33 -> 31; matrix products, arithmetic and copies ran while one was open for 0% -> 0% of each run, Pallas kernels for 12% -> 12%
where the time goes in v3:
time: 145 us; the launch traced here: 144 us
  waiting for transfers between devices  74.1 us (51%)
  Pallas kernels  34.7 us (24%)
  starting transfers between devices  29.9 us (21%)
  other arithmetic  2.38 us (2%)
  local copies, waits for them, and re-layouts  2.04 us (1%)
    ppermute x14, waiting for transfers between devices, body(): permute(front[0 if way > 0 else 1], 'row', pairs(way))  56.5 us
    pallas_call x1, Pallas kernels, all_sums(): pl.pallas_call(functools.partial(sums_kernel, (rows, zs, chip_of, sets, h...  16.9 us
    ppermute x14, starting transfers between devices, body(): permute(front[0 if way > 0 else 1], 'row', pairs(way))  14 us
    pallas_call x4, Pallas kernels, u_blocks(): pl.pallas_call(functools.partial(u_kernel, chips, other), out_shape=[jax....  13.3 us
    ppermute x16, waiting for transfers between devices, swapped(): return permute(array, 'row', swap_core)  10.1 us
    ppermute x7, starting transfers between devices, body(): z_diag = z_diag + permute(source[m:m + 1], 'row', links)  10 us
    ppermute x7, waiting for transfers between devices, body(): z_diag = z_diag + permute(source[m:m + 1], 'row', links)  6.15 us
    pallas_call x1, Pallas kernels, make_plan(): pl.pallas_call(functools.partial(plan_kernel, dims, plan), out_shape=jax....  4.42 us
  transfers between devices with their start and end apart: 38, of which 31 were waited for; matrix products, arithmetic and copies ran while one was open for 0% of the time, Pallas kernels for 12%

profile of v3, /device:TPU:0, one launch (start us, length us, event | category | flops | bytes accessed | tf_op | source)
XLA Modules:
  0.0 143.9 jit_solution(7058724976521901089)
XLA Ops:
  0.6 0.5 collective-permute-start
  1.1 2.6 %collective-permute-start.2 = (f32[3,24,128,128]{3,2,1,0:T(8,128)}, f32[3,24,128,128]{3,2,1,0:T(8,128)}, u32[]{:S(2)}, u32[]{:S(2)}) collective-permute-start(f32[3,24,128,128]{3,2,1,0:T(8,128)} %near.1), channel_id=1, source_target_pairs={{1,0},{0,1},{3,2},{2,3},{5,4},{4,5},{7,6},{6,7},{9,8},{8,9},{11,10... | collective-permute-start | bytes 14155784 | tf_op jit(solution)/shard_map/ppermute | solution.py:372
  3.7 0.6 pad_add_fusion.where
  4.4 1.0 copy-done.21
  5.3 3.3 %u_blocks.7 = (f32[2,4,128,128]{3,2,1,0:T(8,128)}, f32[1,128,128]{2,1,0:T(8,128)}) custom-call(s32[2]{0:T(128)} %pad_add_fusion.where, f32[16,128,128]{2,1,0:T(8,128)} %bitcast.4, f32[16,128,128]{2,1,0:T(8,128)} %copy-done.21, f32[16,128,128]{2,1,0:T(8,128)} %inverse.7, s32[16,16]{1,0:T(8,128)} %token_.3), custom_call_target="tpu_custom_call" | custom-call | flops 1000000000 | bytes 1000 | tf_op jit(solution)/shard_map/u_blocks/pallas_call | solution.py:158
  8.7 2.3 %collective-permute-start.9 = (f32[2,4,128,128]{3,2,1,0:T(8,128)}, f32[2,4,128,128]{3,2,1,0:T(8,128)S(1)}, u32[]{:S(2)}, u32[]{:S(2)}) collective-permute-start(f32[2,4,128,128]{3,2,1,0:T(8,128)} %get-tuple-element.57.refs_8_), channel_id=1, source_target_pairs={{0,8},{2,10},{8,16},{10,18},{16,24},{18,26},{24,28},{26,30},{28,20... | collective-permute-start | bytes 1572872 | tf_op jit(solution)/shard_map/ppermute | solution.py:393
  10.9 3.3 %u_blocks.4 = (f32[2,4,128,128]{3,2,1,0:T(8,128)}, f32[1,128,128]{2,1,0:T(8,128)}) custom-call(s32[2]{0:T(128)} %pad_add_fusion.where, f32[16,128,128]{2,1,0:T(8,128)} %bitcast.5, f32[16,128,128]{2,1,0:T(8,128)} %copy-done.21, f32[16,128,128]{2,1,0:T(8,128)} %inverse.7, s32[16,16]{1,0:T(8,128)} %token_.3), custom_call_target="tpu_custom_call" | custom-call | flops 1000000000 | bytes 1000 | tf_op jit(solution)/shard_map/u_blocks/pallas_call | solution.py:158
  14.3 2.1 %collective-permute-start.1 = (f32[2,4,128,128]{3,2,1,0:T(8,128)}, f32[2,4,128,128]{3,2,1,0:T(8,128)}, u32[]{:S(2)}, u32[]{:S(2)}) collective-permute-start(f32[2,4,128,128]{3,2,1,0:T(8,128)} %get-tuple-element.44.refs_0_), channel_id=1, source_target_pairs={{0,8},{2,10},{8,16},{10,18},{16,24},{18,26},{24,28},{26,30},{28,20... | collective-permute-start | bytes 1572872 | tf_op jit(solution)/shard_map/ppermute | solution.py:393
  16.4 7.4 %collective-permute-done.9.refs_9_ = f32[2,4,128,128]{3,2,1,0:T(8,128)S(1)} collective-permute-done((f32[2,4,128,128]{3,2,1,0:T(8,128)}, f32[2,4,128,128]{3,2,1,0:T(8,128)S(1)}, u32[]{:S(2)}, u32[]{:S(2)}) %collective-permute-start.9) | collective-permute-done | bytes 524320 | tf_op jit(solution)/shard_map/ppermute | solution.py:393
  23.8 2.2 %collective-permute-done.10.refs_12_ = f32[2,4,128,128]{3,2,1,0:T(8,128)S(1)} collective-permute-done((f32[2,4,128,128]{3,2,1,0:T(8,128)}, f32[2,4,128,128]{3,2,1,0:T(8,128)S(1)}, u32[]{:S(2)}, u32[]{:S(2)}) %collective-permute-start.10) | collective-permute-done | bytes 524320 | tf_op jit(solution)/shard_map/ppermute | solution.py:393
  26.0 1.6 %collective-permute-start.11 = (f32[2,4,128,128]{3,2,1,0:T(8,128)S(1)}, f32[2,4,128,128]{3,2,1,0:T(8,128)S(1)}, u32[]{:S(2)}, u32[]{:S(2)}) collective-permute-start(f32[2,4,128,128]{3,2,1,0:T(8,128)S(1)} %collective-permute-done.9.refs_9_), channel_id=1, source_target_pairs={{0,8},{2,10},{8,16},{10,18},{16,24},{18,26},{24,28},{26,30},{28,20... | collective-permute-start | bytes 1572872 | tf_op jit(solution)/shard_map/ppermute | solution.py:393
  27.5 0.5 collective-permute-start.12
  28.0 7.1 %collective-permute-done.1.token.refs_1_ = f32[2,4,128,128]{3,2,1,0:T(8,128)} collective-permute-done((f32[2,4,128,128]{3,2,1,0:T(8,128)}, f32[2,4,128,128]{3,2,1,0:T(8,128)}, u32[]{:S(2)}, u32[]{:S(2)}) %collective-permute-start.1) | collective-permute-done | bytes 524320 | tf_op jit(solution)/shard_map/ppermute | solution.py:393
  35.1 2.1 %collective-permute-done.3.refs_4_ = f32[2,4,128,128]{3,2,1,0:T(8,128)S(1)} collective-permute-done((f32[2,4,128,128]{3,2,1,0:T(8,128)}, f32[2,4,128,128]{3,2,1,0:T(8,128)S(1)}, u32[]{:S(2)}, u32[]{:S(2)}) %collective-permute-start.3) | collective-permute-done | bytes 524320 | tf_op jit(solution)/shard_map/ppermute | solution.py:393
  37.2 1.6 %collective-permute-start.4 = (f32[2,4,128,128]{3,2,1,0:T(8,128)}, f32[2,4,128,128]{3,2,1,0:T(8,128)}, u32[]{:S(2)}, u32[]{:S(2)}) collective-permute-start(f32[2,4,128,128]{3,2,1,0:T(8,128)} %collective-permute-done.1.token.refs_1_), channel_id=1, source_target_pairs={{0,8},{2,10},{8,16},{10,18},{16,24},{18,26},{24,28},{26,30},{28,20... | collective-permute-start | bytes 1572872 | tf_op jit(solution)/shard_map/ppermute | solution.py:393
  38.8 0.5 collective-permute-start.5
  39.2 7.0 %collective-permute-done.11.refs_10_ = f32[2,4,128,128]{3,2,1,0:T(8,128)S(1)} collective-permute-done((f32[2,4,128,128]{3,2,1,0:T(8,128)S(1)}, f32[2,4,128,128]{3,2,1,0:T(8,128)S(1)}, u32[]{:S(2)}, u32[]{:S(2)}) %collective-permute-start.11) | collective-permute-done | bytes 524320 | tf_op jit(solution)/shard_map/ppermute | solution.py:393
  46.2 2.2 %collective-permute-done.12.refs_13_ = f32[2,4,128,128]{3,2,1,0:T(8,128)S(1)} collective-permute-done((f32[2,4,128,128]{3,2,1,0:T(8,128)S(1)}, f32[2,4,128,128]{3,2,1,0:T(8,128)S(1)}, u32[]{:S(2)}, u32[]{:S(2)}) %collective-permute-start.12) | collective-permute-done | bytes 524320 | tf_op jit(solution)/shard_map/ppermute | solution.py:393
  48.4 1.6 %collective-permute-start.13 = (f32[2,4,128,128]{3,2,1,0:T(8,128)S(1)}, f32[2,4,128,128]{3,2,1,0:T(8,128)}, u32[]{:S(2)}, u32[]{:S(2)}) collective-permute-start(f32[2,4,128,128]{3,2,1,0:T(8,128)S(1)} %collective-permute-done.11.refs_10_), channel_id=1, source_target_pairs={{0,8},{2,10},{8,16},{10,18},{16,24},{18,26},{24,28},{26,30},{28,20... | collective-permute-start | bytes 1572872 | tf_op jit(solution)/shard_map/ppermute | solution.py:393
  50.0 0.5 collective-permute-start.14
  50.5 4.4 %plan.1.tables = s32[371]{0:T(512)} custom-call(s32[2]{0:T(128)} %pad_add_fusion.where, s32[256]{0:T(256)} %constant.12.clone.table, s32[8]{0:T(128)} %constant.13.clone.chip_of, s32[16,16]{1,0:T(8,128)} %token_.3, f32[2,4,128,128]{3,2,1,0:T(8,128)} %collective-permute-done.1.token.refs_1_), custom_call_target="tpu_custom_call" | custom-call | flops 1000000000 | bytes 1000 | tf_op jit(solution)/shard_map/plan/pallas_call | solution.py:109
  54.9 2.7 %collective-permute-done.4.token.refs_2_ = f32[2,4,128,128]{3,2,1,0:T(8,128)} collective-permute-done((f32[2,4,128,128]{3,2,1,0:T(8,128)}, f32[2,4,128,128]{3,2,1,0:T(8,128)}, u32[]{:S(2)}, u32[]{:S(2)}) %collective-permute-start.4) | collective-permute-done | bytes 524320 | tf_op jit(solution)/shard_map/ppermute | solution.py:393
  57.6 2.2 %collective-permute-done.5.refs_5_ = f32[2,4,128,128]{3,2,1,0:T(8,128)} collective-permute-done((f32[2,4,128,128]{3,2,1,0:T(8,128)S(1)}, f32[2,4,128,128]{3,2,1,0:T(8,128)}, u32[]{:S(2)}, u32[]{:S(2)}) %collective-permute-start.5) | collective-permute-done | bytes 524320 | tf_op jit(solution)/shard_map/ppermute | solution.py:393
  59.8 1.6 %collective-permute-start.6 = (f32[2,4,128,128]{3,2,1,0:T(8,128)}, f32[2,4,128,128]{3,2,1,0:T(8,128)}, u32[]{:S(2)}, u32[]{:S(2)}) collective-permute-start(f32[2,4,128,128]{3,2,1,0:T(8,128)} %collective-permute-done.4.token.refs_2_), channel_id=1, source_target_pairs={{0,8},{2,10},{8,16},{10,18},{16,24},{18,26},{24,28},{26,30},{28,20... | collective-permute-start | bytes 1572872 | tf_op jit(solution)/shard_map/ppermute | solution.py:393
  61.4 0.5 collective-permute-start.7
  61.8 7.0 %collective-permute-done.13.refs_11_ = f32[2,4,128,128]{3,2,1,0:T(8,128)} collective-permute-done((f32[2,4,128,128]{3,2,1,0:T(8,128)S(1)}, f32[2,4,128,128]{3,2,1,0:T(8,128)}, u32[]{:S(2)}, u32[]{:S(2)}) %collective-permute-start.13) | collective-permute-done | bytes 524320 | tf_op jit(solution)/shard_map/ppermute | solution.py:393
  68.8 2.2 %collective-permute-done.14.refs_14_ = f32[2,4,128,128]{3,2,1,0:T(8,128)} collective-permute-done((f32[2,4,128,128]{3,2,1,0:T(8,128)S(1)}, f32[2,4,128,128]{3,2,1,0:T(8,128)}, u32[]{:S(2)}, u32[]{:S(2)}) %collective-permute-start.14) | collective-permute-done | bytes 524320 | tf_op jit(solution)/shard_map/ppermute | solution.py:393
  71.0 3.3 %u_blocks.6 = (f32[2,4,128,128]{3,2,1,0:T(8,128)}, f32[1,128,128]{2,1,0:T(8,128)}) custom-call(s32[2]{0:T(128)} %pad_add_fusion.where, f32[16,128,128]{2,1,0:T(8,128)} %bitcast.6, f32[16,128,128]{2,1,0:T(8,128)} %copy-done.21, f32[16,128,128]{2,1,0:T(8,128)} %inverse.7, f32[2,4,128,128]{3,2,1,0:T(8,128)} %collective-permute-done.4.token.refs_2_), custom_call_target="tpu_custom_call" | custom-call | flops 1000000000 | bytes 1000 | tf_op jit(solution)/shard_map/u_blocks/pallas_call | solution.py:158
  74.4 3.3 %u_blocks.5 = (f32[2,4,128,128]{3,2,1,0:T(8,128)}, f32[1,128,128]{2,1,0:T(8,128)}) custom-call(s32[2]{0:T(128)} %pad_add_fusion.where, f32[16,128,128]{2,1,0:T(8,128)} %bitcast.7, f32[16,128,128]{2,1,0:T(8,128)} %copy-done.21, f32[16,128,128]{2,1,0:T(8,128)} %inverse.7, f32[2,4,128,128]{3,2,1,0:T(8,128)} %collective-permute-done.4.token.refs_2_), custom_call_target="tpu_custom_call" | custom-call | flops 1000000000 | bytes 1000 | tf_op jit(solution)/shard_map/u_blocks/pallas_call | solution.py:158
  77.7 1.9 %collective-permute-done.6.refs_3_ = f32[2,4,128,128]{3,2,1,0:T(8,128)} collective-permute-done((f32[2,4,128,128]{3,2,1,0:T(8,128)}, f32[2,4,128,128]{3,2,1,0:T(8,128)}, u32[]{:S(2)}, u32[]{:S(2)}) %collective-permute-start.6) | collective-permute-done | bytes 524320 | tf_op jit(solution)/shard_map/ppermute | solution.py:393
  79.6 2.7 %collective-permute-done.7.refs_6_ = f32[2,4,128,128]{3,2,1,0:T(8,128)} collective-permute-done((f32[2,4,128,128]{3,2,1,0:T(8,128)}, f32[2,4,128,128]{3,2,1,0:T(8,128)}, u32[]{:S(2)}, u32[]{:S(2)}) %collective-permute-start.7) | collective-permute-done | bytes 524320 | tf_op jit(solution)/shard_map/ppermute | solution.py:393
  82.3 1.6 %collective-permute-start.8 = (f32[2,4,128,128]{3,2,1,0:T(8,128)}, f32[2,4,128,128]{3,2,1,0:T(8,128)S(1)}, u32[]{:S(2)}, u32[]{:S(2)}) collective-permute-start(f32[2,4,128,128]{3,2,1,0:T(8,128)} %collective-permute-done.6.refs_3_), channel_id=1, source_target_pairs={{0,8},{2,10},{8,16},{10,18},{16,24},{18,26},{24,28},{26,30},{28,20... | collective-permute-start | bytes 1572872 | tf_op jit(solution)/shard_map/ppermute | solution.py:393
  83.8 8.5 %collective-permute-done.15.refs_15_ = f32[2,4,128,128]{3,2,1,0:T(8,128)} collective-permute-done((f32[2,4,128,128]{3,2,1,0:T(8,128)}, f32[2,4,128,128]{3,2,1,0:T(8,128)}, u32[]{:S(2)}, u32[]{:S(2)}) %collective-permute-start.15) | collective-permute-done | bytes 524320 | tf_op jit(solution)/shard_map/ppermute | solution.py:393
  92.4 0.5 collective-permute-start.24
  92.9 1.3 collective-permute-done.8.refs_7_
  94.2 0.8 collective-permute-done.23.refs_25_
  95.0 0.1 collective-permute-start.27
  95.2 0.3 collective-permute-start.28
  95.5 0.5 collective-permute-done.25.refs_27_
  96.1 0.4 collective-permute-done.26.refs_28_
  96.7 0.8 collective-permute-done.27.refs_29_
  97.6 0.6 collective-permute-done.28.refs_30_
  98.4 0.6 collective-permute-done.29.refs_31_
  99.1 0.6 collective-permute-done.16.refs_17_
  99.9 0.6 collective-permute-done.17.refs_18_
  100.6 1.4 collective-permute-done.18.refs_19_
  102.1 0.6 collective-permute-done.20.refs_21_
  102.7 0.7 collective-permute-done.21.refs_22_
  103.5 0.5 collective-permute-done.22.refs_23_
  104.1 0.2 copy-done.18
  104.3 0.8 copy-done.19
  105.1 1.4 collective-permute-done.2.far
  106.5 16.9 %all_sums.1 = (f32[16,3,128,128]{3,2,1,0:T(8,128)}, f32[4,128,128]{2,1,0:T(8,128)}, f32[4,128,128]{2,1,0:T(8,128)}, f32[8,128,128]{2,1,0:T(8,128)}) custom-call(s32[2]{0:T(128)} %pad_add_fusion.where, s32[371]{0:T(512)} %plan.1.tables, f32[3,24,128,128]{3,2,1,0:T(8,128)} %near.1, f32[3,24,128,128]{3,2,1,0:T(8,128)} %collective-permute-done.2.far, ...), custom_call_target="tpu_custom_call" | custom-call | flops 3000000000 | bytes 1000 | tf_op jit(solution)/shard_map/all_sums/pallas_call | solution.py:311
  123.4 0.7 collective-permute-start.30
  124.1 1.7 %collective-permute-done.30 = f32[8,128,128]{2,1,0:T(8,128)S(1)} collective-permute-done((f32[8,128,128]{2,1,0:T(8,128)}, f32[8,128,128]{2,1,0:T(8,128)S(1)}, u32[]{:S(2)}, u32[]{:S(2)}) %collective-permute-start.30) | collective-permute-done | bytes 524320 | tf_op jit(solution)/shard_map/ppermute | solution.py:366
  125.8 1.1 slice_add_fusion
  127.1 4.0 %collective-permute-start.34 = (f32[1,128,128]{2,1,0:T(8,128)S(1)}, f32[1,128,128]{2,1,0:T(8,128)S(1)}, u32[]{:S(2)}, u32[]{:S(2)}) collective-permute-start(f32[1,128,128]{2,1,0:T(8,128)S(1)} %get-tuple-element.85), channel_id=1, source_target_pairs={{0,28},{2,30},{4,24},{6,26},{8,4},{10,6},{12,0},{14,2},{16,12},{18... | collective-permute-start | bytes 196616 | tf_op jit(solution)/shard_map/ppermute | solution.py:418
  131.0 1.2 collective-permute-start.32
  132.3 3.2 %collective-permute-start.35 = (f32[1,128,128]{2,1,0:T(8,128)S(1)}, f32[1,128,128]{2,1,0:T(8,128)S(1)}, u32[]{:S(2)}, u32[]{:S(2)}) collective-permute-start(f32[1,128,128]{2,1,0:T(8,128)S(1)} %get-tuple-element.88), channel_id=1, source_target_pairs={{0,8},{2,10},{4,12},{6,14},{8,16},{10,18},{12,20},{14,22},{16,24},... | collective-permute-start | bytes 196616 | tf_op jit(solution)/shard_map/ppermute | solution.py:418
  135.5 0.7 collective-permute-start.37
  136.2 0.9 collective-permute-start.36
  137.0 4.1 %collective-permute-done.33 = f32[1,128,128]{2,1,0:T(8,128)S(1)} collective-permute-done((f32[1,128,128]{2,1,0:T(8,128)S(1)}, f32[1,128,128]{2,1,0:T(8,128)S(1)}, u32[]{:S(2)}, u32[]{:S(2)}) %collective-permute-start.33) | collective-permute-done | bytes 65568 | tf_op jit(solution)/shard_map/ppermute | solution.py:418
  141.2 2.0 %collective-permute-done.36 = f32[1,128,128]{2,1,0:T(8,128)S(1)} collective-permute-done((f32[1,128,128]{2,1,0:T(8,128)S(1)}, f32[1,128,128]{2,1,0:T(8,128)S(1)}, u32[]{:S(2)}, u32[]{:S(2)}) %collective-permute-start.36) | collective-permute-done | bytes 65568 | tf_op jit(solution)/shard_map/ppermute | solution.py:418
  143.2 0.7 fusion.6
  (67 shorter events, 1.4 us)
Async XLA Ops:
  0.6 3.7 %collective-permute-start = (f32[16,128,128]{2,1,0:T(8,128)}, f32[16,128,128]{2,1,0:T(8,128)S(1)}, u32[]{:S(2)}, u32[]{:S(2)}) collective-permute-start(f32[16,128,128]{2,1,0:T(8,128)} %bitcast.3), channel_id=1, source_target_pairs={{0,2},{2,0},{4,6},{6,4},{8,10},{10,8},{12,14},{14,12},{16,18},{18,... | collective-permute-start | bytes 3145736 | tf_op jit(solution)/shard_map/ppermute | solution.py:366
  1.1 105.3 %collective-permute-start.2 = (f32[3,24,128,128]{3,2,1,0:T(8,128)}, f32[3,24,128,128]{3,2,1,0:T(8,128)}, u32[]{:S(2)}, u32[]{:S(2)}) collective-permute-start(f32[3,24,128,128]{3,2,1,0:T(8,128)} %near.1), channel_id=1, source_target_pairs={{1,0},{0,1},{3,2},{2,3},{5,4},{4,5},{7,6},{6,7},{9,8},{8,9},{11,10... | collective-permute-start | bytes 14155784 | tf_op jit(solution)/shard_map/ppermute | solution.py:372
  4.4 1.0 copy-start.21
  8.7 15.1 %collective-permute-start.9 = (f32[2,4,128,128]{3,2,1,0:T(8,128)}, f32[2,4,128,128]{3,2,1,0:T(8,128)S(1)}, u32[]{:S(2)}, u32[]{:S(2)}) collective-permute-start(f32[2,4,128,128]{3,2,1,0:T(8,128)} %get-tuple-element.57.refs_8_), channel_id=1, source_target_pairs={{0,8},{2,10},{8,16},{10,18},{16,24},{18,26},{24,28},{26,30},{28,20... | collective-permute-start | bytes 1572872 | tf_op jit(solution)/shard_map/ppermute | solution.py:393
  10.9 15.0 %collective-permute-start.10 = (f32[2,4,128,128]{3,2,1,0:T(8,128)}, f32[2,4,128,128]{3,2,1,0:T(8,128)S(1)}, u32[]{:S(2)}, u32[]{:S(2)}) collective-permute-start(f32[2,4,128,128]{3,2,1,0:T(8,128)} %get-tuple-element.57.refs_8_), channel_id=1, source_target_pairs={{0,4},{2,6},{8,0},{10,2},{16,8},{18,10},{24,16},{26,18},{28,24},{3... | collective-permute-start | bytes 1572872 | tf_op jit(solution)/shard_map/ppermute | solution.py:393
  14.3 20.8 %collective-permute-start.1 = (f32[2,4,128,128]{3,2,1,0:T(8,128)}, f32[2,4,128,128]{3,2,1,0:T(8,128)}, u32[]{:S(2)}, u32[]{:S(2)}) collective-permute-start(f32[2,4,128,128]{3,2,1,0:T(8,128)} %get-tuple-element.44.refs_0_), channel_id=1, source_target_pairs={{0,8},{2,10},{8,16},{10,18},{16,24},{18,26},{24,28},{26,30},{28,20... | collective-permute-start | bytes 1572872 | tf_op jit(solution)/shard_map/ppermute | solution.py:393
  16.4 20.8 %collective-permute-start.3 = (f32[2,4,128,128]{3,2,1,0:T(8,128)}, f32[2,4,128,128]{3,2,1,0:T(8,128)S(1)}, u32[]{:S(2)}, u32[]{:S(2)}) collective-permute-start(f32[2,4,128,128]{3,2,1,0:T(8,128)} %get-tuple-element.44.refs_0_), channel_id=1, source_target_pairs={{0,4},{2,6},{8,0},{10,2},{16,8},{18,10},{24,16},{26,18},{28,24},{3... | collective-permute-start | bytes 1572872 | tf_op jit(solution)/shard_map/ppermute | solution.py:393
  23.8 68.6 %copy-start = (f32[2,4,128,128]{3,2,1,0:T(8,128)}, f32[2,4,128,128]{3,2,1,0:T(8,128)S(1)}, u32[]{:S(2)}) copy-start(f32[2,4,128,128]{3,2,1,0:T(8,128)S(1)} %collective-permute-done.9.refs_9_) | copy-start | bytes 1572868
  26.0 68.2 %copy-start.1 = (f32[2,4,128,128]{3,2,1,0:T(8,128)}, f32[2,4,128,128]{3,2,1,0:T(8,128)S(1)}, u32[]{:S(2)}) copy-start(f32[2,4,128,128]{3,2,1,0:T(8,128)S(1)} %collective-permute-done.10.refs_12_) | copy-start | bytes 1572868
  26.0 20.3 %collective-permute-start.11 = (f32[2,4,128,128]{3,2,1,0:T(8,128)S(1)}, f32[2,4,128,128]{3,2,1,0:T(8,128)S(1)}, u32[]{:S(2)}, u32[]{:S(2)}) collective-permute-start(f32[2,4,128,128]{3,2,1,0:T(8,128)S(1)} %collective-permute-done.9.refs_9_), channel_id=1, source_target_pairs={{0,8},{2,10},{8,16},{10,18},{16,24},{18,26},{24,28},{26,30},{28,20... | collective-permute-start | bytes 1572872 | tf_op jit(solution)/shard_map/ppermute | solution.py:393
  27.5 20.9 %collective-permute-start.12 = (f32[2,4,128,128]{3,2,1,0:T(8,128)S(1)}, f32[2,4,128,128]{3,2,1,0:T(8,128)S(1)}, u32[]{:S(2)}, u32[]{:S(2)}) collective-permute-start(f32[2,4,128,128]{3,2,1,0:T(8,128)S(1)} %collective-permute-done.10.refs_12_), channel_id=1, source_target_pairs={{0,4},{2,6},{8,0},{10,2},{16,8},{18,10},{24,16},{26,18},{28,24},{3... | collective-permute-start | bytes 1572872 | tf_op jit(solution)/shard_map/ppermute | solution.py:393
  37.2 61.8 %copy-start.2 = (f32[2,4,128,128]{3,2,1,0:T(8,128)}, f32[2,4,128,128]{3,2,1,0:T(8,128)S(1)}, u32[]{:S(2)}) copy-start(f32[2,4,128,128]{3,2,1,0:T(8,128)S(1)} %collective-permute-done.3.refs_4_) | copy-start | bytes 1572868
  37.2 20.4 %collective-permute-start.4 = (f32[2,4,128,128]{3,2,1,0:T(8,128)}, f32[2,4,128,128]{3,2,1,0:T(8,128)}, u32[]{:S(2)}, u32[]{:S(2)}) collective-permute-start(f32[2,4,128,128]{3,2,1,0:T(8,128)} %collective-permute-done.1.token.refs_1_), channel_id=1, source_target_pairs={{0,8},{2,10},{8,16},{10,18},{16,24},{18,26},{24,28},{26,30},{28,20... | collective-permute-start | bytes 1572872 | tf_op jit(solution)/shard_map/ppermute | solution.py:393
  38.8 21.0 %collective-permute-start.5 = (f32[2,4,128,128]{3,2,1,0:T(8,128)S(1)}, f32[2,4,128,128]{3,2,1,0:T(8,128)}, u32[]{:S(2)}, u32[]{:S(2)}) collective-permute-start(f32[2,4,128,128]{3,2,1,0:T(8,128)S(1)} %collective-permute-done.3.refs_4_), channel_id=1, source_target_pairs={{0,4},{2,6},{8,0},{10,2},{16,8},{18,10},{24,16},{26,18},{28,24},{3... | collective-permute-start | bytes 1572872 | tf_op jit(solution)/shard_map/ppermute | solution.py:393
  46.2 13.5 %copy-start.3 = (f32[2,4,128,128]{3,2,1,0:T(8,128)}, f32[2,4,128,128]{3,2,1,0:T(8,128)S(1)}, u32[]{:S(2)}) copy-start(f32[2,4,128,128]{3,2,1,0:T(8,128)S(1)} %collective-permute-done.11.refs_10_) | copy-start | bytes 1572868
  48.4 20.4 %copy-start.4 = (f32[2,4,128,128]{3,2,1,0:T(8,128)}, f32[2,4,128,128]{3,2,1,0:T(8,128)S(1)}, u32[]{:S(2)}) copy-start(f32[2,4,128,128]{3,2,1,0:T(8,128)S(1)} %collective-permute-done.12.refs_13_) | copy-start | bytes 1572868
  48.4 20.4 %collective-permute-start.13 = (f32[2,4,128,128]{3,2,1,0:T(8,128)S(1)}, f32[2,4,128,128]{3,2,1,0:T(8,128)}, u32[]{:S(2)}, u32[]{:S(2)}) collective-permute-start(f32[2,4,128,128]{3,2,1,0:T(8,128)S(1)} %collective-permute-done.11.refs_10_), channel_id=1, source_target_pairs={{0,8},{2,10},{8,16},{10,18},{16,24},{18,26},{24,28},{26,30},{28,20... | collective-permute-start | bytes 1572872 | tf_op jit(solution)/shard_map/ppermute | solution.py:393
  50.0 21.0 %collective-permute-start.14 = (f32[2,4,128,128]{3,2,1,0:T(8,128)S(1)}, f32[2,4,128,128]{3,2,1,0:T(8,128)}, u32[]{:S(2)}, u32[]{:S(2)}) collective-permute-start(f32[2,4,128,128]{3,2,1,0:T(8,128)S(1)} %collective-permute-done.12.refs_13_), channel_id=1, source_target_pairs={{0,4},{2,6},{8,0},{10,2},{16,8},{18,10},{24,16},{26,18},{28,24},{3... | collective-permute-start | bytes 1572872 | tf_op jit(solution)/shard_map/ppermute | solution.py:393
  59.8 19.8 %collective-permute-start.6 = (f32[2,4,128,128]{3,2,1,0:T(8,128)}, f32[2,4,128,128]{3,2,1,0:T(8,128)}, u32[]{:S(2)}, u32[]{:S(2)}) collective-permute-start(f32[2,4,128,128]{3,2,1,0:T(8,128)} %collective-permute-done.4.token.refs_2_), channel_id=1, source_target_pairs={{0,8},{2,10},{8,16},{10,18},{16,24},{18,26},{24,28},{26,30},{28,20... | collective-permute-start | bytes 1572872 | tf_op jit(solution)/shard_map/ppermute | solution.py:393
  61.4 20.9 %collective-permute-start.7 = (f32[2,4,128,128]{3,2,1,0:T(8,128)}, f32[2,4,128,128]{3,2,1,0:T(8,128)}, u32[]{:S(2)}, u32[]{:S(2)}) collective-permute-start(f32[2,4,128,128]{3,2,1,0:T(8,128)} %collective-permute-done.5.refs_5_), channel_id=1, source_target_pairs={{0,4},{2,6},{8,0},{10,2},{16,8},{18,10},{24,16},{26,18},{28,24},{3... | collective-permute-start | bytes 1572872 | tf_op jit(solution)/shard_map/ppermute | solution.py:393
  71.0 21.3 %collective-permute-start.15 = (f32[2,4,128,128]{3,2,1,0:T(8,128)}, f32[2,4,128,128]{3,2,1,0:T(8,128)}, u32[]{:S(2)}, u32[]{:S(2)}) collective-permute-start(f32[2,4,128,128]{3,2,1,0:T(8,128)} %collective-permute-done.14.refs_14_), channel_id=1, source_target_pairs={{0,4},{2,6},{8,0},{10,2},{16,8},{18,10},{24,16},{26,18},{28,24},{3... | collective-permute-start | bytes 1572872 | tf_op jit(solution)/shard_map/ppermute | solution.py:393
  82.2 60.9 %copy-start.20 = (f32[1,128,128]{2,1,0:T(8,128)S(1)}, f32[1,128,128]{2,1,0:T(8,128)}, u32[]{:S(2)}) copy-start(f32[1,128,128]{2,1,0:T(8,128)} %get-tuple-element.78) | copy-start | bytes 196612
  82.3 11.9 %collective-permute-start.8 = (f32[2,4,128,128]{3,2,1,0:T(8,128)}, f32[2,4,128,128]{3,2,1,0:T(8,128)S(1)}, u32[]{:S(2)}, u32[]{:S(2)}) collective-permute-start(f32[2,4,128,128]{3,2,1,0:T(8,128)} %collective-permute-done.6.refs_3_), channel_id=1, source_target_pairs={{0,8},{2,10},{8,16},{10,18},{16,24},{18,26},{24,28},{26,30},{28,20... | collective-permute-start | bytes 1572872 | tf_op jit(solution)/shard_map/ppermute | solution.py:393
  92.4 2.6 %collective-permute-start.23 = (f32[2,4,128,128]{3,2,1,0:T(8,128)S(1)}, f32[2,4,128,128]{3,2,1,0:T(8,128)S(1)}, u32[]{:S(2)}, u32[]{:S(2)}) collective-permute-start(f32[2,4,128,128]{3,2,1,0:T(8,128)S(1)} %collective-permute-done.9.refs_9_), channel_id=1, source_target_pairs={{0,2},{2,0},{4,6},{6,4},{8,10},{10,8},{12,14},{14,12},{16,18},{18,... | collective-permute-start | bytes 1572872 | tf_op jit(solution)/shard_map/ppermute | solution.py:366
  92.4 2.9 %collective-permute-start.24 = (f32[2,4,128,128]{3,2,1,0:T(8,128)}, f32[2,4,128,128]{3,2,1,0:T(8,128)S(1)}, u32[]{:S(2)}, u32[]{:S(2)}) collective-permute-start(f32[2,4,128,128]{3,2,1,0:T(8,128)} %copy-done.3), channel_id=1, source_target_pairs={{0,2},{2,0},{4,6},{6,4},{8,10},{10,8},{12,14},{14,12},{16,18},{18,... | collective-permute-start | bytes 1572872 | tf_op jit(solution)/shard_map/ppermute | solution.py:366
  92.9 3.1 %collective-permute-start.25 = (f32[2,4,128,128]{3,2,1,0:T(8,128)}, f32[2,4,128,128]{3,2,1,0:T(8,128)S(1)}, u32[]{:S(2)}, u32[]{:S(2)}) collective-permute-start(f32[2,4,128,128]{3,2,1,0:T(8,128)} %collective-permute-done.13.refs_11_), channel_id=1, source_target_pairs={{0,2},{2,0},{4,6},{6,4},{8,10},{10,8},{12,14},{14,12},{16,18},{18,... | collective-permute-start | bytes 1572872 | tf_op jit(solution)/shard_map/ppermute | solution.py:366
  94.1 8.0 %copy-start.5 = (f32[2,4,128,128]{3,2,1,0:T(8,128)}, f32[2,4,128,128]{3,2,1,0:T(8,128)S(1)}, u32[]{:S(2)}) copy-start(f32[2,4,128,128]{3,2,1,0:T(8,128)S(1)} %collective-permute-done.8.refs_7_) | copy-start | bytes 1572868
  94.1 2.4 %collective-permute-start.26 = (f32[2,4,128,128]{3,2,1,0:T(8,128)S(1)}, f32[2,4,128,128]{3,2,1,0:T(8,128)S(1)}, u32[]{:S(2)}, u32[]{:S(2)}) collective-permute-start(f32[2,4,128,128]{3,2,1,0:T(8,128)S(1)} %collective-permute-done.10.refs_12_), channel_id=1, source_target_pairs={{0,2},{2,0},{4,6},{6,4},{8,10},{10,8},{12,14},{14,12},{16,18},{18,... | collective-permute-start | bytes 1572872 | tf_op jit(solution)/shard_map/ppermute | solution.py:366
  95.0 9.0 %copy-start.6 = (f32[2,4,128,128]{3,2,1,0:T(8,128)}, f32[2,4,128,128]{3,2,1,0:T(8,128)S(1)}, u32[]{:S(2)}) copy-start(f32[2,4,128,128]{3,2,1,0:T(8,128)S(1)} %collective-permute-done.23.refs_25_) | copy-start | bytes 1572868
  95.0 2.5 %collective-permute-start.27 = (f32[2,4,128,128]{3,2,1,0:T(8,128)}, f32[2,4,128,128]{3,2,1,0:T(8,128)S(1)}, u32[]{:S(2)}, u32[]{:S(2)}) collective-permute-start(f32[2,4,128,128]{3,2,1,0:T(8,128)} %copy-done.4), channel_id=1, source_target_pairs={{0,2},{2,0},{4,6},{6,4},{8,10},{10,8},{12,14},{14,12},{16,18},{18,... | collective-permute-start | bytes 1572872 | tf_op jit(solution)/shard_map/ppermute | solution.py:366
  95.2 8.8 %copy-start.7 = (f32[2,4,128,128]{3,2,1,0:T(8,128)}, f32[2,4,128,128]{3,2,1,0:T(8,128)S(1)}, u32[]{:S(2)}) copy-start(f32[2,4,128,128]{3,2,1,0:T(8,128)S(1)} %collective-permute-done.24.refs_26_) | copy-start | bytes 1572868
  95.2 3.0 %collective-permute-start.28 = (f32[2,4,128,128]{3,2,1,0:T(8,128)}, f32[2,4,128,128]{3,2,1,0:T(8,128)S(1)}, u32[]{:S(2)}, u32[]{:S(2)}) collective-permute-start(f32[2,4,128,128]{3,2,1,0:T(8,128)} %collective-permute-done.14.refs_14_), channel_id=1, source_target_pairs={{0,2},{2,0},{4,6},{6,4},{8,10},{10,8},{12,14},{14,12},{16,18},{18,... | collective-permute-start | bytes 1572872 | tf_op jit(solution)/shard_map/ppermute | solution.py:366
  96.0 8.0 %copy-start.8 = (f32[2,4,128,128]{3,2,1,0:T(8,128)}, f32[2,4,128,128]{3,2,1,0:T(8,128)S(1)}, u32[]{:S(2)}) copy-start(f32[2,4,128,128]{3,2,1,0:T(8,128)S(1)} %collective-permute-done.25.refs_27_) | copy-start | bytes 1572868
  96.0 3.0 %collective-permute-start.29 = (f32[2,4,128,128]{3,2,1,0:T(8,128)}, f32[2,4,128,128]{3,2,1,0:T(8,128)S(1)}, u32[]{:S(2)}, u32[]{:S(2)}) collective-permute-start(f32[2,4,128,128]{3,2,1,0:T(8,128)} %collective-permute-done.15.refs_15_), channel_id=1, source_target_pairs={{0,2},{2,0},{4,6},{6,4},{8,10},{10,8},{12,14},{14,12},{16,18},{18,... | collective-permute-start | bytes 1572872 | tf_op jit(solution)/shard_map/ppermute | solution.py:366
  96.5 7.5 %copy-start.9 = (f32[2,4,128,128]{3,2,1,0:T(8,128)}, f32[2,4,128,128]{3,2,1,0:T(8,128)S(1)}, u32[]{:S(2)}) copy-start(f32[2,4,128,128]{3,2,1,0:T(8,128)S(1)} %collective-permute-done.26.refs_28_) | copy-start | bytes 1572868
  96.5 3.2 %collective-permute-start.16 = (f32[2,4,128,128]{3,2,1,0:T(8,128)}, f32[2,4,128,128]{3,2,1,0:T(8,128)S(1)}, u32[]{:S(2)}, u32[]{:S(2)}) collective-permute-start(f32[2,4,128,128]{3,2,1,0:T(8,128)} %collective-permute-done.1.token.refs_1_), channel_id=1, source_target_pairs={{0,2},{2,0},{4,6},{6,4},{8,10},{10,8},{12,14},{14,12},{16,18},{18,... | collective-permute-start | bytes 1572872 | tf_op jit(solution)/shard_map/ppermute | solution.py:366
  97.5 9.0 %copy-start.10 = (f32[2,4,128,128]{3,2,1,0:T(8,128)}, f32[2,4,128,128]{3,2,1,0:T(8,128)S(1)}, u32[]{:S(2)}) copy-start(f32[2,4,128,128]{3,2,1,0:T(8,128)S(1)} %collective-permute-done.27.refs_29_) | copy-start | bytes 1572868
  97.5 3.0 %collective-permute-start.17 = (f32[2,4,128,128]{3,2,1,0:T(8,128)}, f32[2,4,128,128]{3,2,1,0:T(8,128)S(1)}, u32[]{:S(2)}, u32[]{:S(2)}) collective-permute-start(f32[2,4,128,128]{3,2,1,0:T(8,128)} %collective-permute-done.4.token.refs_2_), channel_id=1, source_target_pairs={{0,2},{2,0},{4,6},{6,4},{8,10},{10,8},{12,14},{14,12},{16,18},{18,... | collective-permute-start | bytes 1572872 | tf_op jit(solution)/shard_map/ppermute | solution.py:366
  98.2 5.8 %copy-start.11 = (f32[2,4,128,128]{3,2,1,0:T(8,128)}, f32[2,4,128,128]{3,2,1,0:T(8,128)S(1)}, u32[]{:S(2)}) copy-start(f32[2,4,128,128]{3,2,1,0:T(8,128)S(1)} %collective-permute-done.28.refs_30_) | copy-start | bytes 1572868
  98.2 3.7 %collective-permute-start.18 = (f32[2,4,128,128]{3,2,1,0:T(8,128)}, f32[2,4,128,128]{3,2,1,0:T(8,128)S(1)}, u32[]{:S(2)}, u32[]{:S(2)}) collective-permute-start(f32[2,4,128,128]{3,2,1,0:T(8,128)} %collective-permute-done.6.refs_3_), channel_id=1, source_target_pairs={{0,2},{2,0},{4,6},{6,4},{8,10},{10,8},{12,14},{14,12},{16,18},{18,... | collective-permute-start | bytes 1572872 | tf_op jit(solution)/shard_map/ppermute | solution.py:366
  99.0 5.1 %copy-start.12 = (f32[2,4,128,128]{3,2,1,0:T(8,128)}, f32[2,4,128,128]{3,2,1,0:T(8,128)S(1)}, u32[]{:S(2)}) copy-start(f32[2,4,128,128]{3,2,1,0:T(8,128)S(1)} %collective-permute-done.29.refs_31_) | copy-start | bytes 1572868
  99.0 3.1 %collective-permute-start.19 = (f32[2,4,128,128]{3,2,1,0:T(8,128)S(1)}, f32[2,4,128,128]{3,2,1,0:T(8,128)S(1)}, u32[]{:S(2)}, u32[]{:S(2)}) collective-permute-start(f32[2,4,128,128]{3,2,1,0:T(8,128)S(1)} %collective-permute-done.3.refs_4_), channel_id=1, source_target_pairs={{0,2},{2,0},{4,6},{6,4},{8,10},{10,8},{12,14},{14,12},{16,18},{18,... | collective-permute-start | bytes 1572872 | tf_op jit(solution)/shard_map/ppermute | solution.py:366
  99.7 6.7 %copy-start.13 = (f32[2,4,128,128]{3,2,1,0:T(8,128)}, f32[2,4,128,128]{3,2,1,0:T(8,128)S(1)}, u32[]{:S(2)}) copy-start(f32[2,4,128,128]{3,2,1,0:T(8,128)S(1)} %collective-permute-done.16.refs_17_) | copy-start | bytes 1572868
  99.7 3.0 %collective-permute-start.20 = (f32[2,4,128,128]{3,2,1,0:T(8,128)}, f32[2,4,128,128]{3,2,1,0:T(8,128)S(1)}, u32[]{:S(2)}, u32[]{:S(2)}) collective-permute-start(f32[2,4,128,128]{3,2,1,0:T(8,128)} %collective-permute-done.5.refs_5_), channel_id=1, source_target_pairs={{0,2},{2,0},{4,6},{6,4},{8,10},{10,8},{12,14},{14,12},{16,18},{18,... | collective-permute-start | bytes 1572872 | tf_op jit(solution)/shard_map/ppermute | solution.py:366
  100.5 3.6 %copy-start.14 = (f32[2,4,128,128]{3,2,1,0:T(8,128)}, f32[2,4,128,128]{3,2,1,0:T(8,128)S(1)}, u32[]{:S(2)}) copy-start(f32[2,4,128,128]{3,2,1,0:T(8,128)S(1)} %collective-permute-done.17.refs_18_) | copy-start | bytes 1572868
  100.5 3.0 %collective-permute-start.21 = (f32[2,4,128,128]{3,2,1,0:T(8,128)}, f32[2,4,128,128]{3,2,1,0:T(8,128)S(1)}, u32[]{:S(2)}, u32[]{:S(2)}) collective-permute-start(f32[2,4,128,128]{3,2,1,0:T(8,128)} %collective-permute-done.7.refs_6_), channel_id=1, source_target_pairs={{0,2},{2,0},{4,6},{6,4},{8,10},{10,8},{12,14},{14,12},{16,18},{18,... | collective-permute-start | bytes 1572872 | tf_op jit(solution)/shard_map/ppermute | solution.py:366
  102.0 2.1 %copy-start.15 = (f32[2,4,128,128]{3,2,1,0:T(8,128)}, f32[2,4,128,128]{3,2,1,0:T(8,128)S(1)}, u32[]{:S(2)}) copy-start(f32[2,4,128,128]{3,2,1,0:T(8,128)S(1)} %collective-permute-done.18.refs_19_) | copy-start | bytes 1572868
  102.0 2.0 %collective-permute-start.22 = (f32[2,4,128,128]{3,2,1,0:T(8,128)S(1)}, f32[2,4,128,128]{3,2,1,0:T(8,128)S(1)}, u32[]{:S(2)}, u32[]{:S(2)}) collective-permute-start(f32[2,4,128,128]{3,2,1,0:T(8,128)S(1)} %collective-permute-done.8.refs_7_), channel_id=1, source_target_pairs={{0,2},{2,0},{4,6},{6,4},{8,10},{10,8},{12,14},{14,12},{16,18},{18,... | collective-permute-start | bytes 1572872 | tf_op jit(solution)/shard_map/ppermute | solution.py:366
  102.1 2.0 %copy-start.16 = (f32[2,4,128,128]{3,2,1,0:T(8,128)}, f32[2,4,128,128]{3,2,1,0:T(8,128)S(1)}, u32[]{:S(2)}) copy-start(f32[2,4,128,128]{3,2,1,0:T(8,128)S(1)} %collective-permute-done.19.refs_20_) | copy-start | bytes 1572868
  102.7 1.4 copy-start.17
  103.5 0.8 copy-start.18
  104.3 0.8 copy-start.19
  123.4 2.4 %collective-permute-start.30 = (f32[8,128,128]{2,1,0:T(8,128)}, f32[8,128,128]{2,1,0:T(8,128)S(1)}, u32[]{:S(2)}, u32[]{:S(2)}) collective-permute-start(f32[8,128,128]{2,1,0:T(8,128)} %get-tuple-element.80), channel_id=1, source_target_pairs={{0,2},{2,0},{4,6},{6,4},{8,10},{10,8},{12,14},{14,12},{16,18},{18,... | collective-permute-start | bytes 1572872 | tf_op jit(solution)/shard_map/ppermute | solution.py:366
  127.0 8.5 %collective-permute-start.31 = (f32[1,128,128]{2,1,0:T(8,128)S(1)}, f32[1,128,128]{2,1,0:T(8,128)S(1)}, u32[]{:S(2)}, u32[]{:S(2)}) collective-permute-start(f32[1,128,128]{2,1,0:T(8,128)S(1)} %get-tuple-element.84), channel_id=1, source_target_pairs={{0,4},{2,6},{4,0},{6,2},{8,12},{10,14},{12,8},{14,10},{16,20},{18,... | collective-permute-start | bytes 196616 | tf_op jit(solution)/shard_map/ppermute | solution.py:418
  127.1 9.1 %collective-permute-start.34 = (f32[1,128,128]{2,1,0:T(8,128)S(1)}, f32[1,128,128]{2,1,0:T(8,128)S(1)}, u32[]{:S(2)}, u32[]{:S(2)}) collective-permute-start(f32[1,128,128]{2,1,0:T(8,128)S(1)} %get-tuple-element.85), channel_id=1, source_target_pairs={{0,28},{2,30},{4,24},{6,26},{8,4},{10,6},{12,0},{14,2},{16,12},{18... | collective-permute-start | bytes 196616 | tf_op jit(solution)/shard_map/ppermute | solution.py:418
  131.0 10.1 %collective-permute-start.33 = (f32[1,128,128]{2,1,0:T(8,128)S(1)}, f32[1,128,128]{2,1,0:T(8,128)S(1)}, u32[]{:S(2)}, u32[]{:S(2)}) collective-permute-start(f32[1,128,128]{2,1,0:T(8,128)S(1)} %get-tuple-element.86), channel_id=1, source_target_pairs={{0,20},{2,22},{4,16},{6,18},{8,28},{10,30},{12,24},{14,26},{16,4},... | collective-permute-start | bytes 196616 | tf_op jit(solution)/shard_map/ppermute | solution.py:418
  131.0 10.1 %collective-permute-start.32 = (f32[1,128,128]{2,1,0:T(8,128)S(1)}, f32[1,128,128]{2,1,0:T(8,128)S(1)}, u32[]{:S(2)}, u32[]{:S(2)}) collective-permute-start(f32[1,128,128]{2,1,0:T(8,128)S(1)} %get-tuple-element.87), channel_id=1, source_target_pairs={{0,12},{2,14},{4,8},{6,10},{8,20},{10,22},{12,16},{14,18},{16,28},... | collective-permute-start | bytes 196616 | tf_op jit(solution)/shard_map/ppermute | solution.py:418
  132.3 8.9 %collective-permute-start.35 = (f32[1,128,128]{2,1,0:T(8,128)S(1)}, f32[1,128,128]{2,1,0:T(8,128)S(1)}, u32[]{:S(2)}, u32[]{:S(2)}) collective-permute-start(f32[1,128,128]{2,1,0:T(8,128)S(1)} %get-tuple-element.88), channel_id=1, source_target_pairs={{0,8},{2,10},{4,12},{6,14},{8,16},{10,18},{12,20},{14,22},{16,24},... | collective-permute-start | bytes 196616 | tf_op jit(solution)/shard_map/ppermute | solution.py:418
  135.5 5.7 %collective-permute-start.37 = (f32[1,128,128]{2,1,0:T(8,128)S(1)}, f32[1,128,128]{2,1,0:T(8,128)S(1)}, u32[]{:S(2)}, u32[]{:S(2)}) collective-permute-start(f32[1,128,128]{2,1,0:T(8,128)S(1)} %get-tuple-element.89), channel_id=1, source_target_pairs={{0,24},{2,26},{4,28},{6,30},{8,0},{10,2},{12,4},{14,6},{16,8},{18,... | collective-permute-start | bytes 196616 | tf_op jit(solution)/shard_map/ppermute | solution.py:418
  136.2 7.0 %collective-permute-start.36 = (f32[1,128,128]{2,1,0:T(8,128)S(1)}, f32[1,128,128]{2,1,0:T(8,128)S(1)}, u32[]{:S(2)}, u32[]{:S(2)}) collective-permute-start(f32[1,128,128]{2,1,0:T(8,128)S(1)} %get-tuple-element.90), channel_id=1, source_target_pairs={{0,16},{2,18},{4,20},{6,22},{8,24},{10,26},{12,28},{14,30},{16,0},... | collective-permute-start | bytes 196616 | tf_op jit(solution)/shard_map/ppermute | solution.py:418

commit v4 on v3

--- a/solution.py
+++ b/solution.py
@@ -411,7 +411,7 @@
     got = swapped(theirs)
     here, there = mine + got[:zs], across + got[zs:]
     z_diag = square + here[:1]
-    routes = [(m, flip) for flip in (1, 0) for m in range(zs) if m + flip > 0]
+    routes = sorted(((m, flip) for flip in (1, 0) for m in range(zs) if m + flip > 0), key=lambda r: min(r[0], zs - r[0]))
     for m, flip in routes:
         links = [(r, ((r + 4 * m) % n_row) ^ (2 * flip)) for r in range(n_row)]
         source = there if flip else here

time: 145 us -> 143 us (0.986)
  starting transfers between devices: 29.9 us -> 33.4 us
  waiting for transfers between devices: 74.1 us -> 71.1 us
  Pallas kernels: 34.7 us -> 32.8 us
    ppermute x7, starting transfers between devices: 10 us -> 14.2 us  [body(): z_diag = z_diag + permute(source[m:m + 1], 'row', links)]
    ppermute x7, waiting for transfers between devices: 6.15 us -> 2.8 us  [body(): z_diag = z_diag + permute(source[m:m + 1], 'row', links)]
    pallas_call x1, Pallas kernels: 16.9 us -> 15.1 us  [all_sums(): pl.pallas_call(functools.partial(sums_kernel, (rows, zs, chip_of, sets, h...]
where the time goes in v4:
time: 143 us
  waiting for transfers between devices  71.1 us (50%)
  starting transfers between devices  33.4 us (23%)
  Pallas kernels  32.8 us (23%)
  other arithmetic  2.38 us (2%)
  local copies, waits for them, and re-layouts  2.04 us (1%)
    ppermute x14, waiting for transfers between devices, body(): permute(front[0 if way > 0 else 1], 'row', pairs(way))  56.5 us
    pallas_call x1, Pallas kernels, all_sums(): pl.pallas_call(functools.partial(sums_kernel, (rows, zs, chip_of, sets, h...  15.1 us
    ppermute x7, starting transfers between devices, body(): z_diag = z_diag + permute(source[m:m + 1], 'row', links)  14.2 us
    ppermute x14, starting transfers between devices, body(): permute(front[0 if way > 0 else 1], 'row', pairs(way))  14 us
    pallas_call x4, Pallas kernels, u_blocks(): pl.pallas_call(functools.partial(u_kernel, chips, other), out_shape=[jax....  13.3 us
    ppermute x16, waiting for transfers between devices, swapped(): return permute(array, 'row', swap_core)  10.4 us
    pallas_call x1, Pallas kernels, make_plan(): pl.pallas_call(functools.partial(plan_kernel, dims, plan), out_shape=jax....  4.42 us
  transfers between devices with their start and end apart: 38, of which 31 were waited for; matrix products, arithmetic and copies ran while one was open for 0% of the time, Pallas kernels for 12%

profile of v4, /device:TPU:0, one launch (start us, length us, event | category | flops | bytes accessed | tf_op | source)
XLA Modules:
  0.0 142.6 jit_solution(7776867413902991876)
XLA Ops:
  0.6 0.5 collective-permute-start
  1.1 2.6 %collective-permute-start.2 = (f32[3,24,128,128]{3,2,1,0:T(8,128)}, f32[3,24,128,128]{3,2,1,0:T(8,128)}, u32[]{:S(2)}, u32[]{:S(2)}) collective-permute-start(f32[3,24,128,128]{3,2,1,0:T(8,128)} %near.1), channel_id=1, source_target_pairs={{1,0},{0,1},{3,2},{2,3},{5,4},{4,5},{7,6},{6,7},{9,8},{8,9},{11,10... | collective-permute-start | bytes 14155784 | tf_op jit(solution)/shard_map/ppermute | solution.py:372
  3.7 0.6 pad_add_fusion.where
  4.4 1.0 copy-done.21
  5.3 3.3 %u_blocks.7 = (f32[2,4,128,128]{3,2,1,0:T(8,128)}, f32[1,128,128]{2,1,0:T(8,128)}) custom-call(s32[2]{0:T(128)} %pad_add_fusion.where, f32[16,128,128]{2,1,0:T(8,128)} %bitcast.4, f32[16,128,128]{2,1,0:T(8,128)} %copy-done.21, f32[16,128,128]{2,1,0:T(8,128)} %inverse.7, s32[16,16]{1,0:T(8,128)} %token_.3), custom_call_target="tpu_custom_call" | custom-call | flops 1000000000 | bytes 1000 | tf_op jit(solution)/shard_map/u_blocks/pallas_call | solution.py:158
  8.7 2.3 %collective-permute-start.9 = (f32[2,4,128,128]{3,2,1,0:T(8,128)}, f32[2,4,128,128]{3,2,1,0:T(8,128)S(1)}, u32[]{:S(2)}, u32[]{:S(2)}) collective-permute-start(f32[2,4,128,128]{3,2,1,0:T(8,128)} %get-tuple-element.57.refs_8_), channel_id=1, source_target_pairs={{0,8},{2,10},{8,16},{10,18},{16,24},{18,26},{24,28},{26,30},{28,20... | collective-permute-start | bytes 1572872 | tf_op jit(solution)/shard_map/ppermute | solution.py:393
  10.9 3.3 %u_blocks.4 = (f32[2,4,128,128]{3,2,1,0:T(8,128)}, f32[1,128,128]{2,1,0:T(8,128)}) custom-call(s32[2]{0:T(128)} %pad_add_fusion.where, f32[16,128,128]{2,1,0:T(8,128)} %bitcast.5, f32[16,128,128]{2,1,0:T(8,128)} %copy-done.21, f32[16,128,128]{2,1,0:T(8,128)} %inverse.7, s32[16,16]{1,0:T(8,128)} %token_.3), custom_call_target="tpu_custom_call" | custom-call | flops 1000000000 | bytes 1000 | tf_op jit(solution)/shard_map/u_blocks/pallas_call | solution.py:158
  14.3 2.1 %collective-permute-start.1 = (f32[2,4,128,128]{3,2,1,0:T(8,128)}, f32[2,4,128,128]{3,2,1,0:T(8,128)}, u32[]{:S(2)}, u32[]{:S(2)}) collective-permute-start(f32[2,4,128,128]{3,2,1,0:T(8,128)} %get-tuple-element.44.refs_0_), channel_id=1, source_target_pairs={{0,8},{2,10},{8,16},{10,18},{16,24},{18,26},{24,28},{26,30},{28,20... | collective-permute-start | bytes 1572872 | tf_op jit(solution)/shard_map/ppermute | solution.py:393
  16.4 7.4 %collective-permute-done.9.refs_9_ = f32[2,4,128,128]{3,2,1,0:T(8,128)S(1)} collective-permute-done((f32[2,4,128,128]{3,2,1,0:T(8,128)}, f32[2,4,128,128]{3,2,1,0:T(8,128)S(1)}, u32[]{:S(2)}, u32[]{:S(2)}) %collective-permute-start.9) | collective-permute-done | bytes 524320 | tf_op jit(solution)/shard_map/ppermute | solution.py:393
  23.8 2.2 %collective-permute-done.10.refs_12_ = f32[2,4,128,128]{3,2,1,0:T(8,128)S(1)} collective-permute-done((f32[2,4,128,128]{3,2,1,0:T(8,128)}, f32[2,4,128,128]{3,2,1,0:T(8,128)S(1)}, u32[]{:S(2)}, u32[]{:S(2)}) %collective-permute-start.10) | collective-permute-done | bytes 524320 | tf_op jit(solution)/shard_map/ppermute | solution.py:393
  26.0 1.6 %collective-permute-start.11 = (f32[2,4,128,128]{3,2,1,0:T(8,128)S(1)}, f32[2,4,128,128]{3,2,1,0:T(8,128)S(1)}, u32[]{:S(2)}, u32[]{:S(2)}) collective-permute-start(f32[2,4,128,128]{3,2,1,0:T(8,128)S(1)} %collective-permute-done.9.refs_9_), channel_id=1, source_target_pairs={{0,8},{2,10},{8,16},{10,18},{16,24},{18,26},{24,28},{26,30},{28,20... | collective-permute-start | bytes 1572872 | tf_op jit(solution)/shard_map/ppermute | solution.py:393
  27.5 0.5 collective-permute-start.12
  28.0 7.1 %collective-permute-done.1.token.refs_1_ = f32[2,4,128,128]{3,2,1,0:T(8,128)} collective-permute-done((f32[2,4,128,128]{3,2,1,0:T(8,128)}, f32[2,4,128,128]{3,2,1,0:T(8,128)}, u32[]{:S(2)}, u32[]{:S(2)}) %collective-permute-start.1) | collective-permute-done | bytes 524320 | tf_op jit(solution)/shard_map/ppermute | solution.py:393
  35.1 2.1 %collective-permute-done.3.refs_4_ = f32[2,4,128,128]{3,2,1,0:T(8,128)S(1)} collective-permute-done((f32[2,4,128,128]{3,2,1,0:T(8,128)}, f32[2,4,128,128]{3,2,1,0:T(8,128)S(1)}, u32[]{:S(2)}, u32[]{:S(2)}) %collective-permute-start.3) | collective-permute-done | bytes 524320 | tf_op jit(solution)/shard_map/ppermute | solution.py:393
  37.2 1.6 %collective-permute-start.4 = (f32[2,4,128,128]{3,2,1,0:T(8,128)}, f32[2,4,128,128]{3,2,1,0:T(8,128)}, u32[]{:S(2)}, u32[]{:S(2)}) collective-permute-start(f32[2,4,128,128]{3,2,1,0:T(8,128)} %collective-permute-done.1.token.refs_1_), channel_id=1, source_target_pairs={{0,8},{2,10},{8,16},{10,18},{16,24},{18,26},{24,28},{26,30},{28,20... | collective-permute-start | bytes 1572872 | tf_op jit(solution)/shard_map/ppermute | solution.py:393
  38.8 0.5 collective-permute-start.5
  39.2 7.0 %collective-permute-done.11.refs_10_ = f32[2,4,128,128]{3,2,1,0:T(8,128)S(1)} collective-permute-done((f32[2,4,128,128]{3,2,1,0:T(8,128)S(1)}, f32[2,4,128,128]{3,2,1,0:T(8,128)S(1)}, u32[]{:S(2)}, u32[]{:S(2)}) %collective-permute-start.11) | collective-permute-done | bytes 524320 | tf_op jit(solution)/shard_map/ppermute | solution.py:393
  46.2 2.2 %collective-permute-done.12.refs_13_ = f32[2,4,128,128]{3,2,1,0:T(8,128)S(1)} collective-permute-done((f32[2,4,128,128]{3,2,1,0:T(8,128)S(1)}, f32[2,4,128,128]{3,2,1,0:T(8,128)S(1)}, u32[]{:S(2)}, u32[]{:S(2)}) %collective-permute-start.12) | collective-permute-done | bytes 524320 | tf_op jit(solution)/shard_map/ppermute | solution.py:393
  48.4 1.6 %collective-permute-start.13 = (f32[2,4,128,128]{3,2,1,0:T(8,128)S(1)}, f32[2,4,128,128]{3,2,1,0:T(8,128)}, u32[]{:S(2)}, u32[]{:S(2)}) collective-permute-start(f32[2,4,128,128]{3,2,1,0:T(8,128)S(1)} %collective-permute-done.11.refs_10_), channel_id=1, source_target_pairs={{0,8},{2,10},{8,16},{10,18},{16,24},{18,26},{24,28},{26,30},{28,20... | collective-permute-start | bytes 1572872 | tf_op jit(solution)/shard_map/ppermute | solution.py:393
  50.0 0.5 collective-permute-start.14
  50.5 4.4 %plan.1.tables = s32[371]{0:T(512)} custom-call(s32[2]{0:T(128)} %pad_add_fusion.where, s32[256]{0:T(256)} %constant.12.clone.table, s32[8]{0:T(128)} %constant.13.clone.chip_of, s32[16,16]{1,0:T(8,128)} %token_.3, f32[2,4,128,128]{3,2,1,0:T(8,128)} %collective-permute-done.1.token.refs_1_), custom_call_target="tpu_custom_call" | custom-call | flops 1000000000 | bytes 1000 | tf_op jit(solution)/shard_map/plan/pallas_call | solution.py:109
  54.9 2.7 %collective-permute-done.4.token.refs_2_ = f32[2,4,128,128]{3,2,1,0:T(8,128)} collective-permute-done((f32[2,4,128,128]{3,2,1,0:T(8,128)}, f32[2,4,128,128]{3,2,1,0:T(8,128)}, u32[]{:S(2)}, u32[]{:S(2)}) %collective-permute-start.4) | collective-permute-done | bytes 524320 | tf_op jit(solution)/shard_map/ppermute | solution.py:393
  57.6 2.2 %collective-permute-done.5.refs_5_ = f32[2,4,128,128]{3,2,1,0:T(8,128)} collective-permute-done((f32[2,4,128,128]{3,2,1,0:T(8,128)S(1)}, f32[2,4,128,128]{3,2,1,0:T(8,128)}, u32[]{:S(2)}, u32[]{:S(2)}) %collective-permute-start.5) | collective-permute-done | bytes 524320 | tf_op jit(solution)/shard_map/ppermute | solution.py:393
  59.8 1.6 %collective-permute-start.6 = (f32[2,4,128,128]{3,2,1,0:T(8,128)}, f32[2,4,128,128]{3,2,1,0:T(8,128)}, u32[]{:S(2)}, u32[]{:S(2)}) collective-permute-start(f32[2,4,128,128]{3,2,1,0:T(8,128)} %collective-permute-done.4.token.refs_2_), channel_id=1, source_target_pairs={{0,8},{2,10},{8,16},{10,18},{16,24},{18,26},{24,28},{26,30},{28,20... | collective-permute-start | bytes 1572872 | tf_op jit(solution)/shard_map/ppermute | solution.py:393
  61.4 0.5 collective-permute-start.7
  61.8 7.0 %collective-permute-done.13.refs_11_ = f32[2,4,128,128]{3,2,1,0:T(8,128)} collective-permute-done((f32[2,4,128,128]{3,2,1,0:T(8,128)S(1)}, f32[2,4,128,128]{3,2,1,0:T(8,128)}, u32[]{:S(2)}, u32[]{:S(2)}) %collective-permute-start.13) | collective-permute-done | bytes 524320 | tf_op jit(solution)/shard_map/ppermute | solution.py:393
  68.8 2.2 %collective-permute-done.14.refs_14_ = f32[2,4,128,128]{3,2,1,0:T(8,128)} collective-permute-done((f32[2,4,128,128]{3,2,1,0:T(8,128)S(1)}, f32[2,4,128,128]{3,2,1,0:T(8,128)}, u32[]{:S(2)}, u32[]{:S(2)}) %collective-permute-start.14) | collective-permute-done | bytes 524320 | tf_op jit(solution)/shard_map/ppermute | solution.py:393
  71.0 3.3 %u_blocks.6 = (f32[2,4,128,128]{3,2,1,0:T(8,128)}, f32[1,128,128]{2,1,0:T(8,128)}) custom-call(s32[2]{0:T(128)} %pad_add_fusion.where, f32[16,128,128]{2,1,0:T(8,128)} %bitcast.6, f32[16,128,128]{2,1,0:T(8,128)} %copy-done.21, f32[16,128,128]{2,1,0:T(8,128)} %inverse.7, f32[2,4,128,128]{3,2,1,0:T(8,128)} %collective-permute-done.4.token.refs_2_), custom_call_target="tpu_custom_call" | custom-call | flops 1000000000 | bytes 1000 | tf_op jit(solution)/shard_map/u_blocks/pallas_call | solution.py:158
  74.4 3.3 %u_blocks.5 = (f32[2,4,128,128]{3,2,1,0:T(8,128)}, f32[1,128,128]{2,1,0:T(8,128)}) custom-call(s32[2]{0:T(128)} %pad_add_fusion.where, f32[16,128,128]{2,1,0:T(8,128)} %bitcast.7, f32[16,128,128]{2,1,0:T(8,128)} %copy-done.21, f32[16,128,128]{2,1,0:T(8,128)} %inverse.7, f32[2,4,128,128]{3,2,1,0:T(8,128)} %collective-permute-done.4.token.refs_2_), custom_call_target="tpu_custom_call" | custom-call | flops 1000000000 | bytes 1000 | tf_op jit(solution)/shard_map/u_blocks/pallas_call | solution.py:158
  77.7 1.9 %collective-permute-done.6.refs_3_ = f32[2,4,128,128]{3,2,1,0:T(8,128)} collective-permute-done((f32[2,4,128,128]{3,2,1,0:T(8,128)}, f32[2,4,128,128]{3,2,1,0:T(8,128)}, u32[]{:S(2)}, u32[]{:S(2)}) %collective-permute-start.6) | collective-permute-done | bytes 524320 | tf_op jit(solution)/shard_map/ppermute | solution.py:393
  79.6 2.7 %collective-permute-done.7.refs_6_ = f32[2,4,128,128]{3,2,1,0:T(8,128)} collective-permute-done((f32[2,4,128,128]{3,2,1,0:T(8,128)}, f32[2,4,128,128]{3,2,1,0:T(8,128)}, u32[]{:S(2)}, u32[]{:S(2)}) %collective-permute-start.7) | collective-permute-done | bytes 524320 | tf_op jit(solution)/shard_map/ppermute | solution.py:393
  82.3 1.6 %collective-permute-start.8 = (f32[2,4,128,128]{3,2,1,0:T(8,128)}, f32[2,4,128,128]{3,2,1,0:T(8,128)S(1)}, u32[]{:S(2)}, u32[]{:S(2)}) collective-permute-start(f32[2,4,128,128]{3,2,1,0:T(8,128)} %collective-permute-done.6.refs_3_), channel_id=1, source_target_pairs={{0,8},{2,10},{8,16},{10,18},{16,24},{18,26},{24,28},{26,30},{28,20... | collective-permute-start | bytes 1572872 | tf_op jit(solution)/shard_map/ppermute | solution.py:393
  83.8 8.5 %collective-permute-done.15.refs_15_ = f32[2,4,128,128]{3,2,1,0:T(8,128)} collective-permute-done((f32[2,4,128,128]{3,2,1,0:T(8,128)}, f32[2,4,128,128]{3,2,1,0:T(8,128)}, u32[]{:S(2)}, u32[]{:S(2)}) %collective-permute-start.15) | collective-permute-done | bytes 524320 | tf_op jit(solution)/shard_map/ppermute | solution.py:393
  92.4 0.5 collective-permute-start.24
  92.9 1.3 collective-permute-done.8.refs_7_
  94.2 0.8 collective-permute-done.23.refs_25_
  95.2 0.3 collective-permute-start.28
  95.5 0.5 collective-permute-done.25.refs_27_
  96.1 0.4 collective-permute-done.26.refs_28_
  96.7 0.8 collective-permute-done.27.refs_29_
  97.6 0.6 collective-permute-done.28.refs_30_
  98.4 0.6 collective-permute-done.29.refs_31_
  99.1 0.6 collective-permute-done.16.refs_17_
  99.9 0.6 collective-permute-done.17.refs_18_
  100.6 1.4 collective-permute-done.18.refs_19_
  102.1 0.6 collective-permute-done.20.refs_21_
  102.7 0.7 collective-permute-done.21.refs_22_
  103.5 0.5 collective-permute-done.22.refs_23_
  104.1 0.2 copy-done.18
  104.3 0.8 copy-done.19
  105.1 1.4 collective-permute-done.2.far
  106.5 15.1 %all_sums.1 = (f32[16,3,128,128]{3,2,1,0:T(8,128)}, f32[4,128,128]{2,1,0:T(8,128)}, f32[4,128,128]{2,1,0:T(8,128)}, f32[8,128,128]{2,1,0:T(8,128)}) custom-call(s32[2]{0:T(128)} %pad_add_fusion.where, s32[371]{0:T(512)} %plan.1.tables, f32[3,24,128,128]{3,2,1,0:T(8,128)} %near.1, f32[3,24,128,128]{3,2,1,0:T(8,128)} %collective-permute-done.2.far, ...), custom_call_target="tpu_custom_call" | custom-call | flops 3000000000 | bytes 1000 | tf_op jit(solution)/shard_map/all_sums/pallas_call | solution.py:311
  121.7 2.1 %collective-permute-done.30 = f32[8,128,128]{2,1,0:T(8,128)S(1)} collective-permute-done((f32[8,128,128]{2,1,0:T(8,128)}, f32[8,128,128]{2,1,0:T(8,128)S(1)}, u32[]{:S(2)}, u32[]{:S(2)}) %collective-permute-start.30) | collective-permute-done | bytes 524320 | tf_op jit(solution)/shard_map/ppermute | solution.py:366
  123.8 1.1 slice_add_fusion
  124.9 3.0 %collective-permute-start.31 = (f32[1,128,128]{2,1,0:T(8,128)S(1)}, f32[1,128,128]{2,1,0:T(8,128)S(1)}, u32[]{:S(2)}, u32[]{:S(2)}) collective-permute-start(f32[1,128,128]{2,1,0:T(8,128)S(1)} %get-tuple-element.84), channel_id=1, source_target_pairs={{0,4},{2,6},{4,0},{6,2},{8,12},{10,14},{12,8},{14,10},{16,20},{18,... | collective-permute-start | bytes 196616 | tf_op jit(solution)/shard_map/ppermute | solution.py:418
  127.9 1.5 %collective-permute-start.36 = (f32[1,128,128]{2,1,0:T(8,128)S(1)}, f32[1,128,128]{2,1,0:T(8,128)S(1)}, u32[]{:S(2)}, u32[]{:S(2)}) collective-permute-start(f32[1,128,128]{2,1,0:T(8,128)S(1)} %get-tuple-element.85), channel_id=1, source_target_pairs={{0,20},{2,22},{4,16},{6,18},{8,28},{10,30},{12,24},{14,26},{16,4},... | collective-permute-start | bytes 196616 | tf_op jit(solution)/shard_map/ppermute | solution.py:418
  129.4 1.6 %collective-permute-start.33 = (f32[1,128,128]{2,1,0:T(8,128)S(1)}, f32[1,128,128]{2,1,0:T(8,128)S(1)}, u32[]{:S(2)}, u32[]{:S(2)}) collective-permute-start(f32[1,128,128]{2,1,0:T(8,128)S(1)} %get-tuple-element.86), channel_id=1, source_target_pairs={{0,28},{2,30},{4,24},{6,26},{8,4},{10,6},{12,0},{14,2},{16,12},{18... | collective-permute-start | bytes 196616 | tf_op jit(solution)/shard_map/ppermute | solution.py:418
  131.0 1.3 collective-permute-start.32
  132.3 2.2 %collective-permute-start.34 = (f32[1,128,128]{2,1,0:T(8,128)S(1)}, f32[1,128,128]{2,1,0:T(8,128)S(1)}, u32[]{:S(2)}, u32[]{:S(2)}) collective-permute-start(f32[1,128,128]{2,1,0:T(8,128)S(1)} %get-tuple-element.88), channel_id=1, source_target_pairs={{0,8},{2,10},{4,12},{6,14},{8,16},{10,18},{12,20},{14,22},{16,24},... | collective-permute-start | bytes 196616 | tf_op jit(solution)/shard_map/ppermute | solution.py:418
  134.6 2.1 %collective-permute-start.37 = (f32[1,128,128]{2,1,0:T(8,128)S(1)}, f32[1,128,128]{2,1,0:T(8,128)S(1)}, u32[]{:S(2)}, u32[]{:S(2)}) collective-permute-start(f32[1,128,128]{2,1,0:T(8,128)S(1)} %get-tuple-element.89), channel_id=1, source_target_pairs={{0,16},{2,18},{4,20},{6,22},{8,24},{10,26},{12,28},{14,30},{16,0},... | collective-permute-start | bytes 196616 | tf_op jit(solution)/shard_map/ppermute | solution.py:418
  136.7 2.4 %collective-permute-start.35 = (f32[1,128,128]{2,1,0:T(8,128)S(1)}, f32[1,128,128]{2,1,0:T(8,128)S(1)}, u32[]{:S(2)}, u32[]{:S(2)}) collective-permute-start(f32[1,128,128]{2,1,0:T(8,128)S(1)} %get-tuple-element.90), channel_id=1, source_target_pairs={{0,24},{2,26},{4,28},{6,30},{8,0},{10,2},{12,4},{14,6},{16,8},{18,... | collective-permute-start | bytes 196616 | tf_op jit(solution)/shard_map/ppermute | solution.py:418
  139.1 1.1 collective-permute-done.34
  140.2 1.6 %collective-permute-done.37 = f32[1,128,128]{2,1,0:T(8,128)S(1)} collective-permute-done((f32[1,128,128]{2,1,0:T(8,128)S(1)}, f32[1,128,128]{2,1,0:T(8,128)S(1)}, u32[]{:S(2)}, u32[]{:S(2)}) %collective-permute-start.37) | collective-permute-done | bytes 65568 | tf_op jit(solution)/shard_map/ppermute | solution.py:418
  141.9 0.7 fusion.6
  (67 shorter events, 1.6 us)
Async XLA Ops:
  0.6 3.7 %collective-permute-start = (f32[16,128,128]{2,1,0:T(8,128)}, f32[16,128,128]{2,1,0:T(8,128)S(1)}, u32[]{:S(2)}, u32[]{:S(2)}) collective-permute-start(f32[16,128,128]{2,1,0:T(8,128)} %bitcast.3), channel_id=1, source_target_pairs={{0,2},{2,0},{4,6},{6,4},{8,10},{10,8},{12,14},{14,12},{16,18},{18,... | collective-permute-start | bytes 3145736 | tf_op jit(solution)/shard_map/ppermute | solution.py:366
  1.1 105.3 %collective-permute-start.2 = (f32[3,24,128,128]{3,2,1,0:T(8,128)}, f32[3,24,128,128]{3,2,1,0:T(8,128)}, u32[]{:S(2)}, u32[]{:S(2)}) collective-permute-start(f32[3,24,128,128]{3,2,1,0:T(8,128)} %near.1), channel_id=1, source_target_pairs={{1,0},{0,1},{3,2},{2,3},{5,4},{4,5},{7,6},{6,7},{9,8},{8,9},{11,10... | collective-permute-start | bytes 14155784 | tf_op jit(solution)/shard_map/ppermute | solution.py:372
  4.4 1.0 copy-start.21
  8.7 15.1 %collective-permute-start.9 = (f32[2,4,128,128]{3,2,1,0:T(8,128)}, f32[2,4,128,128]{3,2,1,0:T(8,128)S(1)}, u32[]{:S(2)}, u32[]{:S(2)}) collective-permute-start(f32[2,4,128,128]{3,2,1,0:T(8,128)} %get-tuple-element.57.refs_8_), channel_id=1, source_target_pairs={{0,8},{2,10},{8,16},{10,18},{16,24},{18,26},{24,28},{26,30},{28,20... | collective-permute-start | bytes 1572872 | tf_op jit(solution)/shard_map/ppermute | solution.py:393
  10.9 15.0 %collective-permute-start.10 = (f32[2,4,128,128]{3,2,1,0:T(8,128)}, f32[2,4,128,128]{3,2,1,0:T(8,128)S(1)}, u32[]{:S(2)}, u32[]{:S(2)}) collective-permute-start(f32[2,4,128,128]{3,2,1,0:T(8,128)} %get-tuple-element.57.refs_8_), channel_id=1, source_target_pairs={{0,4},{2,6},{8,0},{10,2},{16,8},{18,10},{24,16},{26,18},{28,24},{3... | collective-permute-start | bytes 1572872 | tf_op jit(solution)/shard_map/ppermute | solution.py:393
  14.3 20.8 %collective-permute-start.1 = (f32[2,4,128,128]{3,2,1,0:T(8,128)}, f32[2,4,128,128]{3,2,1,0:T(8,128)}, u32[]{:S(2)}, u32[]{:S(2)}) collective-permute-start(f32[2,4,128,128]{3,2,1,0:T(8,128)} %get-tuple-element.44.refs_0_), channel_id=1, source_target_pairs={{0,8},{2,10},{8,16},{10,18},{16,24},{18,26},{24,28},{26,30},{28,20... | collective-permute-start | bytes 1572872 | tf_op jit(solution)/shard_map/ppermute | solution.py:393
  16.4 20.8 %collective-permute-start.3 = (f32[2,4,128,128]{3,2,1,0:T(8,128)}, f32[2,4,128,128]{3,2,1,0:T(8,128)S(1)}, u32[]{:S(2)}, u32[]{:S(2)}) collective-permute-start(f32[2,4,128,128]{3,2,1,0:T(8,128)} %get-tuple-element.44.refs_0_), channel_id=1, source_target_pairs={{0,4},{2,6},{8,0},{10,2},{16,8},{18,10},{24,16},{26,18},{28,24},{3... | collective-permute-start | bytes 1572872 | tf_op jit(solution)/shard_map/ppermute | solution.py:393
  23.8 68.6 %copy-start = (f32[2,4,128,128]{3,2,1,0:T(8,128)}, f32[2,4,128,128]{3,2,1,0:T(8,128)S(1)}, u32[]{:S(2)}) copy-start(f32[2,4,128,128]{3,2,1,0:T(8,128)S(1)} %collective-permute-done.9.refs_9_) | copy-start | bytes 1572868
  26.0 68.2 %copy-start.1 = (f32[2,4,128,128]{3,2,1,0:T(8,128)}, f32[2,4,128,128]{3,2,1,0:T(8,128)S(1)}, u32[]{:S(2)}) copy-start(f32[2,4,128,128]{3,2,1,0:T(8,128)S(1)} %collective-permute-done.10.refs_12_) | copy-start | bytes 1572868
  26.0 20.3 %collective-permute-start.11 = (f32[2,4,128,128]{3,2,1,0:T(8,128)S(1)}, f32[2,4,128,128]{3,2,1,0:T(8,128)S(1)}, u32[]{:S(2)}, u32[]{:S(2)}) collective-permute-start(f32[2,4,128,128]{3,2,1,0:T(8,128)S(1)} %collective-permute-done.9.refs_9_), channel_id=1, source_target_pairs={{0,8},{2,10},{8,16},{10,18},{16,24},{18,26},{24,28},{26,30},{28,20... | collective-permute-start | bytes 1572872 | tf_op jit(solution)/shard_map/ppermute | solution.py:393
  27.5 20.9 %collective-permute-start.12 = (f32[2,4,128,128]{3,2,1,0:T(8,128)S(1)}, f32[2,4,128,128]{3,2,1,0:T(8,128)S(1)}, u32[]{:S(2)}, u32[]{:S(2)}) collective-permute-start(f32[2,4,128,128]{3,2,1,0:T(8,128)S(1)} %collective-permute-done.10.refs_12_), channel_id=1, source_target_pairs={{0,4},{2,6},{8,0},{10,2},{16,8},{18,10},{24,16},{26,18},{28,24},{3... | collective-permute-start | bytes 1572872 | tf_op jit(solution)/shard_map/ppermute | solution.py:393
  37.2 61.8 %copy-start.2 = (f32[2,4,128,128]{3,2,1,0:T(8,128)}, f32[2,4,128,128]{3,2,1,0:T(8,128)S(1)}, u32[]{:S(2)}) copy-start(f32[2,4,128,128]{3,2,1,0:T(8,128)S(1)} %collective-permute-done.3.refs_4_) | copy-start | bytes 1572868
  37.2 20.4 %collective-permute-start.4 = (f32[2,4,128,128]{3,2,1,0:T(8,128)}, f32[2,4,128,128]{3,2,1,0:T(8,128)}, u32[]{:S(2)}, u32[]{:S(2)}) collective-permute-start(f32[2,4,128,128]{3,2,1,0:T(8,128)} %collective-permute-done.1.token.refs_1_), channel_id=1, source_target_pairs={{0,8},{2,10},{8,16},{10,18},{16,24},{18,26},{24,28},{26,30},{28,20... | collective-permute-start | bytes 1572872 | tf_op jit(solution)/shard_map/ppermute | solution.py:393
  38.8 21.0 %collective-permute-start.5 = (f32[2,4,128,128]{3,2,1,0:T(8,128)S(1)}, f32[2,4,128,128]{3,2,1,0:T(8,128)}, u32[]{:S(2)}, u32[]{:S(2)}) collective-permute-start(f32[2,4,128,128]{3,2,1,0:T(8,128)S(1)} %collective-permute-done.3.refs_4_), channel_id=1, source_target_pairs={{0,4},{2,6},{8,0},{10,2},{16,8},{18,10},{24,16},{26,18},{28,24},{3... | collective-permute-start | bytes 1572872 | tf_op jit(solution)/shard_map/ppermute | solution.py:393
  46.2 13.5 %copy-start.3 = (f32[2,4,128,128]{3,2,1,0:T(8,128)}, f32[2,4,128,128]{3,2,1,0:T(8,128)S(1)}, u32[]{:S(2)}) copy-start(f32[2,4,128,128]{3,2,1,0:T(8,128)S(1)} %collective-permute-done.11.refs_10_) | copy-start | bytes 1572868
  48.4 20.4 %copy-start.4 = (f32[2,4,128,128]{3,2,1,0:T(8,128)}, f32[2,4,128,128]{3,2,1,0:T(8,128)S(1)}, u32[]{:S(2)}) copy-start(f32[2,4,128,128]{3,2,1,0:T(8,128)S(1)} %collective-permute-done.12.refs_13_) | copy-start | bytes 1572868
  48.4 20.4 %collective-permute-start.13 = (f32[2,4,128,128]{3,2,1,0:T(8,128)S(1)}, f32[2,4,128,128]{3,2,1,0:T(8,128)}, u32[]{:S(2)}, u32[]{:S(2)}) collective-permute-start(f32[2,4,128,128]{3,2,1,0:T(8,128)S(1)} %collective-permute-done.11.refs_10_), channel_id=1, source_target_pairs={{0,8},{2,10},{8,16},{10,18},{16,24},{18,26},{24,28},{26,30},{28,20... | collective-permute-start | bytes 1572872 | tf_op jit(solution)/shard_map/ppermute | solution.py:393
  50.0 21.0 %collective-permute-start.14 = (f32[2,4,128,128]{3,2,1,0:T(8,128)S(1)}, f32[2,4,128,128]{3,2,1,0:T(8,128)}, u32[]{:S(2)}, u32[]{:S(2)}) collective-permute-start(f32[2,4,128,128]{3,2,1,0:T(8,128)S(1)} %collective-permute-done.12.refs_13_), channel_id=1, source_target_pairs={{0,4},{2,6},{8,0},{10,2},{16,8},{18,10},{24,16},{26,18},{28,24},{3... | collective-permute-start | bytes 1572872 | tf_op jit(solution)/shard_map/ppermute | solution.py:393
  59.8 19.8 %collective-permute-start.6 = (f32[2,4,128,128]{3,2,1,0:T(8,128)}, f32[2,4,128,128]{3,2,1,0:T(8,128)}, u32[]{:S(2)}, u32[]{:S(2)}) collective-permute-start(f32[2,4,128,128]{3,2,1,0:T(8,128)} %collective-permute-done.4.token.refs_2_), channel_id=1, source_target_pairs={{0,8},{2,10},{8,16},{10,18},{16,24},{18,26},{24,28},{26,30},{28,20... | collective-permute-start | bytes 1572872 | tf_op jit(solution)/shard_map/ppermute | solution.py:393
  61.4 20.9 %collective-permute-start.7 = (f32[2,4,128,128]{3,2,1,0:T(8,128)}, f32[2,4,128,128]{3,2,1,0:T(8,128)}, u32[]{:S(2)}, u32[]{:S(2)}) collective-permute-start(f32[2,4,128,128]{3,2,1,0:T(8,128)} %collective-permute-done.5.refs_5_), channel_id=1, source_target_pairs={{0,4},{2,6},{8,0},{10,2},{16,8},{18,10},{24,16},{26,18},{28,24},{3... | collective-permute-start | bytes 1572872 | tf_op jit(solution)/shard_map/ppermute | solution.py:393
  71.0 21.3 %collective-permute-start.15 = (f32[2,4,128,128]{3,2,1,0:T(8,128)}, f32[2,4,128,128]{3,2,1,0:T(8,128)}, u32[]{:S(2)}, u32[]{:S(2)}) collective-permute-start(f32[2,4,128,128]{3,2,1,0:T(8,128)} %collective-permute-done.14.refs_14_), channel_id=1, source_target_pairs={{0,4},{2,6},{8,0},{10,2},{16,8},{18,10},{24,16},{26,18},{28,24},{3... | collective-permute-start | bytes 1572872 | tf_op jit(solution)/shard_map/ppermute | solution.py:393
  82.2 59.6 %copy-start.20 = (f32[1,128,128]{2,1,0:T(8,128)S(1)}, f32[1,128,128]{2,1,0:T(8,128)}, u32[]{:S(2)}) copy-start(f32[1,128,128]{2,1,0:T(8,128)} %get-tuple-element.78) | copy-start | bytes 196612
  82.3 11.9 %collective-permute-start.8 = (f32[2,4,128,128]{3,2,1,0:T(8,128)}, f32[2,4,128,128]{3,2,1,0:T(8,128)S(1)}, u32[]{:S(2)}, u32[]{:S(2)}) collective-permute-start(f32[2,4,128,128]{3,2,1,0:T(8,128)} %collective-permute-done.6.refs_3_), channel_id=1, source_target_pairs={{0,8},{2,10},{8,16},{10,18},{16,24},{18,26},{24,28},{26,30},{28,20... | collective-permute-start | bytes 1572872 | tf_op jit(solution)/shard_map/ppermute | solution.py:393
  92.4 2.6 %collective-permute-start.23 = (f32[2,4,128,128]{3,2,1,0:T(8,128)S(1)}, f32[2,4,128,128]{3,2,1,0:T(8,128)S(1)}, u32[]{:S(2)}, u32[]{:S(2)}) collective-permute-start(f32[2,4,128,128]{3,2,1,0:T(8,128)S(1)} %collective-permute-done.9.refs_9_), channel_id=1, source_target_pairs={{0,2},{2,0},{4,6},{6,4},{8,10},{10,8},{12,14},{14,12},{16,18},{18,... | collective-permute-start | bytes 1572872 | tf_op jit(solution)/shard_map/ppermute | solution.py:366
  92.4 2.9 %collective-permute-start.24 = (f32[2,4,128,128]{3,2,1,0:T(8,128)}, f32[2,4,128,128]{3,2,1,0:T(8,128)S(1)}, u32[]{:S(2)}, u32[]{:S(2)}) collective-permute-start(f32[2,4,128,128]{3,2,1,0:T(8,128)} %copy-done.3), channel_id=1, source_target_pairs={{0,2},{2,0},{4,6},{6,4},{8,10},{10,8},{12,14},{14,12},{16,18},{18,... | collective-permute-start | bytes 1572872 | tf_op jit(solution)/shard_map/ppermute | solution.py:366
  92.9 3.1 %collective-permute-start.25 = (f32[2,4,128,128]{3,2,1,0:T(8,128)}, f32[2,4,128,128]{3,2,1,0:T(8,128)S(1)}, u32[]{:S(2)}, u32[]{:S(2)}) collective-permute-start(f32[2,4,128,128]{3,2,1,0:T(8,128)} %collective-permute-done.13.refs_11_), channel_id=1, source_target_pairs={{0,2},{2,0},{4,6},{6,4},{8,10},{10,8},{12,14},{14,12},{16,18},{18,... | collective-permute-start | bytes 1572872 | tf_op jit(solution)/shard_map/ppermute | solution.py:366
  94.1 8.0 %copy-start.5 = (f32[2,4,128,128]{3,2,1,0:T(8,128)}, f32[2,4,128,128]{3,2,1,0:T(8,128)S(1)}, u32[]{:S(2)}) copy-start(f32[2,4,128,128]{3,2,1,0:T(8,128)S(1)} %collective-permute-done.8.refs_7_) | copy-start | bytes 1572868
  94.1 2.4 %collective-permute-start.26 = (f32[2,4,128,128]{3,2,1,0:T(8,128)S(1)}, f32[2,4,128,128]{3,2,1,0:T(8,128)S(1)}, u32[]{:S(2)}, u32[]{:S(2)}) collective-permute-start(f32[2,4,128,128]{3,2,1,0:T(8,128)S(1)} %collective-permute-done.10.refs_12_), channel_id=1, source_target_pairs={{0,2},{2,0},{4,6},{6,4},{8,10},{10,8},{12,14},{14,12},{16,18},{18,... | collective-permute-start | bytes 1572872 | tf_op jit(solution)/shard_map/ppermute | solution.py:366
  95.0 9.0 %copy-start.6 = (f32[2,4,128,128]{3,2,1,0:T(8,128)}, f32[2,4,128,128]{3,2,1,0:T(8,128)S(1)}, u32[]{:S(2)}) copy-start(f32[2,4,128,128]{3,2,1,0:T(8,128)S(1)} %collective-permute-done.23.refs_25_) | copy-start | bytes 1572868
  95.0 2.5 %collective-permute-start.27 = (f32[2,4,128,128]{3,2,1,0:T(8,128)}, f32[2,4,128,128]{3,2,1,0:T(8,128)S(1)}, u32[]{:S(2)}, u32[]{:S(2)}) collective-permute-start(f32[2,4,128,128]{3,2,1,0:T(8,128)} %copy-done.4), channel_id=1, source_target_pairs={{0,2},{2,0},{4,6},{6,4},{8,10},{10,8},{12,14},{14,12},{16,18},{18,... | collective-permute-start | bytes 1572872 | tf_op jit(solution)/shard_map/ppermute | solution.py:366
  95.2 8.8 %copy-start.7 = (f32[2,4,128,128]{3,2,1,0:T(8,128)}, f32[2,4,128,128]{3,2,1,0:T(8,128)S(1)}, u32[]{:S(2)}) copy-start(f32[2,4,128,128]{3,2,1,0:T(8,128)S(1)} %collective-permute-done.24.refs_26_) | copy-start | bytes 1572868
  95.2 3.0 %collective-permute-start.28 = (f32[2,4,128,128]{3,2,1,0:T(8,128)}, f32[2,4,128,128]{3,2,1,0:T(8,128)S(1)}, u32[]{:S(2)}, u32[]{:S(2)}) collective-permute-start(f32[2,4,128,128]{3,2,1,0:T(8,128)} %collective-permute-done.14.refs_14_), channel_id=1, source_target_pairs={{0,2},{2,0},{4,6},{6,4},{8,10},{10,8},{12,14},{14,12},{16,18},{18,... | collective-permute-start | bytes 1572872 | tf_op jit(solution)/shard_map/ppermute | solution.py:366
  96.0 8.0 %copy-start.8 = (f32[2,4,128,128]{3,2,1,0:T(8,128)}, f32[2,4,128,128]{3,2,1,0:T(8,128)S(1)}, u32[]{:S(2)}) copy-start(f32[2,4,128,128]{3,2,1,0:T(8,128)S(1)} %collective-permute-done.25.refs_27_) | copy-start | bytes 1572868
  96.0 3.0 %collective-permute-start.29 = (f32[2,4,128,128]{3,2,1,0:T(8,128)}, f32[2,4,128,128]{3,2,1,0:T(8,128)S(1)}, u32[]{:S(2)}, u32[]{:S(2)}) collective-permute-start(f32[2,4,128,128]{3,2,1,0:T(8,128)} %collective-permute-done.15.refs_15_), channel_id=1, source_target_pairs={{0,2},{2,0},{4,6},{6,4},{8,10},{10,8},{12,14},{14,12},{16,18},{18,... | collective-permute-start | bytes 1572872 | tf_op jit(solution)/shard_map/ppermute | solution.py:366
  96.5 7.5 %copy-start.9 = (f32[2,4,128,128]{3,2,1,0:T(8,128)}, f32[2,4,128,128]{3,2,1,0:T(8,128)S(1)}, u32[]{:S(2)}) copy-start(f32[2,4,128,128]{3,2,1,0:T(8,128)S(1)} %collective-permute-done.26.refs_28_) | copy-start | bytes 1572868
  96.5 3.2 %collective-permute-start.16 = (f32[2,4,128,128]{3,2,1,0:T(8,128)}, f32[2,4,128,128]{3,2,1,0:T(8,128)S(1)}, u32[]{:S(2)}, u32[]{:S(2)}) collective-permute-start(f32[2,4,128,128]{3,2,1,0:T(8,128)} %collective-permute-done.1.token.refs_1_), channel_id=1, source_target_pairs={{0,2},{2,0},{4,6},{6,4},{8,10},{10,8},{12,14},{14,12},{16,18},{18,... | collective-permute-start | bytes 1572872 | tf_op jit(solution)/shard_map/ppermute | solution.py:366
  97.5 9.0 %copy-start.10 = (f32[2,4,128,128]{3,2,1,0:T(8,128)}, f32[2,4,128,128]{3,2,1,0:T(8,128)S(1)}, u32[]{:S(2)}) copy-start(f32[2,4,128,128]{3,2,1,0:T(8,128)S(1)} %collective-permute-done.27.refs_29_) | copy-start | bytes 1572868
  97.5 3.0 %collective-permute-start.17 = (f32[2,4,128,128]{3,2,1,0:T(8,128)}, f32[2,4,128,128]{3,2,1,0:T(8,128)S(1)}, u32[]{:S(2)}, u32[]{:S(2)}) collective-permute-start(f32[2,4,128,128]{3,2,1,0:T(8,128)} %collective-permute-done.4.token.refs_2_), channel_id=1, source_target_pairs={{0,2},{2,0},{4,6},{6,4},{8,10},{10,8},{12,14},{14,12},{16,18},{18,... | collective-permute-start | bytes 1572872 | tf_op jit(solution)/shard_map/ppermute | solution.py:366
  98.2 5.8 %copy-start.11 = (f32[2,4,128,128]{3,2,1,0:T(8,128)}, f32[2,4,128,128]{3,2,1,0:T(8,128)S(1)}, u32[]{:S(2)}) copy-start(f32[2,4,128,128]{3,2,1,0:T(8,128)S(1)} %collective-permute-done.28.refs_30_) | copy-start | bytes 1572868
  98.2 3.7 %collective-permute-start.18 = (f32[2,4,128,128]{3,2,1,0:T(8,128)}, f32[2,4,128,128]{3,2,1,0:T(8,128)S(1)}, u32[]{:S(2)}, u32[]{:S(2)}) collective-permute-start(f32[2,4,128,128]{3,2,1,0:T(8,128)} %collective-permute-done.6.refs_3_), channel_id=1, source_target_pairs={{0,2},{2,0},{4,6},{6,4},{8,10},{10,8},{12,14},{14,12},{16,18},{18,... | collective-permute-start | bytes 1572872 | tf_op jit(solution)/shard_map/ppermute | solution.py:366
  99.0 5.1 %copy-start.12 = (f32[2,4,128,128]{3,2,1,0:T(8,128)}, f32[2,4,128,128]{3,2,1,0:T(8,128)S(1)}, u32[]{:S(2)}) copy-start(f32[2,4,128,128]{3,2,1,0:T(8,128)S(1)} %collective-permute-done.29.refs_31_) | copy-start | bytes 1572868
  99.0 3.1 %collective-permute-start.19 = (f32[2,4,128,128]{3,2,1,0:T(8,128)S(1)}, f32[2,4,128,128]{3,2,1,0:T(8,128)S(1)}, u32[]{:S(2)}, u32[]{:S(2)}) collective-permute-start(f32[2,4,128,128]{3,2,1,0:T(8,128)S(1)} %collective-permute-done.3.refs_4_), channel_id=1, source_target_pairs={{0,2},{2,0},{4,6},{6,4},{8,10},{10,8},{12,14},{14,12},{16,18},{18,... | collective-permute-start | bytes 1572872 | tf_op jit(solution)/shard_map/ppermute | solution.py:366
  99.7 6.7 %copy-start.13 = (f32[2,4,128,128]{3,2,1,0:T(8,128)}, f32[2,4,128,128]{3,2,1,0:T(8,128)S(1)}, u32[]{:S(2)}) copy-start(f32[2,4,128,128]{3,2,1,0:T(8,128)S(1)} %collective-permute-done.16.refs_17_) | copy-start | bytes 1572868
  99.7 3.0 %collective-permute-start.20 = (f32[2,4,128,128]{3,2,1,0:T(8,128)}, f32[2,4,128,128]{3,2,1,0:T(8,128)S(1)}, u32[]{:S(2)}, u32[]{:S(2)}) collective-permute-start(f32[2,4,128,128]{3,2,1,0:T(8,128)} %collective-permute-done.5.refs_5_), channel_id=1, source_target_pairs={{0,2},{2,0},{4,6},{6,4},{8,10},{10,8},{12,14},{14,12},{16,18},{18,... | collective-permute-start | bytes 1572872 | tf_op jit(solution)/shard_map/ppermute | solution.py:366
  100.5 3.6 %copy-start.14 = (f32[2,4,128,128]{3,2,1,0:T(8,128)}, f32[2,4,128,128]{3,2,1,0:T(8,128)S(1)}, u32[]{:S(2)}) copy-start(f32[2,4,128,128]{3,2,1,0:T(8,128)S(1)} %collective-permute-done.17.refs_18_) | copy-start | bytes 1572868
  100.5 3.0 %collective-permute-start.21 = (f32[2,4,128,128]{3,2,1,0:T(8,128)}, f32[2,4,128,128]{3,2,1,0:T(8,128)S(1)}, u32[]{:S(2)}, u32[]{:S(2)}) collective-permute-start(f32[2,4,128,128]{3,2,1,0:T(8,128)} %collective-permute-done.7.refs_6_), channel_id=1, source_target_pairs={{0,2},{2,0},{4,6},{6,4},{8,10},{10,8},{12,14},{14,12},{16,18},{18,... | collective-permute-start | bytes 1572872 | tf_op jit(solution)/shard_map/ppermute | solution.py:366
  102.0 2.1 %copy-start.15 = (f32[2,4,128,128]{3,2,1,0:T(8,128)}, f32[2,4,128,128]{3,2,1,0:T(8,128)S(1)}, u32[]{:S(2)}) copy-start(f32[2,4,128,128]{3,2,1,0:T(8,128)S(1)} %collective-permute-done.18.refs_19_) | copy-start | bytes 1572868
  102.0 2.0 %collective-permute-start.22 = (f32[2,4,128,128]{3,2,1,0:T(8,128)S(1)}, f32[2,4,128,128]{3,2,1,0:T(8,128)S(1)}, u32[]{:S(2)}, u32[]{:S(2)}) collective-permute-start(f32[2,4,128,128]{3,2,1,0:T(8,128)S(1)} %collective-permute-done.8.refs_7_), channel_id=1, source_target_pairs={{0,2},{2,0},{4,6},{6,4},{8,10},{10,8},{12,14},{14,12},{16,18},{18,... | collective-permute-start | bytes 1572872 | tf_op jit(solution)/shard_map/ppermute | solution.py:366
  102.1 2.0 %copy-start.16 = (f32[2,4,128,128]{3,2,1,0:T(8,128)}, f32[2,4,128,128]{3,2,1,0:T(8,128)S(1)}, u32[]{:S(2)}) copy-start(f32[2,4,128,128]{3,2,1,0:T(8,128)S(1)} %collective-permute-done.19.refs_20_) | copy-start | bytes 1572868
  102.7 1.4 copy-start.17
  103.5 0.8 copy-start.18
  104.3 0.8 copy-start.19
  121.6 2.2 %collective-permute-start.30 = (f32[8,128,128]{2,1,0:T(8,128)}, f32[8,128,128]{2,1,0:T(8,128)S(1)}, u32[]{:S(2)}, u32[]{:S(2)}) collective-permute-start(f32[8,128,128]{2,1,0:T(8,128)} %get-tuple-element.80), channel_id=1, source_target_pairs={{0,2},{2,0},{4,6},{6,4},{8,10},{10,8},{12,14},{14,12},{16,18},{18,... | collective-permute-start | bytes 1572872 | tf_op jit(solution)/shard_map/ppermute | solution.py:366
  124.9 9.7 %collective-permute-start.31 = (f32[1,128,128]{2,1,0:T(8,128)S(1)}, f32[1,128,128]{2,1,0:T(8,128)S(1)}, u32[]{:S(2)}, u32[]{:S(2)}) collective-permute-start(f32[1,128,128]{2,1,0:T(8,128)S(1)} %get-tuple-element.84), channel_id=1, source_target_pairs={{0,4},{2,6},{4,0},{6,2},{8,12},{10,14},{12,8},{14,10},{16,20},{18,... | collective-permute-start | bytes 196616 | tf_op jit(solution)/shard_map/ppermute | solution.py:418
  127.9 8.9 %collective-permute-start.36 = (f32[1,128,128]{2,1,0:T(8,128)S(1)}, f32[1,128,128]{2,1,0:T(8,128)S(1)}, u32[]{:S(2)}, u32[]{:S(2)}) collective-permute-start(f32[1,128,128]{2,1,0:T(8,128)S(1)} %get-tuple-element.85), channel_id=1, source_target_pairs={{0,20},{2,22},{4,16},{6,18},{8,28},{10,30},{12,24},{14,26},{16,4},... | collective-permute-start | bytes 196616 | tf_op jit(solution)/shard_map/ppermute | solution.py:418
  129.4 9.7 %collective-permute-start.33 = (f32[1,128,128]{2,1,0:T(8,128)S(1)}, f32[1,128,128]{2,1,0:T(8,128)S(1)}, u32[]{:S(2)}, u32[]{:S(2)}) collective-permute-start(f32[1,128,128]{2,1,0:T(8,128)S(1)} %get-tuple-element.86), channel_id=1, source_target_pairs={{0,28},{2,30},{4,24},{6,26},{8,4},{10,6},{12,0},{14,2},{16,12},{18... | collective-permute-start | bytes 196616 | tf_op jit(solution)/shard_map/ppermute | solution.py:418
  131.0 8.1 %collective-permute-start.32 = (f32[1,128,128]{2,1,0:T(8,128)S(1)}, f32[1,128,128]{2,1,0:T(8,128)S(1)}, u32[]{:S(2)}, u32[]{:S(2)}) collective-permute-start(f32[1,128,128]{2,1,0:T(8,128)S(1)} %get-tuple-element.87), channel_id=1, source_target_pairs={{0,12},{2,14},{4,8},{6,10},{8,20},{10,22},{12,16},{14,18},{16,28},... | collective-permute-start | bytes 196616 | tf_op jit(solution)/shard_map/ppermute | solution.py:418
  132.3 7.9 %collective-permute-start.34 = (f32[1,128,128]{2,1,0:T(8,128)S(1)}, f32[1,128,128]{2,1,0:T(8,128)S(1)}, u32[]{:S(2)}, u32[]{:S(2)}) collective-permute-start(f32[1,128,128]{2,1,0:T(8,128)S(1)} %get-tuple-element.88), channel_id=1, source_target_pairs={{0,8},{2,10},{4,12},{6,14},{8,16},{10,18},{12,20},{14,22},{16,24},... | collective-permute-start | bytes 196616 | tf_op jit(solution)/shard_map/ppermute | solution.py:418
  134.6 7.3 %collective-permute-start.37 = (f32[1,128,128]{2,1,0:T(8,128)S(1)}, f32[1,128,128]{2,1,0:T(8,128)S(1)}, u32[]{:S(2)}, u32[]{:S(2)}) collective-permute-start(f32[1,128,128]{2,1,0:T(8,128)S(1)} %get-tuple-element.89), channel_id=1, source_target_pairs={{0,16},{2,18},{4,20},{6,22},{8,24},{10,26},{12,28},{14,30},{16,0},... | collective-permute-start | bytes 196616 | tf_op jit(solution)/shard_map/ppermute | solution.py:418
  136.7 5.2 %collective-permute-start.35 = (f32[1,128,128]{2,1,0:T(8,128)S(1)}, f32[1,128,128]{2,1,0:T(8,128)S(1)}, u32[]{:S(2)}, u32[]{:S(2)}) collective-permute-start(f32[1,128,128]{2,1,0:T(8,128)S(1)} %get-tuple-element.90), channel_id=1, source_target_pairs={{0,24},{2,26},{4,28},{6,30},{8,0},{10,2},{12,4},{14,6},{16,8},{18,... | collective-permute-start | bytes 196616 | tf_op jit(solution)/shard_map/ppermute | solution.py:418

commit v5 on v4

--- a/solution.py
+++ b/solution.py
@@ -261,10 +261,10 @@
                     copy.wait()
 
     def close(a, carry):
-        diagonals(a)
         for t in range(per_set):
             kk = a * per_set + t
             pltpu.make_async_copy(z_buf.at[kk], z_out.at[tables[plan.node + kk]], sems.at[2 + sets]).start()
+        diagonals(a)
         return carry
 
     def step(group, carry):

time: 143 us -> 144 us (level)
  starting transfers between devices: 33.4 us -> 31 us
  waiting for transfers between devices: 71.1 us -> 73.4 us
    ppermute x7, starting transfers between devices: 14.2 us -> 11.7 us  [body(): z_diag = z_diag + permute(source[m:m + 1], 'row', links)]
    ppermute x7, waiting for transfers between devices: 2.8 us -> 5.16 us  [body(): z_diag = z_diag + permute(source[m:m + 1], 'row', links)]
  transfers between devices with their start and end apart: 38 -> 38, of which waited for: 31 -> 33; matrix products, arithmetic and copies ran while one was open for 0% -> 0% of each run, Pallas kernels for 12% -> 12%
where the time goes in v5:
time: 144 us
  waiting for transfers between devices  73.4 us (51%)
  Pallas kernels  34 us (24%)
  starting transfers between devices  31 us (22%)
  other arithmetic  2.38 us (2%)
  local copies, waits for them, and re-layouts  2.04 us (1%)
    ppermute x14, waiting for transfers between devices, body(): permute(front[0 if way > 0 else 1], 'row', pairs(way))  56.5 us
    pallas_call x1, Pallas kernels, all_sums(): pl.pallas_call(functools.partial(sums_kernel, (rows, zs, chip_of, sets, h...  16.3 us
    ppermute x14, starting transfers between devices, body(): permute(front[0 if way > 0 else 1], 'row', pairs(way))  14 us
    pallas_call x4, Pallas kernels, u_blocks(): pl.pallas_call(functools.partial(u_kernel, chips, other), out_shape=[jax....  13.3 us
    ppermute x7, starting transfers between devices, body(): z_diag = z_diag + permute(source[m:m + 1], 'row', links)  11.7 us
    ppermute x16, waiting for transfers between devices, swapped(): return permute(array, 'row', swap_core)  10.4 us
    ppermute x7, waiting for transfers between devices, body(): z_diag = z_diag + permute(source[m:m + 1], 'row', links)  5.16 us
    pallas_call x1, Pallas kernels, make_plan(): pl.pallas_call(functools.partial(plan_kernel, dims, plan), out_shape=jax....  4.42 us
  transfers between devices with their start and end apart: 38, of which 33 were waited for; matrix products, arithmetic and copies ran while one was open for 0% of the time, Pallas kernels for 12%

profile of v5, /device:TPU:0, one launch (start us, length us, event | category | flops | bytes accessed | tf_op | source)
XLA Modules:
  0.0 143.6 jit_solution(8487492531944441363)
XLA Ops:
  0.6 0.5 collective-permute-start
  1.1 2.6 %collective-permute-start.2 = (f32[3,24,128,128]{3,2,1,0:T(8,128)}, f32[3,24,128,128]{3,2,1,0:T(8,128)}, u32[]{:S(2)}, u32[]{:S(2)}) collective-permute-start(f32[3,24,128,128]{3,2,1,0:T(8,128)} %near.1), channel_id=1, source_target_pairs={{1,0},{0,1},{3,2},{2,3},{5,4},{4,5},{7,6},{6,7},{9,8},{8,9},{11,10... | collective-permute-start | bytes 14155784 | tf_op jit(solution)/shard_map/ppermute | solution.py:372
  3.7 0.6 pad_add_fusion.where
  4.4 1.0 copy-done.21
  5.3 3.3 %u_blocks.7 = (f32[2,4,128,128]{3,2,1,0:T(8,128)}, f32[1,128,128]{2,1,0:T(8,128)}) custom-call(s32[2]{0:T(128)} %pad_add_fusion.where, f32[16,128,128]{2,1,0:T(8,128)} %bitcast.4, f32[16,128,128]{2,1,0:T(8,128)} %copy-done.21, f32[16,128,128]{2,1,0:T(8,128)} %inverse.7, s32[16,16]{1,0:T(8,128)} %token_.3), custom_call_target="tpu_custom_call" | custom-call | flops 1000000000 | bytes 1000 | tf_op jit(solution)/shard_map/u_blocks/pallas_call | solution.py:158
  8.7 2.3 %collective-permute-start.9 = (f32[2,4,128,128]{3,2,1,0:T(8,128)}, f32[2,4,128,128]{3,2,1,0:T(8,128)S(1)}, u32[]{:S(2)}, u32[]{:S(2)}) collective-permute-start(f32[2,4,128,128]{3,2,1,0:T(8,128)} %get-tuple-element.57.refs_8_), channel_id=1, source_target_pairs={{0,8},{2,10},{8,16},{10,18},{16,24},{18,26},{24,28},{26,30},{28,20... | collective-permute-start | bytes 1572872 | tf_op jit(solution)/shard_map/ppermute | solution.py:393
  10.9 3.3 %u_blocks.4 = (f32[2,4,128,128]{3,2,1,0:T(8,128)}, f32[1,128,128]{2,1,0:T(8,128)}) custom-call(s32[2]{0:T(128)} %pad_add_fusion.where, f32[16,128,128]{2,1,0:T(8,128)} %bitcast.5, f32[16,128,128]{2,1,0:T(8,128)} %copy-done.21, f32[16,128,128]{2,1,0:T(8,128)} %inverse.7, s32[16,16]{1,0:T(8,128)} %token_.3), custom_call_target="tpu_custom_call" | custom-call | flops 1000000000 | bytes 1000 | tf_op jit(solution)/shard_map/u_blocks/pallas_call | solution.py:158
  14.3 2.1 %collective-permute-start.1 = (f32[2,4,128,128]{3,2,1,0:T(8,128)}, f32[2,4,128,128]{3,2,1,0:T(8,128)}, u32[]{:S(2)}, u32[]{:S(2)}) collective-permute-start(f32[2,4,128,128]{3,2,1,0:T(8,128)} %get-tuple-element.44.refs_0_), channel_id=1, source_target_pairs={{0,8},{2,10},{8,16},{10,18},{16,24},{18,26},{24,28},{26,30},{28,20... | collective-permute-start | bytes 1572872 | tf_op jit(solution)/shard_map/ppermute | solution.py:393
  16.4 7.4 %collective-permute-done.9.refs_9_ = f32[2,4,128,128]{3,2,1,0:T(8,128)S(1)} collective-permute-done((f32[2,4,128,128]{3,2,1,0:T(8,128)}, f32[2,4,128,128]{3,2,1,0:T(8,128)S(1)}, u32[]{:S(2)}, u32[]{:S(2)}) %collective-permute-start.9) | collective-permute-done | bytes 524320 | tf_op jit(solution)/shard_map/ppermute | solution.py:393
  23.8 2.2 %collective-permute-done.10.refs_12_ = f32[2,4,128,128]{3,2,1,0:T(8,128)S(1)} collective-permute-done((f32[2,4,128,128]{3,2,1,0:T(8,128)}, f32[2,4,128,128]{3,2,1,0:T(8,128)S(1)}, u32[]{:S(2)}, u32[]{:S(2)}) %collective-permute-start.10) | collective-permute-done | bytes 524320 | tf_op jit(solution)/shard_map/ppermute | solution.py:393
  26.0 1.6 %collective-permute-start.11 = (f32[2,4,128,128]{3,2,1,0:T(8,128)S(1)}, f32[2,4,128,128]{3,2,1,0:T(8,128)S(1)}, u32[]{:S(2)}, u32[]{:S(2)}) collective-permute-start(f32[2,4,128,128]{3,2,1,0:T(8,128)S(1)} %collective-permute-done.9.refs_9_), channel_id=1, source_target_pairs={{0,8},{2,10},{8,16},{10,18},{16,24},{18,26},{24,28},{26,30},{28,20... | collective-permute-start | bytes 1572872 | tf_op jit(solution)/shard_map/ppermute | solution.py:393
  27.5 0.5 collective-permute-start.12
  28.0 7.1 %collective-permute-done.1.token.refs_1_ = f32[2,4,128,128]{3,2,1,0:T(8,128)} collective-permute-done((f32[2,4,128,128]{3,2,1,0:T(8,128)}, f32[2,4,128,128]{3,2,1,0:T(8,128)}, u32[]{:S(2)}, u32[]{:S(2)}) %collective-permute-start.1) | collective-permute-done | bytes 524320 | tf_op jit(solution)/shard_map/ppermute | solution.py:393
  35.1 2.1 %collective-permute-done.3.refs_4_ = f32[2,4,128,128]{3,2,1,0:T(8,128)S(1)} collective-permute-done((f32[2,4,128,128]{3,2,1,0:T(8,128)}, f32[2,4,128,128]{3,2,1,0:T(8,128)S(1)}, u32[]{:S(2)}, u32[]{:S(2)}) %collective-permute-start.3) | collective-permute-done | bytes 524320 | tf_op jit(solution)/shard_map/ppermute | solution.py:393
  37.2 1.6 %collective-permute-start.4 = (f32[2,4,128,128]{3,2,1,0:T(8,128)}, f32[2,4,128,128]{3,2,1,0:T(8,128)}, u32[]{:S(2)}, u32[]{:S(2)}) collective-permute-start(f32[2,4,128,128]{3,2,1,0:T(8,128)} %collective-permute-done.1.token.refs_1_), channel_id=1, source_target_pairs={{0,8},{2,10},{8,16},{10,18},{16,24},{18,26},{24,28},{26,30},{28,20... | collective-permute-start | bytes 1572872 | tf_op jit(solution)/shard_map/ppermute | solution.py:393
  38.8 0.5 collective-permute-start.5
  39.2 7.0 %collective-permute-done.11.refs_10_ = f32[2,4,128,128]{3,2,1,0:T(8,128)S(1)} collective-permute-done((f32[2,4,128,128]{3,2,1,0:T(8,128)S(1)}, f32[2,4,128,128]{3,2,1,0:T(8,128)S(1)}, u32[]{:S(2)}, u32[]{:S(2)}) %collective-permute-start.11) | collective-permute-done | bytes 524320 | tf_op jit(solution)/shard_map/ppermute | solution.py:393
  46.2 2.2 %collective-permute-done.12.refs_13_ = f32[2,4,128,128]{3,2,1,0:T(8,128)S(1)} collective-permute-done((f32[2,4,128,128]{3,2,1,0:T(8,128)S(1)}, f32[2,4,128,128]{3,2,1,0:T(8,128)S(1)}, u32[]{:S(2)}, u32[]{:S(2)}) %collective-permute-start.12) | collective-permute-done | bytes 524320 | tf_op jit(solution)/shard_map/ppermute | solution.py:393
  48.4 1.6 %collective-permute-start.13 = (f32[2,4,128,128]{3,2,1,0:T(8,128)S(1)}, f32[2,4,128,128]{3,2,1,0:T(8,128)}, u32[]{:S(2)}, u32[]{:S(2)}) collective-permute-start(f32[2,4,128,128]{3,2,1,0:T(8,128)S(1)} %collective-permute-done.11.refs_10_), channel_id=1, source_target_pairs={{0,8},{2,10},{8,16},{10,18},{16,24},{18,26},{24,28},{26,30},{28,20... | collective-permute-start | bytes 1572872 | tf_op jit(solution)/shard_map/ppermute | solution.py:393
  50.0 0.5 collective-permute-start.14
  50.5 4.4 %plan.1.tables = s32[371]{0:T(512)} custom-call(s32[2]{0:T(128)} %pad_add_fusion.where, s32[256]{0:T(256)} %constant.12.clone.table, s32[8]{0:T(128)} %constant.13.clone.chip_of, s32[16,16]{1,0:T(8,128)} %token_.3, f32[2,4,128,128]{3,2,1,0:T(8,128)} %collective-permute-done.1.token.refs_1_), custom_call_target="tpu_custom_call" | custom-call | flops 1000000000 | bytes 1000 | tf_op jit(solution)/shard_map/plan/pallas_call | solution.py:109
  54.9 2.7 %collective-permute-done.4.token.refs_2_ = f32[2,4,128,128]{3,2,1,0:T(8,128)} collective-permute-done((f32[2,4,128,128]{3,2,1,0:T(8,128)}, f32[2,4,128,128]{3,2,1,0:T(8,128)}, u32[]{:S(2)}, u32[]{:S(2)}) %collective-permute-start.4) | collective-permute-done | bytes 524320 | tf_op jit(solution)/shard_map/ppermute | solution.py:393
  57.6 2.2 %collective-permute-done.5.refs_5_ = f32[2,4,128,128]{3,2,1,0:T(8,128)} collective-permute-done((f32[2,4,128,128]{3,2,1,0:T(8,128)S(1)}, f32[2,4,128,128]{3,2,1,0:T(8,128)}, u32[]{:S(2)}, u32[]{:S(2)}) %collective-permute-start.5) | collective-permute-done | bytes 524320 | tf_op jit(solution)/shard_map/ppermute | solution.py:393
  59.8 1.6 %collective-permute-start.6 = (f32[2,4,128,128]{3,2,1,0:T(8,128)}, f32[2,4,128,128]{3,2,1,0:T(8,128)}, u32[]{:S(2)}, u32[]{:S(2)}) collective-permute-start(f32[2,4,128,128]{3,2,1,0:T(8,128)} %collective-permute-done.4.token.refs_2_), channel_id=1, source_target_pairs={{0,8},{2,10},{8,16},{10,18},{16,24},{18,26},{24,28},{26,30},{28,20... | collective-permute-start | bytes 1572872 | tf_op jit(solution)/shard_map/ppermute | solution.py:393
  61.4 0.5 collective-permute-start.7
  61.8 7.0 %collective-permute-done.13.refs_11_ = f32[2,4,128,128]{3,2,1,0:T(8,128)} collective-permute-done((f32[2,4,128,128]{3,2,1,0:T(8,128)S(1)}, f32[2,4,128,128]{3,2,1,0:T(8,128)}, u32[]{:S(2)}, u32[]{:S(2)}) %collective-permute-start.13) | collective-permute-done | bytes 524320 | tf_op jit(solution)/shard_map/ppermute | solution.py:393
  68.8 2.2 %collective-permute-done.14.refs_14_ = f32[2,4,128,128]{3,2,1,0:T(8,128)} collective-permute-done((f32[2,4,128,128]{3,2,1,0:T(8,128)S(1)}, f32[2,4,128,128]{3,2,1,0:T(8,128)}, u32[]{:S(2)}, u32[]{:S(2)}) %collective-permute-start.14) | collective-permute-done | bytes 524320 | tf_op jit(solution)/shard_map/ppermute | solution.py:393
  71.0 3.3 %u_blocks.6 = (f32[2,4,128,128]{3,2,1,0:T(8,128)}, f32[1,128,128]{2,1,0:T(8,128)}) custom-call(s32[2]{0:T(128)} %pad_add_fusion.where, f32[16,128,128]{2,1,0:T(8,128)} %bitcast.6, f32[16,128,128]{2,1,0:T(8,128)} %copy-done.21, f32[16,128,128]{2,1,0:T(8,128)} %inverse.7, f32[2,4,128,128]{3,2,1,0:T(8,128)} %collective-permute-done.4.token.refs_2_), custom_call_target="tpu_custom_call" | custom-call | flops 1000000000 | bytes 1000 | tf_op jit(solution)/shard_map/u_blocks/pallas_call | solution.py:158
  74.4 3.3 %u_blocks.5 = (f32[2,4,128,128]{3,2,1,0:T(8,128)}, f32[1,128,128]{2,1,0:T(8,128)}) custom-call(s32[2]{0:T(128)} %pad_add_fusion.where, f32[16,128,128]{2,1,0:T(8,128)} %bitcast.7, f32[16,128,128]{2,1,0:T(8,128)} %copy-done.21, f32[16,128,128]{2,1,0:T(8,128)} %inverse.7, f32[2,4,128,128]{3,2,1,0:T(8,128)} %collective-permute-done.4.token.refs_2_), custom_call_target="tpu_custom_call" | custom-call | flops 1000000000 | bytes 1000 | tf_op jit(solution)/shard_map/u_blocks/pallas_call | solution.py:158
  77.7 1.9 %collective-permute-done.6.refs_3_ = f32[2,4,128,128]{3,2,1,0:T(8,128)} collective-permute-done((f32[2,4,128,128]{3,2,1,0:T(8,128)}, f32[2,4,128,128]{3,2,1,0:T(8,128)}, u32[]{:S(2)}, u32[]{:S(2)}) %collective-permute-start.6) | collective-permute-done | bytes 524320 | tf_op jit(solution)/shard_map/ppermute | solution.py:393
  79.6 2.7 %collective-permute-done.7.refs_6_ = f32[2,4,128,128]{3,2,1,0:T(8,128)} collective-permute-done((f32[2,4,128,128]{3,2,1,0:T(8,128)}, f32[2,4,128,128]{3,2,1,0:T(8,128)}, u32[]{:S(2)}, u32[]{:S(2)}) %collective-permute-start.7) | collective-permute-done | bytes 524320 | tf_op jit(solution)/shard_map/ppermute | solution.py:393
  82.3 1.6 %collective-permute-start.8 = (f32[2,4,128,128]{3,2,1,0:T(8,128)}, f32[2,4,128,128]{3,2,1,0:T(8,128)S(1)}, u32[]{:S(2)}, u32[]{:S(2)}) collective-permute-start(f32[2,4,128,128]{3,2,1,0:T(8,128)} %collective-permute-done.6.refs_3_), channel_id=1, source_target_pairs={{0,8},{2,10},{8,16},{10,18},{16,24},{18,26},{24,28},{26,30},{28,20... | collective-permute-start | bytes 1572872 | tf_op jit(solution)/shard_map/ppermute | solution.py:393
  83.8 8.5 %collective-permute-done.15.refs_15_ = f32[2,4,128,128]{3,2,1,0:T(8,128)} collective-permute-done((f32[2,4,128,128]{3,2,1,0:T(8,128)}, f32[2,4,128,128]{3,2,1,0:T(8,128)}, u32[]{:S(2)}, u32[]{:S(2)}) %collective-permute-start.15) | collective-permute-done | bytes 524320 | tf_op jit(solution)/shard_map/ppermute | solution.py:393
  92.4 0.5 collective-permute-start.24
  92.9 1.3 collective-permute-done.8.refs_7_
  94.2 0.8 collective-permute-done.23.refs_25_
  95.2 0.3 collective-permute-start.28
  95.5 0.5 collective-permute-done.25.refs_27_
  96.1 0.4 collective-permute-done.26.refs_28_
  96.7 0.8 collective-permute-done.27.refs_29_
  97.6 0.6 collective-permute-done.28.refs_30_
  98.4 0.6 collective-permute-done.29.refs_31_
  99.1 0.6 collective-permute-done.16.refs_17_
  99.9 0.6 collective-permute-done.17.refs_18_
  100.6 1.4 collective-permute-done.18.refs_19_
  102.1 0.6 collective-permute-done.20.refs_21_
  102.7 0.7 collective-permute-done.21.refs_22_
  103.5 0.5 collective-permute-done.22.refs_23_
  104.1 0.2 copy-done.18
  104.3 0.8 copy-done.19
  105.1 1.4 collective-permute-done.2.far
  106.5 16.3 %all_sums.1 = (f32[16,3,128,128]{3,2,1,0:T(8,128)}, f32[4,128,128]{2,1,0:T(8,128)}, f32[4,128,128]{2,1,0:T(8,128)}, f32[8,128,128]{2,1,0:T(8,128)}) custom-call(s32[2]{0:T(128)} %pad_add_fusion.where, s32[371]{0:T(512)} %plan.1.tables, f32[3,24,128,128]{3,2,1,0:T(8,128)} %near.1, f32[3,24,128,128]{3,2,1,0:T(8,128)} %collective-permute-done.2.far, ...), custom_call_target="tpu_custom_call" | custom-call | flops 3000000000 | bytes 1000 | tf_op jit(solution)/shard_map/all_sums/pallas_call | solution.py:311
  122.8 2.1 %collective-permute-done.30 = f32[8,128,128]{2,1,0:T(8,128)S(1)} collective-permute-done((f32[8,128,128]{2,1,0:T(8,128)}, f32[8,128,128]{2,1,0:T(8,128)S(1)}, u32[]{:S(2)}, u32[]{:S(2)}) %collective-permute-start.30) | collective-permute-done | bytes 524320 | tf_op jit(solution)/shard_map/ppermute | solution.py:366
  124.9 1.1 slice_add_fusion
  126.1 1.4 collective-permute-start.31
  127.5 3.2 %collective-permute-start.36 = (f32[1,128,128]{2,1,0:T(8,128)S(1)}, f32[1,128,128]{2,1,0:T(8,128)S(1)}, u32[]{:S(2)}, u32[]{:S(2)}) collective-permute-start(f32[1,128,128]{2,1,0:T(8,128)S(1)} %get-tuple-element.85), channel_id=1, source_target_pairs={{0,20},{2,22},{4,16},{6,18},{8,28},{10,30},{12,24},{14,26},{16,4},... | collective-permute-start | bytes 196616 | tf_op jit(solution)/shard_map/ppermute | solution.py:418
  130.6 2.7 %collective-permute-start.33 = (f32[1,128,128]{2,1,0:T(8,128)S(1)}, f32[1,128,128]{2,1,0:T(8,128)S(1)}, u32[]{:S(2)}, u32[]{:S(2)}) collective-permute-start(f32[1,128,128]{2,1,0:T(8,128)S(1)} %get-tuple-element.86), channel_id=1, source_target_pairs={{0,28},{2,30},{4,24},{6,26},{8,4},{10,6},{12,0},{14,2},{16,12},{18... | collective-permute-start | bytes 196616 | tf_op jit(solution)/shard_map/ppermute | solution.py:418
  133.4 0.2 collective-permute-start.32
  133.6 1.0 collective-permute-start.34
  134.6 3.2 %collective-permute-start.37 = (f32[1,128,128]{2,1,0:T(8,128)S(1)}, f32[1,128,128]{2,1,0:T(8,128)S(1)}, u32[]{:S(2)}, u32[]{:S(2)}) collective-permute-start(f32[1,128,128]{2,1,0:T(8,128)S(1)} %get-tuple-element.89), channel_id=1, source_target_pairs={{0,16},{2,18},{4,20},{6,22},{8,24},{10,26},{12,28},{14,30},{16,0},... | collective-permute-start | bytes 196616 | tf_op jit(solution)/shard_map/ppermute | solution.py:418
  137.8 3.4 %collective-permute-done.32 = f32[1,128,128]{2,1,0:T(8,128)S(1)} collective-permute-done((f32[1,128,128]{2,1,0:T(8,128)S(1)}, f32[1,128,128]{2,1,0:T(8,128)S(1)}, u32[]{:S(2)}, u32[]{:S(2)}) %collective-permute-start.32) | collective-permute-done | bytes 65568 | tf_op jit(solution)/shard_map/ppermute | solution.py:418
  141.3 1.4 %collective-permute-done.37 = f32[1,128,128]{2,1,0:T(8,128)S(1)} collective-permute-done((f32[1,128,128]{2,1,0:T(8,128)S(1)}, f32[1,128,128]{2,1,0:T(8,128)S(1)}, u32[]{:S(2)}, u32[]{:S(2)}) %collective-permute-start.37) | collective-permute-done | bytes 65568 | tf_op jit(solution)/shard_map/ppermute | solution.py:418
  142.8 0.2 collective-permute-done.35
  143.0 0.7 fusion.6
  (67 shorter events, 1.7 us)
Async XLA Ops:
  0.6 3.7 %collective-permute-start = (f32[16,128,128]{2,1,0:T(8,128)}, f32[16,128,128]{2,1,0:T(8,128)S(1)}, u32[]{:S(2)}, u32[]{:S(2)}) collective-permute-start(f32[16,128,128]{2,1,0:T(8,128)} %bitcast.3), channel_id=1, source_target_pairs={{0,2},{2,0},{4,6},{6,4},{8,10},{10,8},{12,14},{14,12},{16,18},{18,... | collective-permute-start | bytes 3145736 | tf_op jit(solution)/shard_map/ppermute | solution.py:366
  1.1 105.3 %collective-permute-start.2 = (f32[3,24,128,128]{3,2,1,0:T(8,128)}, f32[3,24,128,128]{3,2,1,0:T(8,128)}, u32[]{:S(2)}, u32[]{:S(2)}) collective-permute-start(f32[3,24,128,128]{3,2,1,0:T(8,128)} %near.1), channel_id=1, source_target_pairs={{1,0},{0,1},{3,2},{2,3},{5,4},{4,5},{7,6},{6,7},{9,8},{8,9},{11,10... | collective-permute-start | bytes 14155784 | tf_op jit(solution)/shard_map/ppermute | solution.py:372
  4.4 1.0 copy-start.21
  8.7 15.1 %collective-permute-start.9 = (f32[2,4,128,128]{3,2,1,0:T(8,128)}, f32[2,4,128,128]{3,2,1,0:T(8,128)S(1)}, u32[]{:S(2)}, u32[]{:S(2)}) collective-permute-start(f32[2,4,128,128]{3,2,1,0:T(8,128)} %get-tuple-element.57.refs_8_), channel_id=1, source_target_pairs={{0,8},{2,10},{8,16},{10,18},{16,24},{18,26},{24,28},{26,30},{28,20... | collective-permute-start | bytes 1572872 | tf_op jit(solution)/shard_map/ppermute | solution.py:393
  10.9 15.0 %collective-permute-start.10 = (f32[2,4,128,128]{3,2,1,0:T(8,128)}, f32[2,4,128,128]{3,2,1,0:T(8,128)S(1)}, u32[]{:S(2)}, u32[]{:S(2)}) collective-permute-start(f32[2,4,128,128]{3,2,1,0:T(8,128)} %get-tuple-element.57.refs_8_), channel_id=1, source_target_pairs={{0,4},{2,6},{8,0},{10,2},{16,8},{18,10},{24,16},{26,18},{28,24},{3... | collective-permute-start | bytes 1572872 | tf_op jit(solution)/shard_map/ppermute | solution.py:393
  14.3 20.8 %collective-permute-start.1 = (f32[2,4,128,128]{3,2,1,0:T(8,128)}, f32[2,4,128,128]{3,2,1,0:T(8,128)}, u32[]{:S(2)}, u32[]{:S(2)}) collective-permute-start(f32[2,4,128,128]{3,2,1,0:T(8,128)} %get-tuple-element.44.refs_0_), channel_id=1, source_target_pairs={{0,8},{2,10},{8,16},{10,18},{16,24},{18,26},{24,28},{26,30},{28,20... | collective-permute-start | bytes 1572872 | tf_op jit(solution)/shard_map/ppermute | solution.py:393
  16.4 20.8 %collective-permute-start.3 = (f32[2,4,128,128]{3,2,1,0:T(8,128)}, f32[2,4,128,128]{3,2,1,0:T(8,128)S(1)}, u32[]{:S(2)}, u32[]{:S(2)}) collective-permute-start(f32[2,4,128,128]{3,2,1,0:T(8,128)} %get-tuple-element.44.refs_0_), channel_id=1, source_target_pairs={{0,4},{2,6},{8,0},{10,2},{16,8},{18,10},{24,16},{26,18},{28,24},{3... | collective-permute-start | bytes 1572872 | tf_op jit(solution)/shard_map/ppermute | solution.py:393
  23.8 68.6 %copy-start = (f32[2,4,128,128]{3,2,1,0:T(8,128)}, f32[2,4,128,128]{3,2,1,0:T(8,128)S(1)}, u32[]{:S(2)}) copy-start(f32[2,4,128,128]{3,2,1,0:T(8,128)S(1)} %collective-permute-done.9.refs_9_) | copy-start | bytes 1572868
  26.0 68.2 %copy-start.1 = (f32[2,4,128,128]{3,2,1,0:T(8,128)}, f32[2,4,128,128]{3,2,1,0:T(8,128)S(1)}, u32[]{:S(2)}) copy-start(f32[2,4,128,128]{3,2,1,0:T(8,128)S(1)} %collective-permute-done.10.refs_12_) | copy-start | bytes 1572868
  26.0 20.3 %collective-permute-start.11 = (f32[2,4,128,128]{3,2,1,0:T(8,128)S(1)}, f32[2,4,128,128]{3,2,1,0:T(8,128)S(1)}, u32[]{:S(2)}, u32[]{:S(2)}) collective-permute-start(f32[2,4,128,128]{3,2,1,0:T(8,128)S(1)} %collective-permute-done.9.refs_9_), channel_id=1, source_target_pairs={{0,8},{2,10},{8,16},{10,18},{16,24},{18,26},{24,28},{26,30},{28,20... | collective-permute-start | bytes 1572872 | tf_op jit(solution)/shard_map/ppermute | solution.py:393
  27.5 20.9 %collective-permute-start.12 = (f32[2,4,128,128]{3,2,1,0:T(8,128)S(1)}, f32[2,4,128,128]{3,2,1,0:T(8,128)S(1)}, u32[]{:S(2)}, u32[]{:S(2)}) collective-permute-start(f32[2,4,128,128]{3,2,1,0:T(8,128)S(1)} %collective-permute-done.10.refs_12_), channel_id=1, source_target_pairs={{0,4},{2,6},{8,0},{10,2},{16,8},{18,10},{24,16},{26,18},{28,24},{3... | collective-permute-start | bytes 1572872 | tf_op jit(solution)/shard_map/ppermute | solution.py:393
  37.2 61.8 %copy-start.2 = (f32[2,4,128,128]{3,2,1,0:T(8,128)}, f32[2,4,128,128]{3,2,1,0:T(8,128)S(1)}, u32[]{:S(2)}) copy-start(f32[2,4,128,128]{3,2,1,0:T(8,128)S(1)} %collective-permute-done.3.refs_4_) | copy-start | bytes 1572868
  37.2 20.4 %collective-permute-start.4 = (f32[2,4,128,128]{3,2,1,0:T(8,128)}, f32[2,4,128,128]{3,2,1,0:T(8,128)}, u32[]{:S(2)}, u32[]{:S(2)}) collective-permute-start(f32[2,4,128,128]{3,2,1,0:T(8,128)} %collective-permute-done.1.token.refs_1_), channel_id=1, source_target_pairs={{0,8},{2,10},{8,16},{10,18},{16,24},{18,26},{24,28},{26,30},{28,20... | collective-permute-start | bytes 1572872 | tf_op jit(solution)/shard_map/ppermute | solution.py:393
  38.8 21.0 %collective-permute-start.5 = (f32[2,4,128,128]{3,2,1,0:T(8,128)S(1)}, f32[2,4,128,128]{3,2,1,0:T(8,128)}, u32[]{:S(2)}, u32[]{:S(2)}) collective-permute-start(f32[2,4,128,128]{3,2,1,0:T(8,128)S(1)} %collective-permute-done.3.refs_4_), channel_id=1, source_target_pairs={{0,4},{2,6},{8,0},{10,2},{16,8},{18,10},{24,16},{26,18},{28,24},{3... | collective-permute-start | bytes 1572872 | tf_op jit(solution)/shard_map/ppermute | solution.py:393
  46.2 13.5 %copy-start.3 = (f32[2,4,128,128]{3,2,1,0:T(8,128)}, f32[2,4,128,128]{3,2,1,0:T(8,128)S(1)}, u32[]{:S(2)}) copy-start(f32[2,4,128,128]{3,2,1,0:T(8,128)S(1)} %collective-permute-done.11.refs_10_) | copy-start | bytes 1572868
  48.4 20.4 %copy-start.4 = (f32[2,4,128,128]{3,2,1,0:T(8,128)}, f32[2,4,128,128]{3,2,1,0:T(8,128)S(1)}, u32[]{:S(2)}) copy-start(f32[2,4,128,128]{3,2,1,0:T(8,128)S(1)} %collective-permute-done.12.refs_13_) | copy-start | bytes 1572868
  48.4 20.4 %collective-permute-start.13 = (f32[2,4,128,128]{3,2,1,0:T(8,128)S(1)}, f32[2,4,128,128]{3,2,1,0:T(8,128)}, u32[]{:S(2)}, u32[]{:S(2)}) collective-permute-start(f32[2,4,128,128]{3,2,1,0:T(8,128)S(1)} %collective-permute-done.11.refs_10_), channel_id=1, source_target_pairs={{0,8},{2,10},{8,16},{10,18},{16,24},{18,26},{24,28},{26,30},{28,20... | collective-permute-start | bytes 1572872 | tf_op jit(solution)/shard_map/ppermute | solution.py:393
  50.0 21.0 %collective-permute-start.14 = (f32[2,4,128,128]{3,2,1,0:T(8,128)S(1)}, f32[2,4,128,128]{3,2,1,0:T(8,128)}, u32[]{:S(2)}, u32[]{:S(2)}) collective-permute-start(f32[2,4,128,128]{3,2,1,0:T(8,128)S(1)} %collective-permute-done.12.refs_13_), channel_id=1, source_target_pairs={{0,4},{2,6},{8,0},{10,2},{16,8},{18,10},{24,16},{26,18},{28,24},{3... | collective-permute-start | bytes 1572872 | tf_op jit(solution)/shard_map/ppermute | solution.py:393
  59.8 19.8 %collective-permute-start.6 = (f32[2,4,128,128]{3,2,1,0:T(8,128)}, f32[2,4,128,128]{3,2,1,0:T(8,128)}, u32[]{:S(2)}, u32[]{:S(2)}) collective-permute-start(f32[2,4,128,128]{3,2,1,0:T(8,128)} %collective-permute-done.4.token.refs_2_), channel_id=1, source_target_pairs={{0,8},{2,10},{8,16},{10,18},{16,24},{18,26},{24,28},{26,30},{28,20... | collective-permute-start | bytes 1572872 | tf_op jit(solution)/shard_map/ppermute | solution.py:393
  61.4 20.9 %collective-permute-start.7 = (f32[2,4,128,128]{3,2,1,0:T(8,128)}, f32[2,4,128,128]{3,2,1,0:T(8,128)}, u32[]{:S(2)}, u32[]{:S(2)}) collective-permute-start(f32[2,4,128,128]{3,2,1,0:T(8,128)} %collective-permute-done.5.refs_5_), channel_id=1, source_target_pairs={{0,4},{2,6},{8,0},{10,2},{16,8},{18,10},{24,16},{26,18},{28,24},{3... | collective-permute-start | bytes 1572872 | tf_op jit(solution)/shard_map/ppermute | solution.py:393
  71.0 21.3 %collective-permute-start.15 = (f32[2,4,128,128]{3,2,1,0:T(8,128)}, f32[2,4,128,128]{3,2,1,0:T(8,128)}, u32[]{:S(2)}, u32[]{:S(2)}) collective-permute-start(f32[2,4,128,128]{3,2,1,0:T(8,128)} %collective-permute-done.14.refs_14_), channel_id=1, source_target_pairs={{0,4},{2,6},{8,0},{10,2},{16,8},{18,10},{24,16},{26,18},{28,24},{3... | collective-permute-start | bytes 1572872 | tf_op jit(solution)/shard_map/ppermute | solution.py:393
  82.2 60.7 %copy-start.20 = (f32[1,128,128]{2,1,0:T(8,128)S(1)}, f32[1,128,128]{2,1,0:T(8,128)}, u32[]{:S(2)}) copy-start(f32[1,128,128]{2,1,0:T(8,128)} %get-tuple-element.78) | copy-start | bytes 196612
  82.3 11.9 %collective-permute-start.8 = (f32[2,4,128,128]{3,2,1,0:T(8,128)}, f32[2,4,128,128]{3,2,1,0:T(8,128)S(1)}, u32[]{:S(2)}, u32[]{:S(2)}) collective-permute-start(f32[2,4,128,128]{3,2,1,0:T(8,128)} %collective-permute-done.6.refs_3_), channel_id=1, source_target_pairs={{0,8},{2,10},{8,16},{10,18},{16,24},{18,26},{24,28},{26,30},{28,20... | collective-permute-start | bytes 1572872 | tf_op jit(solution)/shard_map/ppermute | solution.py:393
  92.4 2.6 %collective-permute-start.23 = (f32[2,4,128,128]{3,2,1,0:T(8,128)S(1)}, f32[2,4,128,128]{3,2,1,0:T(8,128)S(1)}, u32[]{:S(2)}, u32[]{:S(2)}) collective-permute-start(f32[2,4,128,128]{3,2,1,0:T(8,128)S(1)} %collective-permute-done.9.refs_9_), channel_id=1, source_target_pairs={{0,2},{2,0},{4,6},{6,4},{8,10},{10,8},{12,14},{14,12},{16,18},{18,... | collective-permute-start | bytes 1572872 | tf_op jit(solution)/shard_map/ppermute | solution.py:366
  92.4 2.9 %collective-permute-start.24 = (f32[2,4,128,128]{3,2,1,0:T(8,128)}, f32[2,4,128,128]{3,2,1,0:T(8,128)S(1)}, u32[]{:S(2)}, u32[]{:S(2)}) collective-permute-start(f32[2,4,128,128]{3,2,1,0:T(8,128)} %copy-done.3), channel_id=1, source_target_pairs={{0,2},{2,0},{4,6},{6,4},{8,10},{10,8},{12,14},{14,12},{16,18},{18,... | collective-permute-start | bytes 1572872 | tf_op jit(solution)/shard_map/ppermute | solution.py:366
  92.9 3.1 %collective-permute-start.25 = (f32[2,4,128,128]{3,2,1,0:T(8,128)}, f32[2,4,128,128]{3,2,1,0:T(8,128)S(1)}, u32[]{:S(2)}, u32[]{:S(2)}) collective-permute-start(f32[2,4,128,128]{3,2,1,0:T(8,128)} %collective-permute-done.13.refs_11_), channel_id=1, source_target_pairs={{0,2},{2,0},{4,6},{6,4},{8,10},{10,8},{12,14},{14,12},{16,18},{18,... | collective-permute-start | bytes 1572872 | tf_op jit(solution)/shard_map/ppermute | solution.py:366
  94.1 8.0 %copy-start.5 = (f32[2,4,128,128]{3,2,1,0:T(8,128)}, f32[2,4,128,128]{3,2,1,0:T(8,128)S(1)}, u32[]{:S(2)}) copy-start(f32[2,4,128,128]{3,2,1,0:T(8,128)S(1)} %collective-permute-done.8.refs_7_) | copy-start | bytes 1572868
  94.1 2.4 %collective-permute-start.26 = (f32[2,4,128,128]{3,2,1,0:T(8,128)S(1)}, f32[2,4,128,128]{3,2,1,0:T(8,128)S(1)}, u32[]{:S(2)}, u32[]{:S(2)}) collective-permute-start(f32[2,4,128,128]{3,2,1,0:T(8,128)S(1)} %collective-permute-done.10.refs_12_), channel_id=1, source_target_pairs={{0,2},{2,0},{4,6},{6,4},{8,10},{10,8},{12,14},{14,12},{16,18},{18,... | collective-permute-start | bytes 1572872 | tf_op jit(solution)/shard_map/ppermute | solution.py:366
  95.0 9.0 %copy-start.6 = (f32[2,4,128,128]{3,2,1,0:T(8,128)}, f32[2,4,128,128]{3,2,1,0:T(8,128)S(1)}, u32[]{:S(2)}) copy-start(f32[2,4,128,128]{3,2,1,0:T(8,128)S(1)} %collective-permute-done.23.refs_25_) | copy-start | bytes 1572868
  95.0 2.5 %collective-permute-start.27 = (f32[2,4,128,128]{3,2,1,0:T(8,128)}, f32[2,4,128,128]{3,2,1,0:T(8,128)S(1)}, u32[]{:S(2)}, u32[]{:S(2)}) collective-permute-start(f32[2,4,128,128]{3,2,1,0:T(8,128)} %copy-done.4), channel_id=1, source_target_pairs={{0,2},{2,0},{4,6},{6,4},{8,10},{10,8},{12,14},{14,12},{16,18},{18,... | collective-permute-start | bytes 1572872 | tf_op jit(solution)/shard_map/ppermute | solution.py:366
  95.2 8.8 %copy-start.7 = (f32[2,4,128,128]{3,2,1,0:T(8,128)}, f32[2,4,128,128]{3,2,1,0:T(8,128)S(1)}, u32[]{:S(2)}) copy-start(f32[2,4,128,128]{3,2,1,0:T(8,128)S(1)} %collective-permute-done.24.refs_26_) | copy-start | bytes 1572868
  95.2 3.0 %collective-permute-start.28 = (f32[2,4,128,128]{3,2,1,0:T(8,128)}, f32[2,4,128,128]{3,2,1,0:T(8,128)S(1)}, u32[]{:S(2)}, u32[]{:S(2)}) collective-permute-start(f32[2,4,128,128]{3,2,1,0:T(8,128)} %collective-permute-done.14.refs_14_), channel_id=1, source_target_pairs={{0,2},{2,0},{4,6},{6,4},{8,10},{10,8},{12,14},{14,12},{16,18},{18,... | collective-permute-start | bytes 1572872 | tf_op jit(solution)/shard_map/ppermute | solution.py:366
  96.0 8.0 %copy-start.8 = (f32[2,4,128,128]{3,2,1,0:T(8,128)}, f32[2,4,128,128]{3,2,1,0:T(8,128)S(1)}, u32[]{:S(2)}) copy-start(f32[2,4,128,128]{3,2,1,0:T(8,128)S(1)} %collective-permute-done.25.refs_27_) | copy-start | bytes 1572868
  96.0 3.0 %collective-permute-start.29 = (f32[2,4,128,128]{3,2,1,0:T(8,128)}, f32[2,4,128,128]{3,2,1,0:T(8,128)S(1)}, u32[]{:S(2)}, u32[]{:S(2)}) collective-permute-start(f32[2,4,128,128]{3,2,1,0:T(8,128)} %collective-permute-done.15.refs_15_), channel_id=1, source_target_pairs={{0,2},{2,0},{4,6},{6,4},{8,10},{10,8},{12,14},{14,12},{16,18},{18,... | collective-permute-start | bytes 1572872 | tf_op jit(solution)/shard_map/ppermute | solution.py:366
  96.5 7.5 %copy-start.9 = (f32[2,4,128,128]{3,2,1,0:T(8,128)}, f32[2,4,128,128]{3,2,1,0:T(8,128)S(1)}, u32[]{:S(2)}) copy-start(f32[2,4,128,128]{3,2,1,0:T(8,128)S(1)} %collective-permute-done.26.refs_28_) | copy-start | bytes 1572868
  96.5 3.2 %collective-permute-start.16 = (f32[2,4,128,128]{3,2,1,0:T(8,128)}, f32[2,4,128,128]{3,2,1,0:T(8,128)S(1)}, u32[]{:S(2)}, u32[]{:S(2)}) collective-permute-start(f32[2,4,128,128]{3,2,1,0:T(8,128)} %collective-permute-done.1.token.refs_1_), channel_id=1, source_target_pairs={{0,2},{2,0},{4,6},{6,4},{8,10},{10,8},{12,14},{14,12},{16,18},{18,... | collective-permute-start | bytes 1572872 | tf_op jit(solution)/shard_map/ppermute | solution.py:366
  97.5 9.0 %copy-start.10 = (f32[2,4,128,128]{3,2,1,0:T(8,128)}, f32[2,4,128,128]{3,2,1,0:T(8,128)S(1)}, u32[]{:S(2)}) copy-start(f32[2,4,128,128]{3,2,1,0:T(8,128)S(1)} %collective-permute-done.27.refs_29_) | copy-start | bytes 1572868
  97.5 3.0 %collective-permute-start.17 = (f32[2,4,128,128]{3,2,1,0:T(8,128)}, f32[2,4,128,128]{3,2,1,0:T(8,128)S(1)}, u32[]{:S(2)}, u32[]{:S(2)}) collective-permute-start(f32[2,4,128,128]{3,2,1,0:T(8,128)} %collective-permute-done.4.token.refs_2_), channel_id=1, source_target_pairs={{0,2},{2,0},{4,6},{6,4},{8,10},{10,8},{12,14},{14,12},{16,18},{18,... | collective-permute-start | bytes 1572872 | tf_op jit(solution)/shard_map/ppermute | solution.py:366
  98.2 5.8 %copy-start.11 = (f32[2,4,128,128]{3,2,1,0:T(8,128)}, f32[2,4,128,128]{3,2,1,0:T(8,128)S(1)}, u32[]{:S(2)}) copy-start(f32[2,4,128,128]{3,2,1,0:T(8,128)S(1)} %collective-permute-done.28.refs_30_) | copy-start | bytes 1572868
  98.2 3.7 %collective-permute-start.18 = (f32[2,4,128,128]{3,2,1,0:T(8,128)}, f32[2,4,128,128]{3,2,1,0:T(8,128)S(1)}, u32[]{:S(2)}, u32[]{:S(2)}) collective-permute-start(f32[2,4,128,128]{3,2,1,0:T(8,128)} %collective-permute-done.6.refs_3_), channel_id=1, source_target_pairs={{0,2},{2,0},{4,6},{6,4},{8,10},{10,8},{12,14},{14,12},{16,18},{18,... | collective-permute-start | bytes 1572872 | tf_op jit(solution)/shard_map/ppermute | solution.py:366
  99.0 5.1 %copy-start.12 = (f32[2,4,128,128]{3,2,1,0:T(8,128)}, f32[2,4,128,128]{3,2,1,0:T(8,128)S(1)}, u32[]{:S(2)}) copy-start(f32[2,4,128,128]{3,2,1,0:T(8,128)S(1)} %collective-permute-done.29.refs_31_) | copy-start | bytes 1572868
  99.0 3.1 %collective-permute-start.19 = (f32[2,4,128,128]{3,2,1,0:T(8,128)S(1)}, f32[2,4,128,128]{3,2,1,0:T(8,128)S(1)}, u32[]{:S(2)}, u32[]{:S(2)}) collective-permute-start(f32[2,4,128,128]{3,2,1,0:T(8,128)S(1)} %collective-permute-done.3.refs_4_), channel_id=1, source_target_pairs={{0,2},{2,0},{4,6},{6,4},{8,10},{10,8},{12,14},{14,12},{16,18},{18,... | collective-permute-start | bytes 1572872 | tf_op jit(solution)/shard_map/ppermute | solution.py:366
  99.7 6.7 %copy-start.13 = (f32[2,4,128,128]{3,2,1,0:T(8,128)}, f32[2,4,128,128]{3,2,1,0:T(8,128)S(1)}, u32[]{:S(2)}) copy-start(f32[2,4,128,128]{3,2,1,0:T(8,128)S(1)} %collective-permute-done.16.refs_17_) | copy-start | bytes 1572868
  99.7 3.0 %collective-permute-start.20 = (f32[2,4,128,128]{3,2,1,0:T(8,128)}, f32[2,4,128,128]{3,2,1,0:T(8,128)S(1)}, u32[]{:S(2)}, u32[]{:S(2)}) collective-permute-start(f32[2,4,128,128]{3,2,1,0:T(8,128)} %collective-permute-done.5.refs_5_), channel_id=1, source_target_pairs={{0,2},{2,0},{4,6},{6,4},{8,10},{10,8},{12,14},{14,12},{16,18},{18,... | collective-permute-start | bytes 1572872 | tf_op jit(solution)/shard_map/ppermute | solution.py:366
  100.5 3.6 %copy-start.14 = (f32[2,4,128,128]{3,2,1,0:T(8,128)}, f32[2,4,128,128]{3,2,1,0:T(8,128)S(1)}, u32[]{:S(2)}) copy-start(f32[2,4,128,128]{3,2,1,0:T(8,128)S(1)} %collective-permute-done.17.refs_18_) | copy-start | bytes 1572868
  100.5 3.0 %collective-permute-start.21 = (f32[2,4,128,128]{3,2,1,0:T(8,128)}, f32[2,4,128,128]{3,2,1,0:T(8,128)S(1)}, u32[]{:S(2)}, u32[]{:S(2)}) collective-permute-start(f32[2,4,128,128]{3,2,1,0:T(8,128)} %collective-permute-done.7.refs_6_), channel_id=1, source_target_pairs={{0,2},{2,0},{4,6},{6,4},{8,10},{10,8},{12,14},{14,12},{16,18},{18,... | collective-permute-start | bytes 1572872 | tf_op jit(solution)/shard_map/ppermute | solution.py:366
  102.0 2.1 %copy-start.15 = (f32[2,4,128,128]{3,2,1,0:T(8,128)}, f32[2,4,128,128]{3,2,1,0:T(8,128)S(1)}, u32[]{:S(2)}) copy-start(f32[2,4,128,128]{3,2,1,0:T(8,128)S(1)} %collective-permute-done.18.refs_19_) | copy-start | bytes 1572868
  102.0 2.0 %collective-permute-start.22 = (f32[2,4,128,128]{3,2,1,0:T(8,128)S(1)}, f32[2,4,128,128]{3,2,1,0:T(8,128)S(1)}, u32[]{:S(2)}, u32[]{:S(2)}) collective-permute-start(f32[2,4,128,128]{3,2,1,0:T(8,128)S(1)} %collective-permute-done.8.refs_7_), channel_id=1, source_target_pairs={{0,2},{2,0},{4,6},{6,4},{8,10},{10,8},{12,14},{14,12},{16,18},{18,... | collective-permute-start | bytes 1572872 | tf_op jit(solution)/shard_map/ppermute | solution.py:366
  102.1 2.0 %copy-start.16 = (f32[2,4,128,128]{3,2,1,0:T(8,128)}, f32[2,4,128,128]{3,2,1,0:T(8,128)S(1)}, u32[]{:S(2)}) copy-start(f32[2,4,128,128]{3,2,1,0:T(8,128)S(1)} %collective-permute-done.19.refs_20_) | copy-start | bytes 1572868
  102.7 1.4 copy-start.17
  103.5 0.8 copy-start.18
  104.3 0.8 copy-start.19
  122.7 2.2 %collective-permute-start.30 = (f32[8,128,128]{2,1,0:T(8,128)}, f32[8,128,128]{2,1,0:T(8,128)S(1)}, u32[]{:S(2)}, u32[]{:S(2)}) collective-permute-start(f32[8,128,128]{2,1,0:T(8,128)} %get-tuple-element.80), channel_id=1, source_target_pairs={{0,2},{2,0},{4,6},{6,4},{8,10},{10,8},{12,14},{14,12},{16,18},{18,... | collective-permute-start | bytes 1572872 | tf_op jit(solution)/shard_map/ppermute | solution.py:366
  126.1 8.5 %collective-permute-start.31 = (f32[1,128,128]{2,1,0:T(8,128)S(1)}, f32[1,128,128]{2,1,0:T(8,128)S(1)}, u32[]{:S(2)}, u32[]{:S(2)}) collective-permute-start(f32[1,128,128]{2,1,0:T(8,128)S(1)} %get-tuple-element.84), channel_id=1, source_target_pairs={{0,4},{2,6},{4,0},{6,2},{8,12},{10,14},{12,8},{14,10},{16,20},{18,... | collective-permute-start | bytes 196616 | tf_op jit(solution)/shard_map/ppermute | solution.py:418
  127.5 10.3 %collective-permute-start.36 = (f32[1,128,128]{2,1,0:T(8,128)S(1)}, f32[1,128,128]{2,1,0:T(8,128)S(1)}, u32[]{:S(2)}, u32[]{:S(2)}) collective-permute-start(f32[1,128,128]{2,1,0:T(8,128)S(1)} %get-tuple-element.85), channel_id=1, source_target_pairs={{0,20},{2,22},{4,16},{6,18},{8,28},{10,30},{12,24},{14,26},{16,4},... | collective-permute-start | bytes 196616 | tf_op jit(solution)/shard_map/ppermute | solution.py:418
  130.6 7.2 %collective-permute-start.33 = (f32[1,128,128]{2,1,0:T(8,128)S(1)}, f32[1,128,128]{2,1,0:T(8,128)S(1)}, u32[]{:S(2)}, u32[]{:S(2)}) collective-permute-start(f32[1,128,128]{2,1,0:T(8,128)S(1)} %get-tuple-element.86), channel_id=1, source_target_pairs={{0,28},{2,30},{4,24},{6,26},{8,4},{10,6},{12,0},{14,2},{16,12},{18... | collective-permute-start | bytes 196616 | tf_op jit(solution)/shard_map/ppermute | solution.py:418
  133.4 7.9 %collective-permute-start.32 = (f32[1,128,128]{2,1,0:T(8,128)S(1)}, f32[1,128,128]{2,1,0:T(8,128)S(1)}, u32[]{:S(2)}, u32[]{:S(2)}) collective-permute-start(f32[1,128,128]{2,1,0:T(8,128)S(1)} %get-tuple-element.87), channel_id=1, source_target_pairs={{0,12},{2,14},{4,8},{6,10},{8,20},{10,22},{12,16},{14,18},{16,28},... | collective-permute-start | bytes 196616 | tf_op jit(solution)/shard_map/ppermute | solution.py:418
  133.6 7.8 %collective-permute-start.34 = (f32[1,128,128]{2,1,0:T(8,128)S(1)}, f32[1,128,128]{2,1,0:T(8,128)S(1)}, u32[]{:S(2)}, u32[]{:S(2)}) collective-permute-start(f32[1,128,128]{2,1,0:T(8,128)S(1)} %get-tuple-element.88), channel_id=1, source_target_pairs={{0,8},{2,10},{4,12},{6,14},{8,16},{10,18},{12,20},{14,22},{16,24},... | collective-permute-start | bytes 196616 | tf_op jit(solution)/shard_map/ppermute | solution.py:418
  134.6 8.2 %collective-permute-start.37 = (f32[1,128,128]{2,1,0:T(8,128)S(1)}, f32[1,128,128]{2,1,0:T(8,128)S(1)}, u32[]{:S(2)}, u32[]{:S(2)}) collective-permute-start(f32[1,128,128]{2,1,0:T(8,128)S(1)} %get-tuple-element.89), channel_id=1, source_target_pairs={{0,16},{2,18},{4,20},{6,22},{8,24},{10,26},{12,28},{14,30},{16,0},... | collective-permute-start | bytes 196616 | tf_op jit(solution)/shard_map/ppermute | solution.py:418
  137.8 5.2 %collective-permute-start.35 = (f32[1,128,128]{2,1,0:T(8,128)S(1)}, f32[1,128,128]{2,1,0:T(8,128)S(1)}, u32[]{:S(2)}, u32[]{:S(2)}) collective-permute-start(f32[1,128,128]{2,1,0:T(8,128)S(1)} %get-tuple-element.90), channel_id=1, source_target_pairs={{0,24},{2,26},{4,28},{6,30},{8,0},{10,2},{12,4},{14,6},{16,8},{18,... | collective-permute-start | bytes 196616 | tf_op jit(solution)/shard_map/ppermute | solution.py:418
